TPU v7x, 32 devices: a whole 2x2x4 slice. The times are simulated.
32 devices in a mesh: tile: 8 (over y, x, core), phi: 4 (over z).
Axes of the slice: x: 2, y: 2, z: 4, core: 2. Of those that a mesh axis runs over, the one named last changes fastest.
Arguments:
- blocks: bfloat16 [2048, 5, 64, 256], P(('tile', 'phi')), may hold values from -6 to 6
- levels: int32 [2048], P(('tile', 'phi')), may hold values from 0 to 3
- block_dest: int32 [2048], P(('tile', 'phi')), may hold values from 0 to 7, as said below
- block_phi: int32 [2048], P(('tile', 'phi')), may hold values from 0 to 7, as said below
- block_group: int32 [2048], P(('tile', 'phi')), may hold values from 0 to 7, as said below
Outputs:
- spectra: float32 [5, 64, 256, 2048], P(None, 'tile', 'phi')
Inputs may be any that keep to these rules, and one draw needn't show every extreme that they name: `block_dest`: at most 16 of one device's blocks name one tile, and some device sends exactly 16 to some tile; for each tile and each phi segment, the blocks of that segment that name the tile are exactly 64. Among the blocks of one phi segment that name one tile, the pairs (block_phi, block_group) take each of the 64 values once. `block_group`: see block_phi.
All inputs are finite; a program needn't handle non-finite values.
Results may differ from a plain program's by a relative error of at most 0.003.
Values may be sent and summed in bfloat16 or wider, within the bound.
No kernel may reach another device: no remote copies, remote signals or barrier semaphores. Data moves between devices by JAX's collectives and lax.ppermute only.
A program may use at most 192 MiB of HBM per device.

v0:
```python
import math

import jax
import jax.numpy as jnp
from jax import lax
from jax.sharding import PartitionSpec as P

FIELDS = 5
NPHI = 2048
BPHI = 64
COLS = 256
CG_DEV = 8


def dft_basis(length):
    column = jnp.arange(length, dtype=jnp.int32)
    half = length // 2
    mode = jnp.where(column <= half, column, column - half)
    phase = column[:, None] * mode[None, :] % length
    angle = phase.astype(jnp.float32) * jnp.float32(2.0 * math.pi / length)
    values = jnp.where((column <= half)[None, :], jnp.cos(angle), jnp.sin(angle))
    return (values * jnp.float32(1.0 / math.sqrt(length))).astype(jnp.bfloat16)


def local(blocks, levels, block_dest, block_phi, block_group):
    tile_count = lax.axis_size("tile")
    plane_count = lax.axis_size("phi")
    slot_count = blocks.shape[0]
    per_plane = NPHI // BPHI // plane_count
    capacity = 2 * slot_count // tile_count
    sliver = COLS // plane_count
    weight = (1.0 / jnp.left_shift(1, levels).astype(jnp.float32)).astype(jnp.bfloat16)
    weighted = blocks * weight[:, None, None, None]
    onehot_dest = (block_dest[:, None] == jnp.arange(tile_count, dtype=jnp.int32)[None, :]).astype(
        jnp.int32
    )
    slot_rank = jnp.sum((jnp.cumsum(onehot_dest, axis=0) - 1) * onehot_dest, axis=1)
    send_slot = block_dest * capacity + slot_rank
    outbox = (
        jnp.zeros((tile_count * capacity,) + blocks.shape[1:], jnp.bfloat16)
        .at[send_slot]
        .set(weighted)
    )
    basis_table = dft_basis(NPHI).reshape(plane_count, per_plane, BPHI, NPHI)
    phi_out = jnp.full((tile_count * capacity,), -1, jnp.int32).at[send_slot].set(block_phi)
    group_out = jnp.full((tile_count * capacity,), -1, jnp.int32).at[send_slot].set(block_group)
    arrived, arrived_phi, arrived_group = (
        lax.all_to_all(outbox, "tile", split_axis=0, concat_axis=0, tiled=True),
        lax.all_to_all(phi_out, "tile", split_axis=0, concat_axis=0, tiled=True),
        lax.all_to_all(group_out, "tile", split_axis=0, concat_axis=0, tiled=True),
    )
    recv_slot = jnp.where(arrived_phi >= 0, arrived_phi * CG_DEV + arrived_group, slot_count)
    arranged = (
        jnp.zeros((slot_count,) + blocks.shape[1:], jnp.bfloat16)
        .at[recv_slot]
        .set(arrived, mode="drop")
    )
    arranged = arranged.reshape(per_plane, CG_DEV, FIELDS, BPHI, plane_count, sliver)
    arranged = jnp.transpose(arranged, (4, 2, 0, 1, 3, 5)).reshape(
        plane_count, FIELDS, per_plane, CG_DEV, BPHI * sliver
    )
    pieces = lax.all_to_all(arranged, "phi", split_axis=0, concat_axis=0, tiled=True)
    field_count = pieces.shape[1]
    shaped = pieces.reshape(plane_count, field_count, per_plane, CG_DEV, BPHI, sliver)
    return jnp.einsum("pnagbc,pabk->ngck", shaped, basis_table, preferred_element_type=jnp.float32)


def solution(mesh):
    in_specs = (
        P(("tile", "phi"), None, None, None),
        P(("tile", "phi")),
        P(("tile", "phi")),
        P(("tile", "phi")),
        P(("tile", "phi")),
    )
    out_specs = P(None, "tile", "phi", None)
    return jax.shard_map(local, mesh=mesh, in_specs=in_specs, out_specs=out_specs, check_vma=False)
```

profile of v0, /device:TPU:10, one launch (start us, length us, event | category | flops | bytes accessed | tf_op | source)
XLA Modules:
  0.0 771.0 jit_solution(5112710800719456086)
XLA Ops:
  0.0 0.7 fusion.15
  0.7 0.1 reduce_window_sum.11
  0.8 0.8 select_reduce_fusion
  1.7 0.7 compare_select_fusion.2
  2.3 0.9 scatter_custom_fusion
  3.2 0.7 all_to_all.18
  3.9 4.3 all-to-all-start
  8.2 0.7 divide_convert_fusion
  8.8 0.9 scatter_custom_fusion.1
  9.7 0.7 all_to_all.20
  10.4 0.9 all-to-all-done
  11.3 4.7 all-to-all-start.1
  16.0 10.0 %broadcast_multiply_fusion = bf16[64,5,64,256]{3,2,1,0:T(8,128)(2,1)} fusion(bf16[64,5,64,256]{3,2,1,0:T(8,128)(2,1)} %param.5, bf16[64]{0:T(256)(128)(2,1)S(1)} %divide_convert_fusion), kind=kLoop, calls=%fused_computation.25 | loop fusion | flops 5242880 | bytes 20971648 | tf_op jit(solution)/shard_map/mul | solution.py:33
  26.0 7.4 broadcast_in_dim.36
  33.3 24.3 %scatter_fusion = bf16[128,5,64,256]{3,2,1,0:T(8,128)(2,1)} fusion(bf16[128,5,64,256]{3,2,1,0:T(8,128)(2,1)} %broadcast_in_dim.36, s32[64]{0:T(128)S(1)} %compare_select_fusion.2, bf16[64,5,64,256]{3,2,1,0:T(8,128)(2,1)} %broadcast_multiply_fusion), kind=kCustom, calls=%fused_computation.2 | custom fusion | bytes 31457536 | tf_op jit(solution)/shard_map/scatter | solution.py:42
  57.6 0.0 all-to-all-done.1
  57.6 6.1 all-to-all-start.2
  63.8 0.1 select_n.52
  63.8 227.4 %all-to-all-done.2 = bf16[128,5,64,256]{3,2,1,0:T(8,128)(2,1)} async-done(((bf16[128,5,64,256]{3,2,1,0:T(8,128)(2,1)}), bf16[128,5,64,256]{3,2,1,0:T(8,128)(2,1)}, u32[]{:S(2)}, u32[]{:S(2)}) %all-to-all-start.2) | async-done | bytes 20971552 | tf_op jit(solution)/shard_map/all_to_all | solution.py:48
  291.2 5.3 broadcast_in_dim.32
  296.5 43.8 %scatter_fusion.1 = bf16[64,5,64,256]{3,2,1,0:T(8,128)(2,1)} fusion(bf16[64,5,64,256]{3,2,1,0:T(8,128)(2,1)} %broadcast_in_dim.32, s32[128]{0:T(128)S(1)} %fusion.17, bf16[128,5,64,256]{3,2,1,0:T(8,128)(2,1)} %all-to-all-done.2), kind=kCustom, calls=%fused_computation.3 | custom fusion | bytes 62915072 | tf_op jit(solution)/shard_map/scatter | solution.py:56
  340.3 30.3 %reshape.98 = bf16[8,8,5,64,4,64]{5,4,3,2,1,0:T(4,128)(2,1)} reshape(bf16[64,5,64,256]{3,2,1,0:T(8,128)(2,1)} %scatter_fusion.1) | data formatting | bytes 20971520 | tf_op jit(solution)/shard_map/reshape | solution.py:58
  370.6 18.9 %copy.12 = bf16[4,5,8,8,64,64]{5,4,3,2,1,0:T(8,128)(2,1)} copy(bf16[4,5,8,8,64,64]{5,0,4,1,3,2:T(4,128)(2,1)} %bitcast.21) | data formatting | bytes 20971520 | tf_op jit(solution)/shard_map/transpose | solution.py:59
  389.5 28.0 %reshape.99 = bf16[4,5,8,8,4096]{4,3,2,1,0:T(8,128)(2,1)} reshape(bf16[4,5,8,8,64,64]{5,4,3,2,1,0:T(8,128)(2,1)} %copy.12) | data formatting | bytes 20971520 | tf_op jit(solution)/shard_map/reshape | solution.py:59
  417.5 6.3 all-to-all-start.3
  423.9 225.2 %all-to-all-done.3 = bf16[4,5,8,8,4096]{4,3,2,1,0:T(8,128)(2,1)} async-done(((bf16[4,5,8,8,4096]{4,3,2,1,0:T(8,128)(2,1)}), bf16[4,5,8,8,4096]{4,3,2,1,0:T(8,128)(2,1)}, u32[]{:S(2)}, u32[]{:S(2)}) %all-to-all-start.3) | async-done | bytes 10485792 | tf_op jit(solution)/shard_map/all_to_all | solution.py:62
  649.1 29.3 %reshape.100 = bf16[4,5,8,8,64,64]{5,4,3,2,1,0:T(8,128)(2,1)} reshape(bf16[4,5,8,8,4096]{4,3,2,1,0:T(8,128)(2,1)} %all-to-all-done.3) | data formatting | bytes 20971520 | tf_op jit(solution)/shard_map/reshape | solution.py:64
  678.4 85.2 %fusion = f32[5,8,64,2048,1,1]{3,2,4,0,1,5:T(8,128)S(1)} fusion(bf16[4,5,8,8,64,64]{5,4,3,2,1,0:T(8,128)(2,1)} %reshape.100, s32[2048]{0:T(1024)S(1)} %add_select_fusion.1, s32[4,8,64]{2,1,0:T(8,128)S(1)} %multiply_add_fusion, pred[2048]{0:T(1024)(128)(4,1)S(1)} %iota_compare_fusion.1), kind=kOutput, calls=%fused_computation.9 | convolution fusion | flops 21546139648 | bytes 31475712 | tf_op jit(solution)/shard_map/pnagbc,pabk->ngck/dot_general | solution.py:65
  763.6 7.5 copy.22
  (5 shorter events, 0.0 us)
Async XLA Ops:
  3.9 7.4 all-to-all-start
  11.3 46.4 %all-to-all-start.1 = ((s32[8,16,1]{1,2,0:T(1,128)}), s32[8,16,1]{1,2,0:T(1,128)S(1)}, u32[]{:S(2)}, u32[]{:S(2)}) async-start(s32[8,16,1]{1,2,0:T(1,128)} %bitcast.1), calls=%async_computation.1 | async-start | bytes 8192 | tf_op jit(solution)/shard_map/all_to_all | solution.py:50
  57.6 233.6 %all-to-all-start.2 = ((bf16[128,5,64,256]{3,2,1,0:T(8,128)(2,1)}), bf16[128,5,64,256]{3,2,1,0:T(8,128)(2,1)}, u32[]{:S(2)}, u32[]{:S(2)}) async-start(bf16[128,5,64,256]{3,2,1,0:T(8,128)(2,1)} %scatter_fusion), calls=%async_computation.2 | async-start | bytes 41943040 | tf_op jit(solution)/shard_map/all_to_all | solution.py:48
  417.5 231.6 %all-to-all-start.3 = ((bf16[4,5,8,8,4096]{4,3,2,1,0:T(8,128)(2,1)}), bf16[4,5,8,8,4096]{4,3,2,1,0:T(8,128)(2,1)}, u32[]{:S(2)}, u32[]{:S(2)}) async-start(bf16[4,5,8,8,4096]{4,3,2,1,0:T(8,128)(2,1)} %reshape.99), calls=%async_computation.3 | async-start | bytes 20971520 | tf_op jit(solution)/shard_map/all_to_all | solution.py:62
where the time goes:
time: 778 us; the launch traced here: 771 us
  waiting for transfers between devices  454 us (58%)
  local copies, waits for them, and re-layouts  198 us (25%)
  matrix products  85.2 us (11%)
  starting transfers between devices  21.4 us (3%)
  other arithmetic  13 us (2%)
    all_to_all x1, waiting for transfers between devices, local(): lax.all_to_all(outbox, 'tile', split_axis=0, concat_axis=0, tiled=True)  227 us
    all_to_all x1, waiting for transfers between devices, local(): lax.all_to_all(arranged, 'phi', split_axis=0, concat_axis=0, tiled=True)  225 us
    dot_general x1, matrix products, local(): jnp.einsum('pnagbc,pabk->ngck', shaped, basis_table, preferred_element_ty...  85.2 us
    scatter x1, local copies, waits for them, and re-layouts, local(): arranged = jnp.zeros((slot_count,) + blocks.shape[1:], jnp.bfloat16).at[r...  43.8 us
    reshape x1, local copies, waits for them, and re-layouts, local(): arranged.reshape(per_plane, CG_DEV, FIELDS, BPHI, plane_count, sliver)  30.3 us
    reshape x1, local copies, waits for them, and re-layouts, local(): pieces.reshape(plane_count, field_count, per_plane, CG_DEV, BPHI, sliver)  29.3 us
    reshape x1, local copies, waits for them, and re-layouts, local(): jnp.transpose(arranged, (4, 2, 0, 1, 3, 5))  28 us
    scatter x1, local copies, waits for them, and re-layouts, local(): outbox = jnp.zeros((tile_count * capacity,) + blocks.shape[1:], jnp.bfloa...  24.3 us
  transfers between devices with their start and end apart: 4, of which 3 were waited for; matrix products, arithmetic and copies ran while one was open for 6% of the time, Pallas kernels for 0%

commit v1 on v0

v1 whole, which is shorter than its diff:
```python
import functools
import math

import jax
import jax.numpy as jnp
from jax import lax
from jax.experimental import pallas as pl
from jax.experimental.pallas import tpu as pltpu
from jax.sharding import PartitionSpec as P

FIELDS = 5
NPHI = 2048
BPHI = 64
COLS = 256
CG_DEV = 8
LANES = 128
FIRST = 2
VMEM_BYTES = 48 * 1024 * 1024

ANY = pl.BlockSpec(memory_space=pl.ANY)
SMEM = pl.BlockSpec(memory_space=pltpu.SMEM)
VMEM = pl.BlockSpec(memory_space=pltpu.VMEM)


def rotated_basis(length, start):
    row = start
    column = jnp.arange(length, dtype=jnp.int32)
    half = length // 2
    mode = jnp.where(column <= half, column, column - half)
    phase = row[:, None] * mode[None, :] % length
    angle = phase.astype(jnp.float32) * jnp.float32(2.0 * math.pi / length)
    values = jnp.where((column <= half)[None, :], jnp.cos(angle), jnp.sin(angle))
    return (values * jnp.float32(1.0 / math.sqrt(length))).astype(jnp.bfloat16)


def granules(block, planes):
    turned = block.T
    sliver = COLS // planes
    half = sliver // 2
    out = []
    for p in range(planes):
        low = turned[p * sliver : p * sliver + half]
        high = turned[p * sliver + half : (p + 1) * sliver]
        out.append(jnp.concatenate([low, high], axis=1))
    return out


def params(**kw):
    return pltpu.CompilerParams(vmem_limit_bytes=VMEM_BYTES, **kw)


def cut_kernel(planes, chunk, count, me_ref, weight_ref, x_ref, *outs):
    base = pl.program_id(0) * chunk
    me = me_ref[0]
    for mine in range(planes):

        @pl.when(me == mine)
        def _():
            def body(i, carry):
                w = weight_ref[base + i]
                for f in range(count):
                    x = (x_ref[i, f].astype(jnp.float32) * w).astype(jnp.bfloat16)
                    for p, g in enumerate(granules(x, planes)):
                        outs[(p - mine) % planes][f, i] = g
                return carry

            lax.fori_loop(0, chunk, body, 0)


def cut(blocks, weight, me, planes, count):
    slots = blocks.shape[0]
    chunk = 8
    half = COLS // planes // 2
    return pl.pallas_call(
        functools.partial(cut_kernel, planes, chunk, count),
        grid=(slots // chunk,),
        in_specs=[
            SMEM,
            SMEM,
            pl.BlockSpec((chunk, count, BPHI, COLS), lambda i: (i, 0, 0, 0)),
        ],
        out_specs=[pl.BlockSpec((count, chunk, half, LANES), lambda i: (0, i, 0, 0))] * planes,
        out_shape=[jax.ShapeDtypeStruct((count, slots, half, LANES), jnp.bfloat16)] * planes,
        compiler_params=params(),
        name="cut",
    )(me, weight, blocks)


def post_kernel(fields, slot_ref, x_ref, *rest):
    outs, sems = rest[:-1], rest[-1]
    slots = slot_ref.shape[0]
    for k, f in enumerate(fields):

        def body(i, carry):
            pltpu.make_async_copy(x_ref.at[i, f], outs[k].at[slot_ref[i]], sems.at[k]).start()
            return carry

        lax.fori_loop(0, slots, body, 0)
    for k, f in enumerate(fields):
        part = outs[k].at[pl.ds(0, slots)]
        pltpu.make_async_copy(part, part, sems.at[k]).wait()


def post(blocks, slot, fields, room):
    return pl.pallas_call(
        functools.partial(post_kernel, fields),
        in_specs=[SMEM, ANY],
        out_specs=[ANY] * len(fields),
        out_shape=[jax.ShapeDtypeStruct((room, BPHI, COLS), jnp.bfloat16)] * len(fields),
        scratch_shapes=[pltpu.SemaphoreType.DMA((len(fields),))],
        compiler_params=params(),
        name="post",
    )(slot, blocks)


def sort_kernel(planes, me_ref, slot_ref, weight_ref, x_ref, *rest):
    outs, (buf, sem) = rest[:planes], rest[planes:]
    places = slot_ref.shape[0]
    me = me_ref[0]

    def fetch(i, carry):
        pltpu.make_async_copy(x_ref.at[slot_ref[i]], buf.at[i], sem).start()
        return carry

    lax.fori_loop(0, places, fetch, 0)
    pltpu.make_async_copy(buf, buf, sem).wait()
    for mine in range(planes):

        @pl.when(me == mine)
        def _():
            def body(i, carry):
                x = (buf[i].astype(jnp.float32) * weight_ref[i]).astype(jnp.bfloat16)
                for p, g in enumerate(granules(x, planes)):
                    outs[(p - mine) % planes][i] = g
                return carry

            lax.fori_loop(0, places, body, 0)


def sort(arrived, slot, weight, me, planes):
    places = slot.shape[0]
    half = COLS // planes // 2
    return pl.pallas_call(
        functools.partial(sort_kernel, planes),
        in_specs=[SMEM, SMEM, SMEM, ANY],
        out_specs=[VMEM] * planes,
        out_shape=[jax.ShapeDtypeStruct((places, half, LANES), jnp.bfloat16)] * planes,
        scratch_shapes=[
            pltpu.VMEM((places, BPHI, COLS), jnp.bfloat16),
            pltpu.SemaphoreType.DMA,
        ],
        compiler_params=params(),
        name="sort",
    )(me, slot, weight, arrived)


def mail_kernel(planes, count, slot_ref, *rest):
    ins, outs, sems = rest[:planes], rest[planes : planes + count], rest[-1]
    slots = slot_ref.shape[1]
    for f in range(count):
        for d in range(planes):

            def body(i, carry):
                pltpu.make_async_copy(
                    ins[d].at[f, i], outs[f].at[slot_ref[d, i]], sems.at[f, d]
                ).start()
                return carry

            lax.fori_loop(0, slots, body, 0)
    for f in range(count):
        for d in range(planes):
            part = outs[f].at[pl.ds(0, slots)]
            pltpu.make_async_copy(part, part, sems.at[f, d]).wait()


def mail(parts, slot, room):
    planes = len(parts)
    count, _, half, _ = parts[0].shape
    return pl.pallas_call(
        functools.partial(mail_kernel, planes, count),
        in_specs=[SMEM] + [ANY] * planes,
        out_specs=[ANY] * count,
        out_shape=[jax.ShapeDtypeStruct((room, half, LANES), jnp.bfloat16)] * count,
        scratch_shapes=[pltpu.SemaphoreType.DMA((count, planes))],
        compiler_params=params(),
        name="mail",
    )(slot, *parts)


def transform_kernel(planes, field, routed, chained, *refs):
    refs = list(refs)
    slot_ref = refs.pop(0) if routed else None
    ins = [refs.pop(0)] if routed else [refs.pop(0) for _ in range(planes)]
    basis_hbm = refs.pop(0)
    if chained:
        refs.pop(0)
    out_hbm, gran, rows, basis, acc, in_sems, basis_sems, out_sems = refs
    per_plane = gran.shape[1]
    half = gran.shape[3]
    chunks = basis_sems.shape[0]
    wide = NPHI // chunks

    for j in range(chunks):
        span = pl.ds(j * wide, wide)
        pltpu.make_async_copy(basis_hbm.at[:, span], basis.at[j], basis_sems.at[j]).start()
    for d in range(planes):
        if routed:

            def fetch(i, carry):
                a, b = i // CG_DEV, i % CG_DEV
                pltpu.make_async_copy(
                    ins[0].at[slot_ref[d, i]], gran.at[d, a, b], in_sems.at[d]
                ).start()
                return carry

            lax.fori_loop(0, per_plane * CG_DEV, fetch, 0)
        else:
            pltpu.make_async_copy(ins[d], gran.at[d], in_sems.at[d]).start()
    low = lax.broadcasted_iota(jnp.int32, (half, LANES), 1) < BPHI
    for d in range(planes):
        pltpu.make_async_copy(gran.at[d], gran.at[d], in_sems.at[d]).wait()
        for j in range(per_plane // 2):
            for g in range(CG_DEV):
                even = gran[d, 2 * j, g]
                odd = gran[d, 2 * j + 1, g]
                first = jnp.concatenate([even[:, :BPHI], odd[:, :BPHI]], axis=1)
                second = jnp.concatenate([even[:, BPHI:], odd[:, BPHI:]], axis=1)
                lanes = pl.ds((d * per_plane + 2 * j) * BPHI, LANES)
                rows[pl.ds(2 * g * half, half), lanes] = first
                rows[pl.ds((2 * g + 1) * half, half), lanes] = second
    copies = []
    for j in range(chunks):
        pltpu.make_async_copy(basis.at[j], basis.at[j], basis_sems.at[j]).wait()
        if j >= 2:
            copies[j - 2].wait()
        acc[j % 2] = jnp.dot(rows[...], basis[j], preferred_element_type=jnp.float32).reshape(
            acc.shape[1:]
        )
        copy = pltpu.make_async_copy(
            acc.at[j % 2], out_hbm.at[field, :, :, pl.ds(j * wide, wide)], out_sems.at[j]
        )
        copy.start()
        copies.append(copy)
    for copy in copies[-2:]:
        copy.wait()


def transform(inputs, slot, basis, total, field, planes, per_plane):
    sliver = COLS // planes
    chunks = 4
    routed = slot is not None
    operands = ([slot] if routed else []) + list(inputs) + [basis]
    specs = ([SMEM] if routed else []) + [ANY] * (len(inputs) + 1)
    aliases = {}
    if total is not None:
        aliases = {len(operands): 0}
        operands.append(total)
        specs.append(ANY)
    wide = NPHI // chunks
    return pl.pallas_call(
        functools.partial(transform_kernel, planes, field, routed, total is not None),
        in_specs=specs,
        out_specs=ANY,
        out_shape=jax.ShapeDtypeStruct((FIELDS, CG_DEV, sliver, NPHI), jnp.float32),
        scratch_shapes=[
            pltpu.VMEM((planes, per_plane, CG_DEV, sliver // 2, LANES), jnp.bfloat16),
            pltpu.VMEM((CG_DEV * sliver, NPHI), jnp.bfloat16),
            pltpu.VMEM((chunks, NPHI, wide), jnp.bfloat16),
            pltpu.VMEM((2, CG_DEV, sliver, wide), jnp.float32),
            pltpu.SemaphoreType.DMA((planes,)),
            pltpu.SemaphoreType.DMA((chunks,)),
            pltpu.SemaphoreType.DMA((chunks,)),
        ],
        input_output_aliases=aliases,
        compiler_params=params(),
        name="transform",
    )(*operands)


def rank_of(dest):
    slots = dest.shape[-1]
    at = jnp.arange(slots, dtype=jnp.int32)
    same = (dest[..., :, None] == dest[..., None, :]) & (at[None, :] < at[:, None])
    return jnp.sum(same.astype(jnp.int32), axis=-1)


def local(blocks, levels, block_dest, block_phi, block_group):
    tiles = lax.axis_size("tile")
    planes = lax.axis_size("phi")
    tile = lax.axis_index("tile")
    plane = lax.axis_index("phi")
    slots = blocks.shape[0]
    per_plane = NPHI // BPHI // planes
    places = per_plane * CG_DEV
    capacity = 2 * slots // tiles
    me = plane.astype(jnp.int32).reshape(1)
    weight = 1.0 / jnp.left_shift(1, levels).astype(jnp.float32)

    def over_phi(parts):
        moved = [parts[0]]
        for d in range(1, planes):
            pairs = [(s, (s + d) % planes) for s in range(planes)]
            moved.append(lax.ppermute(parts[d], "phi", pairs))
        return moved

    def over_tile(box):
        return lax.all_to_all(box, "tile", split_axis=0, concat_axis=0, tiled=True)

    code = ((levels * tiles + block_dest) * per_plane + block_phi) * CG_DEV + block_group
    codes = lax.all_gather(code, ("tile", "phi"), axis=0, tiled=True)
    codes = codes.reshape(tiles, planes, slots)

    own_rank = rank_of(block_dest)
    later = tuple(range(FIRST, FIELDS))
    boxes = post(blocks, block_dest * capacity + own_rank, later, tiles * capacity)
    pieces = cut(blocks, weight, me, planes, FIRST)

    back = (plane - jnp.arange(planes, dtype=jnp.int32)) % planes
    near = jnp.take(codes, back, axis=1)
    dest = near // places % tiles
    rank = rank_of(dest)
    level = near // (places * tiles)
    here = (dest == tile)[..., None] & (
        (near % places)[..., None] == jnp.arange(places, dtype=jnp.int32)
    )
    from_tile = jnp.arange(tiles, dtype=jnp.int32)[:, None, None]
    distance = jnp.arange(planes, dtype=jnp.int32)[None, :, None]
    routed = (from_tile * planes + distance) * capacity + rank
    routed = jnp.sum(jnp.where(here, routed[..., None], 0), axis=(0, 2))
    arrived = from_tile[:, 0] * capacity + rank[:, 0]
    arrived = jnp.sum(jnp.where(here[:, 0], arrived[..., None], 0), axis=(0, 1))
    arrived_level = jnp.sum(jnp.where(here[:, 0], level[:, 0, :, None], 0), axis=(0, 1))
    arrived_weight = 1.0 / jnp.left_shift(1, arrived_level).astype(jnp.float32)
    out_dest = lax.dynamic_index_in_dim(dest, tile, 0, keepdims=False)
    out_rank = lax.dynamic_index_in_dim(rank, tile, 0, keepdims=False)
    out_slot = (out_dest * planes + distance[0]) * capacity + out_rank

    cell = jnp.arange(per_plane * BPHI, dtype=jnp.int32)
    basis = rotated_basis(NPHI, (back[:, None] * (per_plane * BPHI) + cell[None, :]).reshape(NPHI))

    sent = over_phi(pieces)
    outboxes = None
    parts = {}
    for f, box in zip(later, boxes):
        parts[f] = over_phi(sort(over_tile(box), arrived, arrived_weight, me, planes))
    outboxes = mail(sent, out_slot, tiles * planes * capacity)
    for f in range(FIRST):
        parts[f] = over_tile(outboxes[f])
    total = None
    for f in [2, 0, 3, 1, 4]:
        got = parts[f]
        if f < FIRST:
            total = transform([got], routed, basis, total, f, planes, per_plane)
        else:
            got = [g.reshape(per_plane, CG_DEV, *g.shape[1:]) for g in got]
            total = transform(got, None, basis, total, f, planes, per_plane)
    return total


def solution(mesh):
    in_specs = (
        P(("tile", "phi"), None, None, None),
        P(("tile", "phi")),
        P(("tile", "phi")),
        P(("tile", "phi")),
        P(("tile", "phi")),
    )
    out_specs = P(None, "tile", "phi", None)
    return jax.shard_map(local, mesh=mesh, in_specs=in_specs, out_specs=out_specs, check_vma=False)
```

time: 778 us -> 654 us (0.84)
  waiting for transfers between devices: 454 us -> 69 us
  Pallas kernels: 0 us -> 258 us
  blocking collectives: 0 us -> 216 us
  local copies, waits for them, and re-layouts: 198 us -> 0.66 us
  matrix products: 85.2 us -> 0 us
  other arithmetic: 13 us -> 74.6 us
  starting transfers between devices: 21.4 us -> 34.4 us
    all_to_all x4 -> x3, waiting for transfers between devices: 454 us -> 47.2 us  [over_tile(): return lax.all_to_all(box, 'tile', split_axis=0, concat_axis=0, tiled=True)]
    pallas_call x0 -> x11, Pallas kernels: none -> 258 us  [the longest x1 129 us: post(): pl.pallas_call(functools.partial(post_kernel, fields), in_specs=[SMEM, AN...]
    unnamed x0 -> x1, blocking collectives: none -> 110 us
    all_to_all x0 -> x2, blocking collectives: none -> 106 us  [over_tile(): return lax.all_to_all(box, 'tile', split_axis=0, concat_axis=0, tiled=True)]
    reshape x3 -> x2, local copies, waits for them, and re-layouts: 87.6 us -> 0.08 us  [local(): codes = codes.reshape(tiles, planes, slots)]
    dot_general x1 -> x0, matrix products: 85.2 us -> none  [local(): jnp.einsum('pnagbc,pabk->ngck', shaped, basis_table, preferred_element_ty...]
    scatter x4 -> x0, local copies, waits for them, and re-layouts: 69.9 us -> none  [the longest x1 43.8 us: local(): arranged = jnp.zeros((slot_count,) + blocks.shape[1:], jnp.bfloat16).at[r...]
    convert_element_type x2 -> x1, other arithmetic: 1.39 us -> 69.3 us  [rotated_basis(): return (values * jnp.float32(1.0 / math.sqrt(length))).astype(jnp.bfloat16)]
  transfers between devices with their start and end apart: 4 -> 15, of which waited for: 3 -> 4; matrix products, arithmetic and copies ran while one was open for 6% -> 11% of each run, Pallas kernels for 0% -> 19%
where the time goes in v1:
time: 654 us; the launch traced here: 653 us
  Pallas kernels  258 us (39%)
  blocking collectives  216 us (33%)
  other arithmetic  74.6 us (11%)
  waiting for transfers between devices  69 us (11%)
  starting transfers between devices  34.4 us (5%)
    pallas_call x1, Pallas kernels, post(): pl.pallas_call(functools.partial(post_kernel, fields), in_specs=[SMEM, AN...  129 us
    unnamed x1, blocking collectives  110 us
    all_to_all x2, blocking collectives, over_tile(): return lax.all_to_all(box, 'tile', split_axis=0, concat_axis=0, tiled=True)  106 us
    convert_element_type x1, other arithmetic, rotated_basis(): return (values * jnp.float32(1.0 / math.sqrt(length))).astype(jnp.bfloat16)  69.3 us
    all_to_all x3, waiting for transfers between devices, over_tile(): return lax.all_to_all(box, 'tile', split_axis=0, concat_axis=0, tiled=True)  47.2 us
    pallas_call x5, Pallas kernels, transform(): pl.pallas_call(functools.partial(transform_kernel, planes, field, routed,...  45.7 us
    pallas_call x3, Pallas kernels, sort(): pl.pallas_call(functools.partial(sort_kernel, planes), in_specs=[SMEM, SM...  35 us
    pallas_call x1, Pallas kernels, mail(): pl.pallas_call(functools.partial(mail_kernel, planes, count), in_specs=[S...  35 us
  transfers between devices with their start and end apart: 15, of which 4 were waited for; matrix products, arithmetic and copies ran while one was open for 11% of the time, Pallas kernels for 19%

profile of v1, /device:TPU:10, one launch (start us, length us, event | category | flops | bytes accessed | tf_op | source)
XLA Modules:
  0.0 652.6 jit_solution(4630042274842411323)
XLA Ops:
  0.0 0.9 convert_reduce_fusion.1
  0.9 0.8 multiply_add_fusion
  1.7 129.1 %post.1 = (bf16[128,64,256]{2,1,0:T(8,128)(2,1)S(1)}, bf16[128,64,256]{2,1,0:T(8,128)(2,1)}, bf16[128,64,256]{2,1,0:T(8,128)(2,1)}) custom-call(s32[64]{0:T(128)S(1)} %get-tuple-element.54.slot_ref, bf16[64,5,64,256]{3,2,1,0:T(8,128)(2,1)} %x_ref.3), custom_call_target="tpu_custom_call" | custom-call | tf_op jit(solution)/shard_map/post/pallas_call | solution.py:105
  130.9 52.6 %all_to_all.25.x_ref = bf16[128,64,256]{2,1,0:T(8,128)(2,1)} all-to-all(bf16[128,64,256]{2,1,0:T(8,128)(2,1)} %get-tuple-element.26), channel_id=1, replica_groups=mesh['tile'=8,'phi'=4] {'tile'}, dimensions={0} | all-to-all | bytes 8388608 | tf_op jit(solution)/shard_map/all_to_all | solution.py:307
  183.5 53.5 %all_to_all.26.x_ref = bf16[128,64,256]{2,1,0:T(8,128)(2,1)} all-to-all(bf16[128,64,256]{2,1,0:T(8,128)(2,1)} %get-tuple-element.36), channel_id=1, replica_groups=mesh['tile'=8,'phi'=4] {'tile'}, dimensions={0} | all-to-all | bytes 8388608 | tf_op jit(solution)/shard_map/all_to_all | solution.py:307
  237.1 5.9 all-to-all-start.4
  243.0 13.0 %cut.1 = (bf16[2,64,32,128]{3,2,1,0:T(8,128)(2,1)S(1)}, bf16[2,64,32,128]{3,2,1,0:T(8,128)(2,1)}, bf16[2,64,32,128]{3,2,1,0:T(8,128)(2,1)}, bf16[2,64,32,128]{3,2,1,0:T(8,128)(2,1)}) custom-call(s32[1]{0:T(128)} %bitcast.me_ref, f32[64]{0:T(128)S(1)} %convert_divide_fusion.weight_ref, bf16[64,5,64,256]{3,2,1,0:T(8,128)(2,1)} %x_ref.3), custom_call_target="tpu_custom_call" | custom-call | tf_op jit(solution)/shard_map/cut/pallas_call | solution.py:74
  256.0 1.6 collective-permute-start.3
  257.5 1.0 collective-permute-start.4
  258.6 2.0 collective-permute-start.5
  260.6 109.6 %all-reduce = s32[2048]{0:T(1024)S(1)} all-reduce(s32[2048]{0:T(1024)S(1)} %get-tuple-element.55), channel_id=1, replica_groups=mesh['tile'=8,'phi'=4] {'tile','phi'}, use_global_device_ids=true, to_apply=%add | all-reduce | flops 2048 | bytes 16384
  370.2 0.1 reshape.275
  370.3 0.6 gather_fusion
  370.9 0.1 broadcast_compare_fusion
  371.0 1.0 convert_reduce_fusion
  372.0 0.0 collective-permute-done.3.rest_1_
  372.0 35.0 %mail.1 = (bf16[512,32,128]{2,1,0:T(8,128)(2,1)}, bf16[512,32,128]{2,1,0:T(8,128)(2,1)}) custom-call(s32[4,64]{1,0:T(4,128)S(1)} %bitcast_add_fusion.slot_ref, bf16[2,64,32,128]{3,2,1,0:T(8,128)(2,1)S(1)} %get-tuple-element.31.rest_0_, bf16[2,64,32,128]{3,2,1,0:T(8,128)(2,1)S(1)} %collective-permute-done.3.rest_1_, ...), custom_call_target="tpu_custom_call" | custom-call | tf_op jit(solution)/shard_map/mail/pallas_call | solution.py:179
  407.0 4.5 all-to-all-start.3
  411.5 0.1 add_bitcast_fusion
  411.6 0.1 broadcast_add_fusion.1
  411.7 47.2 %all-to-all-done.3.refs_1_ = bf16[512,32,128]{2,1,0:T(8,128)(2,1)} async-done(((bf16[512,32,128]{2,1,0:T(8,128)(2,1)}), bf16[512,32,128]{2,1,0:T(8,128)(2,1)}, u32[]{:S(2)}, u32[]{:S(2)}) %all-to-all-start.3) | async-done | bytes 4194336 | tf_op jit(solution)/shard_map/all_to_all | solution.py:307
  458.9 6.0 all-to-all-start.1
  464.9 0.7 fusion.3
  465.6 0.2 select_reduce_fusion.1
  465.8 11.4 %sort.5 = (bf16[64,32,128]{2,1,0:T(8,128)(2,1)S(1)}, bf16[64,32,128]{2,1,0:T(8,128)(2,1)S(1)}, bf16[64,32,128]{2,1,0:T(8,128)(2,1)S(1)}, bf16[64,32,128]{2,1,0:T(8,128)(2,1)S(1)}) custom-call(s32[1]{0:T(128)} %bitcast.me_ref, s32[64]{0:T(128)S(1)} %get-tuple-element.48.slot_ref, f32[64]{0:T(128)S(1)} %convert_divide_fusion.1.weight_ref, ...), custom_call_target="tpu_custom_call" | custom-call | tf_op jit(solution)/shard_map/sort/pallas_call | solution.py:143
  477.2 1.4 collective-permute-start.9
  478.7 3.1 collective-permute-start.10
  481.8 0.5 collective-permute-start.11
  482.2 11.4 %sort.4 = (bf16[64,32,128]{2,1,0:T(8,128)(2,1)S(1)}, bf16[64,32,128]{2,1,0:T(8,128)(2,1)S(1)}, bf16[64,32,128]{2,1,0:T(8,128)(2,1)S(1)}, bf16[64,32,128]{2,1,0:T(8,128)(2,1)S(1)}) custom-call(s32[1]{0:T(128)} %bitcast.me_ref, s32[64]{0:T(128)S(1)} %get-tuple-element.48.slot_ref, f32[64]{0:T(128)S(1)} %convert_divide_fusion.1.weight_ref, ...), custom_call_target="tpu_custom_call" | custom-call | tf_op jit(solution)/shard_map/sort/pallas_call | solution.py:143
  493.6 1.6 collective-permute-start.6
  495.2 69.3 %multiply_convert_fusion.refs_4_.refs_2_ = bf16[2048,2048]{1,0:T(8,128)(2,1)} fusion(s32[2048]{0:T(1024)S(1)} %add_select_fusion.4, s32[2048]{0:T(1024)S(1)} %bitcast.57, pred[2048]{0:T(1024)(128)(4,1)S(1)} %iota_compare_fusion.2), kind=kLoop, calls=%fused_computation.9 | loop fusion | flops 71303168 | bytes 8407040 | tf_op jit(solution)/shard_map/convert_element_type | solution.py:33
  564.6 1.8 collective-permute-start.7
  566.4 12.2 %sort.3 = (bf16[64,32,128]{2,1,0:T(8,128)(2,1)S(1)}, bf16[64,32,128]{2,1,0:T(8,128)(2,1)}, bf16[64,32,128]{2,1,0:T(8,128)(2,1)S(1)}, bf16[64,32,128]{2,1,0:T(8,128)(2,1)S(1)}) custom-call(s32[1]{0:T(128)} %bitcast.me_ref, s32[64]{0:T(128)S(1)} %get-tuple-element.48.slot_ref, f32[64]{0:T(128)S(1)} %convert_divide_fusion.1.weight_ref, ...), custom_call_target="tpu_custom_call" | custom-call | tf_op jit(solution)/shard_map/sort/pallas_call | solution.py:143
  578.6 0.1 collective-permute-start.8
  578.7 2.0 collective-permute-start
  580.7 2.9 collective-permute-start.1
  583.6 0.0 collective-permute-start.2
  583.6 0.1 add_multiply_fusion
  583.7 0.1 broadcast_add_fusion
  583.8 1.1 select_reduce_fusion.refs_0_
  584.9 7.7 %transform.5.refs_3_ = f32[5,8,64,2048]{3,2,1,0:T(8,128)} custom-call(bf16[8,8,32,128]{3,2,1,0:T(8,128)(2,1)S(1)} %bitcast.44, bf16[8,8,32,128]{3,2,1,0:T(8,128)(2,1)S(1)} %bitcast.46, bf16[8,8,32,128]{3,2,1,0:T(8,128)(2,1)S(1)} %bitcast.48, bf16[8,8,32,128]{3,2,1,0:T(8,128)(2,1)S(1)} %bitcast.49, bf16[2048,2048]{1,0:T(8,128)(2,1)} %multiply_convert_fusion.refs_4_.refs_2_), custom_call_target="tpu_custom_call" | custom-call | tf_op jit(solution)/shard_map/transform/pallas_call | solution.py:260
  592.6 11.3 %transform.6.refs_5_ = f32[5,8,64,2048]{3,2,1,0:T(8,128)} custom-call(s32[4,64]{1,0:T(4,128)S(1)} %select_reduce_fusion.refs_0_, bf16[512,32,128]{2,1,0:T(8,128)(2,1)} %all-to-all-done.3.refs_1_, bf16[2048,2048]{1,0:T(8,128)(2,1)} %multiply_convert_fusion.refs_4_.refs_2_, f32[5,8,64,2048]{3,2,1,0:T(8,128)} %transform.5.refs_3_), custom_call_target="tpu_custom_call", output_to_operand_aliasing={{}: (3, {})} | custom-call | tf_op jit(solution)/shard_map/transform/pallas_call | solution.py:260
  603.9 19.5 %collective-permute-done.8 = bf16[64,32,128]{2,1,0:T(8,128)(2,1)S(1)} collective-permute-done((bf16[64,32,128]{2,1,0:T(8,128)(2,1)S(1)}, bf16[64,32,128]{2,1,0:T(8,128)(2,1)S(1)}, u32[]{:S(2)}, u32[]{:S(2)}) %collective-permute-start.8) | collective-permute-done | bytes 524320 | tf_op jit(solution)/shard_map/ppermute | solution.py:303
  623.5 7.7 %transform.7.refs_3_ = f32[5,8,64,2048]{3,2,1,0:T(8,128)} custom-call(bf16[8,8,32,128]{3,2,1,0:T(8,128)(2,1)S(1)} %bitcast.45, bf16[8,8,32,128]{3,2,1,0:T(8,128)(2,1)S(1)} %bitcast.47, bf16[8,8,32,128]{3,2,1,0:T(8,128)(2,1)S(1)} %bitcast.51, bf16[8,8,32,128]{3,2,1,0:T(8,128)(2,1)S(1)} %bitcast.54, ...), custom_call_target="tpu_custom_call", output_to_operand_aliasing={{}: (5, {})} | custom-call | tf_op jit(solution)/shard_map/transform/pallas_call | solution.py:260
  631.2 11.3 %transform.8.refs_5_ = f32[5,8,64,2048]{3,2,1,0:T(8,128)} custom-call(s32[4,64]{1,0:T(4,128)S(1)} %select_reduce_fusion.refs_0_, bf16[512,32,128]{2,1,0:T(8,128)(2,1)} %all-to-all-done.1.refs_1_, bf16[2048,2048]{1,0:T(8,128)(2,1)} %multiply_convert_fusion.refs_4_.refs_2_, f32[5,8,64,2048]{3,2,1,0:T(8,128)} %transform.7.refs_3_), custom_call_target="tpu_custom_call", output_to_operand_aliasing={{}: (3, {})} | custom-call | tf_op jit(solution)/shard_map/transform/pallas_call | solution.py:260
  642.5 1.2 collective-permute-done.1
  643.7 1.1 collective-permute-done.2
  644.8 7.7 %transform.9 = f32[5,8,64,2048]{3,2,1,0:T(8,128)} custom-call(bf16[8,8,32,128]{3,2,1,0:T(8,128)(2,1)S(1)} %bitcast.43, bf16[8,8,32,128]{3,2,1,0:T(8,128)(2,1)S(1)} %bitcast.50, bf16[8,8,32,128]{3,2,1,0:T(8,128)(2,1)S(1)} %bitcast.52, bf16[8,8,32,128]{3,2,1,0:T(8,128)(2,1)S(1)} %bitcast.53, ...), custom_call_target="tpu_custom_call", output_to_operand_aliasing={{}: (5, {})} | custom-call | tf_op jit(solution)/shard_map/transform/pallas_call | solution.py:260
  (32 shorter events, 0.2 us)
Async XLA Ops:
  1.7 241.3 %copy-start.1 = (s32[64]{0:T(128)S(1)}, s32[64]{0:T(128)}, u32[]{:S(2)}) copy-start(s32[64]{0:T(128)} %param.6) | copy-start | bytes 772
  130.9 106.2 %copy-start = (bf16[128,64,256]{2,1,0:T(8,128)(2,1)}, bf16[128,64,256]{2,1,0:T(8,128)(2,1)S(1)}, u32[]{:S(2)}) copy-start(bf16[128,64,256]{2,1,0:T(8,128)(2,1)S(1)} %get-tuple-element.42) | copy-start | bytes 12582916
  237.1 169.9 %all-to-all-start.4 = ((bf16[128,64,256]{2,1,0:T(8,128)(2,1)}), bf16[128,64,256]{2,1,0:T(8,128)(2,1)}, u32[]{:S(2)}, u32[]{:S(2)}) async-start(bf16[128,64,256]{2,1,0:T(8,128)(2,1)} %copy-done), calls=%async_computation.4 | async-start | bytes 8388608 | tf_op jit(solution)/shard_map/all_to_all | solution.py:307
  256.0 116.0 %collective-permute-start.3 = (bf16[2,64,32,128]{3,2,1,0:T(8,128)(2,1)}, bf16[2,64,32,128]{3,2,1,0:T(8,128)(2,1)S(1)}, u32[]{:S(2)}, u32[]{:S(2)}) collective-permute-start(bf16[2,64,32,128]{3,2,1,0:T(8,128)(2,1)} %get-tuple-element.32), channel_id=1, source_target_pairs={{0,1},{1,2},{2,3},{3,0},{4,5},{5,6},{6,7},{7,4},{8,9},{9,10},{10,1... | collective-permute-start | bytes 3145736 | tf_op jit(solution)/shard_map/ppermute | solution.py:303
  257.5 114.5 %collective-permute-start.4 = (bf16[2,64,32,128]{3,2,1,0:T(8,128)(2,1)}, bf16[2,64,32,128]{3,2,1,0:T(8,128)(2,1)S(1)}, u32[]{:S(2)}, u32[]{:S(2)}) collective-permute-start(bf16[2,64,32,128]{3,2,1,0:T(8,128)(2,1)} %get-tuple-element.33), channel_id=1, source_target_pairs={{0,2},{1,3},{2,0},{3,1},{4,6},{5,7},{6,4},{7,5},{8,10},{9,11},{10,... | collective-permute-start | bytes 3145736 | tf_op jit(solution)/shard_map/ppermute | solution.py:303
  258.6 113.4 %collective-permute-start.5 = (bf16[2,64,32,128]{3,2,1,0:T(8,128)(2,1)}, bf16[2,64,32,128]{3,2,1,0:T(8,128)(2,1)}, u32[]{:S(2)}, u32[]{:S(2)}) collective-permute-start(bf16[2,64,32,128]{3,2,1,0:T(8,128)(2,1)} %get-tuple-element.34), channel_id=1, source_target_pairs={{0,3},{1,0},{2,1},{3,2},{4,7},{5,4},{6,5},{7,6},{8,11},{9,8},{10,9... | collective-permute-start | bytes 3145736 | tf_op jit(solution)/shard_map/ppermute | solution.py:303
  407.0 52.0 %all-to-all-start.3 = ((bf16[512,32,128]{2,1,0:T(8,128)(2,1)}), bf16[512,32,128]{2,1,0:T(8,128)(2,1)}, u32[]{:S(2)}, u32[]{:S(2)}) async-start(bf16[512,32,128]{2,1,0:T(8,128)(2,1)} %get-tuple-element.41), calls=%async_computation.3 | async-start | bytes 8388608 | tf_op jit(solution)/shard_map/all_to_all | solution.py:307
  458.9 172.2 %all-to-all-start.1 = ((bf16[512,32,128]{2,1,0:T(8,128)(2,1)}), bf16[512,32,128]{2,1,0:T(8,128)(2,1)}, u32[]{:S(2)}, u32[]{:S(2)}) async-start(bf16[512,32,128]{2,1,0:T(8,128)(2,1)} %get-tuple-element.35), calls=%async_computation.1 | async-start | bytes 8388608 | tf_op jit(solution)/shard_map/all_to_all | solution.py:307
  477.2 101.4 %collective-permute-start.9 = (bf16[64,32,128]{2,1,0:T(8,128)(2,1)S(1)}, bf16[64,32,128]{2,1,0:T(8,128)(2,1)S(1)}, u32[]{:S(2)}, u32[]{:S(2)}) collective-permute-start(bf16[64,32,128]{2,1,0:T(8,128)(2,1)S(1)} %get-tuple-element.44), channel_id=1, source_target_pairs={{0,1},{1,2},{2,3},{3,0},{4,5},{5,6},{6,7},{7,4},{8,9},{9,10},{10,1... | collective-permute-start | bytes 1572872 | tf_op jit(solution)/shard_map/ppermute | solution.py:303
  478.7 100.0 %collective-permute-start.10 = (bf16[64,32,128]{2,1,0:T(8,128)(2,1)S(1)}, bf16[64,32,128]{2,1,0:T(8,128)(2,1)S(1)}, u32[]{:S(2)}, u32[]{:S(2)}) collective-permute-start(bf16[64,32,128]{2,1,0:T(8,128)(2,1)S(1)} %get-tuple-element.45), channel_id=1, source_target_pairs={{0,2},{1,3},{2,0},{3,1},{4,6},{5,7},{6,4},{7,5},{8,10},{9,11},{10,... | collective-permute-start | bytes 1572872 | tf_op jit(solution)/shard_map/ppermute | solution.py:303
  481.8 98.9 %collective-permute-start.11 = (bf16[64,32,128]{2,1,0:T(8,128)(2,1)S(1)}, bf16[64,32,128]{2,1,0:T(8,128)(2,1)S(1)}, u32[]{:S(2)}, u32[]{:S(2)}) collective-permute-start(bf16[64,32,128]{2,1,0:T(8,128)(2,1)S(1)} %get-tuple-element.46), channel_id=1, source_target_pairs={{0,3},{1,0},{2,1},{3,2},{4,7},{5,4},{6,5},{7,6},{8,11},{9,8},{10,9... | collective-permute-start | bytes 1572872 | tf_op jit(solution)/shard_map/ppermute | solution.py:303
  493.6 90.0 %collective-permute-start.6 = (bf16[64,32,128]{2,1,0:T(8,128)(2,1)S(1)}, bf16[64,32,128]{2,1,0:T(8,128)(2,1)S(1)}, u32[]{:S(2)}, u32[]{:S(2)}) collective-permute-start(bf16[64,32,128]{2,1,0:T(8,128)(2,1)S(1)} %get-tuple-element.38), channel_id=1, source_target_pairs={{0,1},{1,2},{2,3},{3,0},{4,5},{5,6},{6,7},{7,4},{8,9},{9,10},{10,1... | collective-permute-start | bytes 1572872 | tf_op jit(solution)/shard_map/ppermute | solution.py:303
  564.6 39.4 %collective-permute-start.7 = (bf16[64,32,128]{2,1,0:T(8,128)(2,1)S(1)}, bf16[64,32,128]{2,1,0:T(8,128)(2,1)S(1)}, u32[]{:S(2)}, u32[]{:S(2)}) collective-permute-start(bf16[64,32,128]{2,1,0:T(8,128)(2,1)S(1)} %get-tuple-element.39), channel_id=1, source_target_pairs={{0,2},{1,3},{2,0},{3,1},{4,6},{5,7},{6,4},{7,5},{8,10},{9,11},{10,... | collective-permute-start | bytes 1572872 | tf_op jit(solution)/shard_map/ppermute | solution.py:303
  578.6 44.9 %collective-permute-start.8 = (bf16[64,32,128]{2,1,0:T(8,128)(2,1)S(1)}, bf16[64,32,128]{2,1,0:T(8,128)(2,1)S(1)}, u32[]{:S(2)}, u32[]{:S(2)}) collective-permute-start(bf16[64,32,128]{2,1,0:T(8,128)(2,1)S(1)} %get-tuple-element.40), channel_id=1, source_target_pairs={{0,3},{1,0},{2,1},{3,2},{4,7},{5,4},{6,5},{7,6},{8,11},{9,8},{10,9... | collective-permute-start | bytes 1572872 | tf_op jit(solution)/shard_map/ppermute | solution.py:303
  578.7 63.8 %collective-permute-start = (bf16[64,32,128]{2,1,0:T(8,128)(2,1)}, bf16[64,32,128]{2,1,0:T(8,128)(2,1)S(1)}, u32[]{:S(2)}, u32[]{:S(2)}) collective-permute-start(bf16[64,32,128]{2,1,0:T(8,128)(2,1)} %get-tuple-element.28), channel_id=1, source_target_pairs={{0,1},{1,2},{2,3},{3,0},{4,5},{5,6},{6,7},{7,4},{8,9},{9,10},{10,1... | collective-permute-start | bytes 1572872 | tf_op jit(solution)/shard_map/ppermute | solution.py:303
  580.7 63.0 %collective-permute-start.1 = (bf16[64,32,128]{2,1,0:T(8,128)(2,1)S(1)}, bf16[64,32,128]{2,1,0:T(8,128)(2,1)S(1)}, u32[]{:S(2)}, u32[]{:S(2)}) collective-permute-start(bf16[64,32,128]{2,1,0:T(8,128)(2,1)S(1)} %get-tuple-element.29), channel_id=1, source_target_pairs={{0,2},{1,3},{2,0},{3,1},{4,6},{5,7},{6,4},{7,5},{8,10},{9,11},{10,... | collective-permute-start | bytes 1572872 | tf_op jit(solution)/shard_map/ppermute | solution.py:303
  583.6 61.2 %collective-permute-start.2 = (bf16[64,32,128]{2,1,0:T(8,128)(2,1)S(1)}, bf16[64,32,128]{2,1,0:T(8,128)(2,1)S(1)}, u32[]{:S(2)}, u32[]{:S(2)}) collective-permute-start(bf16[64,32,128]{2,1,0:T(8,128)(2,1)S(1)} %get-tuple-element.30), channel_id=1, source_target_pairs={{0,3},{1,0},{2,1},{3,2},{4,7},{5,4},{6,5},{7,6},{8,11},{9,8},{10,9... | collective-permute-start | bytes 1572872 | tf_op jit(solution)/shard_map/ppermute | solution.py:303

commit v2 on v0

v2 whole, which is shorter than its diff:
```python
import functools
import math

import jax
import jax.numpy as jnp
from jax import lax
from jax.experimental import pallas as pl
from jax.experimental.pallas import tpu as pltpu
from jax.sharding import PartitionSpec as P

FIELDS = 5
NPHI = 2048
BPHI = 64
COLS = 256
CG_DEV = 8
LANES = 128
NOTE = 16
PAIR = (0, 1)
GROUPS = ((2, 3), (4,))
VMEM_BYTES = 32 * 1024 * 1024
SPANS = 4
LIGHT = pl.CostEstimate(flops=0, bytes_accessed=0, transcendentals=0)

ANY = pl.BlockSpec(memory_space=pl.ANY)
HBM = pl.BlockSpec(memory_space=pltpu.HBM)
SMEM = pl.BlockSpec(memory_space=pltpu.SMEM)
VMEM = pl.BlockSpec(memory_space=pltpu.VMEM)


def rotated_basis(length, back):
    planes = back.shape[0]
    per = length // planes
    column = jnp.arange(length, dtype=jnp.int32)
    half = length // 2
    mode = jnp.where(column <= half, column, column - half)
    coarse = (back[:, None] * per + jnp.arange(0, per, BPHI, dtype=jnp.int32)[None, :]).reshape(-1)
    fine = jnp.arange(BPHI, dtype=jnp.int32)

    def angle(row):
        phase = row[:, None] * mode[None, :] % length
        return phase.astype(jnp.float32) * jnp.float32(2.0 * math.pi / length)

    even = (column <= half)[None, :]
    scale = jnp.float32(1.0 / math.sqrt(length))
    far, near = angle(coarse), angle(fine)
    by_cos = jnp.where(even, jnp.cos(far), jnp.sin(far)) * scale
    by_sin = jnp.where(even, -jnp.sin(far), jnp.cos(far)) * scale
    near_cos, near_sin = jnp.cos(near), jnp.sin(near)

    def spans(x):
        return x.reshape(x.shape[0], SPANS, length // SPANS).transpose(1, 0, 2)

    by_cos, by_sin = spans(by_cos)[:, :, None], spans(by_sin)[:, :, None]
    near_cos, near_sin = spans(near_cos)[:, None], spans(near_sin)[:, None]
    by_cos, by_sin, near_cos, near_sin = lax.optimization_barrier((by_cos, by_sin, near_cos, near_sin))
    table = by_cos * near_cos + by_sin * near_sin
    return table.reshape(SPANS, length, length // SPANS).astype(jnp.bfloat16)


def in_hbm(*arrays):
    return [pltpu.with_memory_space_constraint(a, pltpu.HBM) for a in arrays]


def params():
    return pltpu.CompilerParams(vmem_limit_bytes=VMEM_BYTES)


def scaled(block, weight):
    return block * jnp.full((1, 1), weight, jnp.float32).astype(jnp.bfloat16)


def cut_kernel(planes, chunk, me_ref, weight_ref, x_ref, *outs):
    base = pl.program_id(0) * chunk
    sliver = COLS // planes
    for mine in range(planes):

        @pl.when(me_ref[0] == mine)
        def _():
            def body(i, carry):
                x = scaled(x_ref[i].reshape(LANES, COLS), weight_ref[base + i]).T
                for p in range(planes):
                    outs[(p - mine) % planes][i] = x[p * sliver : (p + 1) * sliver]
                return carry

            lax.fori_loop(0, chunk, body, 0, unroll=4)


def cut(blocks, weight, me, planes):
    slots = blocks.shape[0]
    chunk = 16
    sliver = COLS // planes
    return pl.pallas_call(
        functools.partial(cut_kernel, planes, chunk),
        grid=(slots // chunk,),
        in_specs=[SMEM, SMEM, pl.BlockSpec((chunk, 2, BPHI, COLS), lambda i: (i, 0, 0, 0))],
        out_specs=[pl.BlockSpec((chunk, sliver, LANES), lambda i: (i, 0, 0))] * planes,
        out_shape=[pltpu.HBM((slots, sliver, LANES), jnp.bfloat16)] * planes,
        compiler_params=params(),
        cost_estimate=LIGHT,
        name="cut",
    )(me, weight, *in_hbm(blocks))


def post_kernel(fields, tiles, capacity, slot_ref, note_ref, x_ref, out_ref, box_ref, buf, sems, out_sems):
    slots = slot_ref.shape[0]
    count = len(fields)
    rows = count * BPHI
    parts = sems.shape[0]
    some = slots // parts
    for k in range(parts):
        span = pl.ds(k * some, some)
        source = x_ref.at[span, pl.ds(fields[0], count)]
        pltpu.make_async_copy(source, buf.at[span], sems.at[k]).start()
    for t in range(tiles):
        box_ref[t, pl.ds(capacity * rows, NOTE)] = note_ref[...]
    for k in range(parts):
        span = pl.ds(k * some, some)
        pltpu.make_async_copy(buf.at[span], buf.at[span], sems.at[k]).wait()

        def body(i, carry):
            to = slot_ref[i]
            row = pl.multiple_of((to % capacity) * rows, rows)
            box_ref[to // capacity, pl.ds(row, rows)] = buf[i].reshape(rows, COLS)
            return carry

        lax.fori_loop(k * some, (k + 1) * some, body, 0)
    for t in range(tiles):
        pltpu.make_async_copy(box_ref.at[t], out_ref.at[t], out_sems.at[t]).start()
    for t in range(tiles):
        pltpu.make_async_copy(box_ref.at[t], out_ref.at[t], out_sems.at[t]).wait()


def post(blocks, slot, note, fields, tiles, capacity):
    slots = blocks.shape[0]
    rows = capacity * len(fields) * BPHI + NOTE
    return pl.pallas_call(
        functools.partial(post_kernel, fields, tiles, capacity),
        in_specs=[SMEM, VMEM, ANY],
        out_specs=HBM,
        out_shape=pltpu.HBM((tiles, rows, COLS), jnp.bfloat16),
        scratch_shapes=[
            pltpu.VMEM((tiles, rows, COLS), jnp.bfloat16),
            pltpu.VMEM((slots, len(fields), BPHI, COLS), jnp.bfloat16),
            pltpu.SemaphoreType.DMA((4,)),
            pltpu.SemaphoreType.DMA((tiles,)),
        ],
        compiler_params=params(),
        cost_estimate=LIGHT,
        name="post",
    )(slot, note, *in_hbm(blocks))


def sort_kernel(planes, count, capacity, me_ref, slot_ref, weight_ref, x_ref, *rest):
    outs, (buf, made, sems, out_sems) = rest[:-4], rest[-4:]
    tiles = buf.shape[0]
    per_plane = slot_ref.shape[0] // CG_DEV
    sliver = COLS // planes
    rows = count * BPHI
    me = me_ref[0]
    for t in range(tiles):
        pltpu.make_async_copy(x_ref.at[t], buf.at[t], sems.at[t]).start()
    for t in range(tiles):
        pltpu.make_async_copy(buf.at[t], buf.at[t], sems.at[t]).wait()

    def block(place, f):
        at = slot_ref[place]
        row = pl.multiple_of((at % capacity) * rows + f * BPHI, BPHI)
        return scaled(buf[at // capacity, pl.ds(row, BPHI)], weight_ref[place])

    for f in range(count):
        for j in range(per_plane // 2):

            def body(g, carry):
                even = block(2 * j * CG_DEV + g, f)
                odd = block((2 * j + 1) * CG_DEV + g, f)
                x = jnp.concatenate([even, odd], axis=0).T
                to = pl.ds(pl.multiple_of(g * sliver, sliver), sliver)
                for p in range(planes):
                    distance = (p - me + planes) % planes
                    made[f, distance, to, pl.ds(j * LANES, LANES)] = x[
                        p * sliver : (p + 1) * sliver
                    ]
                return carry

            lax.fori_loop(0, CG_DEV, body, 0, unroll=4)
        for d in range(planes):
            n = f * planes + d
            pltpu.make_async_copy(made.at[f, d], outs[d].at[f], out_sems.at[n]).start()
    for f in range(count):
        for d in range(planes):
            n = f * planes + d
            pltpu.make_async_copy(made.at[f, d], outs[d].at[f], out_sems.at[n]).wait()


def sort(arrived, slot, weight, me, planes, count, capacity):
    cells = slot.shape[0] // CG_DEV * BPHI
    slab = (CG_DEV * (COLS // planes), cells)
    return pl.pallas_call(
        functools.partial(sort_kernel, planes, count, capacity),
        in_specs=[SMEM, SMEM, SMEM, ANY],
        out_specs=[HBM] * planes,
        out_shape=[pltpu.HBM((count,) + slab, jnp.bfloat16)] * planes,
        scratch_shapes=[
            pltpu.VMEM(arrived.shape, jnp.bfloat16),
            pltpu.VMEM((count, planes) + slab, jnp.bfloat16),
            pltpu.SemaphoreType.DMA((arrived.shape[0],)),
            pltpu.SemaphoreType.DMA((count * planes,)),
        ],
        compiler_params=params(),
        cost_estimate=LIGHT,
        name="sort",
    )(me, slot, weight, *in_hbm(arrived))


def mail_kernel(planes, tiles, capacity, slot_ref, *rest):
    ins, (out_ref, box_ref, buf, sems, out_sems) = rest[:planes], rest[planes:]
    slots, sliver, _ = ins[0].shape
    for d in range(planes):
        pltpu.make_async_copy(ins[d], buf.at[d], sems.at[d]).start()
    for d in range(planes):
        pltpu.make_async_copy(buf.at[d], buf.at[d], sems.at[d]).wait()

        def body(i, carry):
            to = slot_ref[d, i]
            row = pl.multiple_of((to % (planes * capacity)) * sliver, sliver)
            box_ref[to // (planes * capacity), pl.ds(row, sliver)] = buf[d, i]
            return carry

        lax.fori_loop(0, slots, body, 0, unroll=4)
    for t in range(tiles):
        pltpu.make_async_copy(box_ref.at[t], out_ref.at[t], out_sems.at[t]).start()
    for t in range(tiles):
        pltpu.make_async_copy(box_ref.at[t], out_ref.at[t], out_sems.at[t]).wait()


def mail(parts, slot, tiles, capacity):
    planes = len(parts)
    slots, sliver, _ = parts[0].shape
    rows = planes * capacity * sliver
    return pl.pallas_call(
        functools.partial(mail_kernel, planes, tiles, capacity),
        in_specs=[SMEM] + [ANY] * planes,
        out_specs=HBM,
        out_shape=pltpu.HBM((tiles, rows, LANES), jnp.bfloat16),
        scratch_shapes=[
            pltpu.VMEM((tiles, rows, LANES), jnp.bfloat16),
            pltpu.VMEM((planes, slots, sliver, LANES), jnp.bfloat16),
            pltpu.SemaphoreType.DMA((planes,)),
            pltpu.SemaphoreType.DMA((tiles,)),
        ],
        compiler_params=params(),
        cost_estimate=LIGHT,
        name="mail",
    )(slot, *in_hbm(*parts))


def load_basis(basis_hbm, basis, sems):
    for j in range(SPANS):
        pltpu.make_async_copy(basis_hbm.at[j], basis.at[j], sems.at[j]).start()


def multiply(fields, base, basis, out_hbm, rows, acc, basis_sems, sems, steps=0, beside=None):
    wide = acc.shape[-1]
    copies = []
    for f in range(fields):
        for j in range(SPANS):
            n = len(copies)
            if f == 0:
                pltpu.make_async_copy(basis.at[j], basis.at[j], basis_sems.at[j]).wait()
                for step in range(j * steps // SPANS, (j + 1) * steps // SPANS):
                    beside(step)
            if n >= 2:
                copies[n - 2].wait()
            acc[n % 2] = jnp.dot(
                rows[f], basis[j], preferred_element_type=jnp.float32
            ).reshape(acc.shape[1:])
            copy = pltpu.make_async_copy(
                acc.at[n % 2], out_hbm.at[base + f, :, :, pl.ds(j * wide, wide)], sems.at[n % 2]
            )
            copy.start()
            copies.append(copy)
    for copy in copies[-2:]:
        copy.wait()


def rows_kernel(planes, take, base, chained, *refs):
    ins, basis_hbm = refs[:planes], refs[planes]
    out_hbm, rows, basis, acc, basis_sems, out_sems, in_sems = refs[planes + 1 + chained :]
    cells = ins[0].shape[2]
    for d in range(planes):
        to = rows.at[0, :, pl.ds(d * cells, cells)]
        pltpu.make_async_copy(ins[d].at[take], to, in_sems.at[d]).start()
    load_basis(basis_hbm, basis, basis_sems)
    for d in range(planes):
        to = rows.at[0, :, pl.ds(d * cells, cells)]
        pltpu.make_async_copy(to, to, in_sems.at[d]).wait()
    multiply(1, base, basis, out_hbm, rows, acc, basis_sems, out_sems)


def box_kernel(planes, per_plane, capacity, base, chained, *refs):
    slot_ref, box_hbm, basis_hbm = refs[:3]
    out_hbm, rows, basis, acc, basis_sems, out_sems, box, in_sems = refs[3 + chained :]
    tiles = box.shape[0]
    sliver = COLS // planes
    for t in range(tiles):
        pltpu.make_async_copy(box_hbm.at[t], box.at[t], in_sems.at[t]).start()
    load_basis(basis_hbm, basis, basis_sems)
    for t in range(tiles):
        pltpu.make_async_copy(box.at[t], box.at[t], in_sems.at[t]).wait()

    def piece(d, place):
        at = slot_ref[d, place]
        row = pl.multiple_of((at % (planes * capacity)) * sliver, sliver)
        return box[at // (planes * capacity), pl.ds(row, sliver)]

    def gather(field, d):
        cells = slice(0, BPHI) if field == 0 else slice(BPHI, LANES)
        for j in range(per_plane // 2):
            lanes = pl.ds((d * per_plane + 2 * j) * BPHI, LANES)
            for g in range(CG_DEV):
                even = piece(d, 2 * j * CG_DEV + g)
                odd = piece(d, (2 * j + 1) * CG_DEV + g)
                both = jnp.concatenate([even[:, cells], odd[:, cells]], axis=1)
                rows[field, pl.ds(g * sliver, sliver), lanes] = both

    for d in range(planes):
        gather(0, d)
    multiply(
        2, base, basis, out_hbm, rows, acc, basis_sems, out_sems, planes, lambda d: gather(1, d)
    )


def transform(kernel, operands, specs, total, basis, fields, planes, scratch, name):
    sliver = COLS // planes
    operands = operands + in_hbm(basis)
    specs = specs + [ANY]
    aliases = {}
    if total is not None:
        aliases = {len(operands): 0}
        operands, specs = operands + [total], specs + [ANY]
    return pl.pallas_call(
        kernel,
        in_specs=specs,
        out_specs=HBM,
        out_shape=pltpu.HBM((FIELDS, CG_DEV, sliver, NPHI), jnp.float32),
        scratch_shapes=[
            pltpu.VMEM((fields, CG_DEV * sliver, NPHI), jnp.bfloat16),
            pltpu.VMEM((SPANS, NPHI, NPHI // SPANS), jnp.bfloat16),
            pltpu.VMEM((2, CG_DEV, sliver, NPHI // SPANS), jnp.float32),
            pltpu.SemaphoreType.DMA((SPANS,)),
            pltpu.SemaphoreType.DMA((2,)),
        ]
        + scratch,
        input_output_aliases=aliases,
        compiler_params=params(),
        cost_estimate=LIGHT,
        name=name,
    )(*operands)


def transform_rows(slabs, take, basis, total, base):
    planes = len(slabs)
    kernel = functools.partial(rows_kernel, planes, take, base, int(total is not None))
    scratch = [pltpu.SemaphoreType.DMA((planes,))]
    return transform(
        kernel, in_hbm(*slabs), [ANY] * planes, total, basis, 1, planes, scratch, "rows"
    )


def transform_box(box, slot, basis, total, base, per_plane, capacity):
    planes = slot.shape[0]
    kernel = functools.partial(box_kernel, planes, per_plane, capacity, base, int(total is not None))
    scratch = [pltpu.VMEM(box.shape, jnp.bfloat16), pltpu.SemaphoreType.DMA((box.shape[0],))]
    return transform(kernel, [slot] + in_hbm(box), [SMEM, ANY], total, basis, 2, planes, scratch, "box")


def rank_of(dest):
    slots = dest.shape[-1]
    at = jnp.arange(slots, dtype=jnp.int32)
    same = (dest[..., :, None] == dest[..., None, :]) & (at[None, :] < at[:, None])
    return jnp.sum(same.astype(jnp.int32), axis=-1)


def as_note(dest, place_level, width):
    count = dest.size
    pad = -count % width
    each = (count + pad) // width
    codes = [jnp.pad(c.reshape(-1), (0, pad)).reshape(each, width) for c in (dest, place_level)]
    both = jnp.concatenate(codes, axis=0)
    return jnp.pad(both, ((0, NOTE - 2 * each), (0, 0))).astype(jnp.bfloat16)


def from_note(box, count):
    width = box.shape[2]
    each = -(-count // width)
    note = box[:, box.shape[1] - NOTE :, :].astype(jnp.float32).astype(jnp.int32)
    dest = note[:, :each].reshape(-1, each * width)[:, :count]
    place_level = note[:, each : 2 * each].reshape(-1, each * width)[:, :count]
    return dest, place_level


def local(blocks, levels, block_dest, block_phi, block_group):
    tiles = lax.axis_size("tile")
    planes = lax.axis_size("phi")
    tile = lax.axis_index("tile")
    plane = lax.axis_index("phi")
    slots = blocks.shape[0]
    per_plane = NPHI // BPHI // planes
    places = per_plane * CG_DEV
    capacity = 2 * slots // tiles
    me = plane.astype(jnp.int32).reshape(1)
    weight = 1.0 / jnp.left_shift(1, levels).astype(jnp.float32)
    place_iota = jnp.arange(places, dtype=jnp.int32)

    def over_phi(parts):
        moved = [parts[0]]
        for d in range(1, planes):
            pairs = [(s, (s + d) % planes) for s in range(planes)]
            moved.append(lax.ppermute(parts[d], "phi", pairs))
        return moved

    def over_tile(box):
        return lax.all_to_all(box, "tile", split_axis=0, concat_axis=0, tiled=True)

    def tie(value, *others):
        return lax.optimization_barrier((value,) + others)[0]

    place_level = levels * places + block_phi * CG_DEV + block_group
    own_slot = block_dest * capacity + rank_of(block_dest)
    own_note = as_note(block_dest, place_level, COLS)
    box = post(blocks, own_slot, own_note, GROUPS[0], tiles, capacity)
    pieces = cut(blocks, weight, me, planes)

    back = (plane - jnp.arange(planes, dtype=jnp.int32)) % planes
    basis = rotated_basis(NPHI, back)

    code = tie(block_dest * (4 * places) + place_level, pieces[0])
    codes = jnp.stack(over_phi([code] * planes))
    dest = codes // (4 * places)
    distance = jnp.arange(planes, dtype=jnp.int32)[:, None]
    out_slot = (dest * planes + distance) * capacity + rank_of(dest)
    out_note = as_note(dest, codes % (4 * places), COLS)
    next_box = post(blocks, own_slot, out_note, GROUPS[1], tiles, capacity)

    first = over_tile(box)
    sent = over_phi(pieces)
    second = over_tile(tie(next_box, first, basis, *sent))

    got_dest, got_code = from_note(first, slots)
    got_slot = jnp.arange(tiles, dtype=jnp.int32)[:, None] * capacity + rank_of(got_dest)
    here = (got_dest == tile)[..., None] & ((got_code % places)[..., None] == place_iota)
    slot = jnp.sum(jnp.where(here, got_slot[..., None], 0), axis=(0, 1))
    level = jnp.sum(jnp.where(here, (got_code // places)[..., None], 0), axis=(0, 1))
    got_weight = 1.0 / jnp.left_shift(1, level).astype(jnp.float32)

    outbox = mail(sent, out_slot, tiles, capacity)
    early = over_phi(sort(first, slot, got_weight, me, planes, 2, capacity))
    last = over_tile(tie(outbox, second, early[1], early[planes - 1]))
    rest = sort(second, slot, got_weight, me, planes, 1, capacity)
    rest = list(lax.optimization_barrier((tuple(rest), tuple(early)))[0])

    from_dest, from_code = from_note(second, planes * slots)
    from_dest = from_dest.reshape(tiles, planes, slots)
    from_place = from_code.reshape(tiles, planes, slots) % places
    start = jnp.arange(tiles, dtype=jnp.int32)[:, None, None] * planes + distance
    from_slot = start * capacity + rank_of(from_dest)
    here = (from_dest == tile)[..., None] & (from_place[..., None] == place_iota)
    routed = jnp.sum(jnp.where(here, from_slot[..., None], 0), axis=(0, 2))

    early = [tie(early[0], *rest)] + early[1:]
    rest = over_phi(rest)
    total = transform_rows(early, 0, basis, None, GROUPS[0][0])
    total = transform_rows(early, 1, basis, total, GROUPS[0][1])
    total = transform_rows(rest, 0, basis, total, GROUPS[1][0])
    return transform_box(last, routed, basis, total, PAIR[0], per_plane, capacity)


def solution(mesh):
    in_specs = (
        P(("tile", "phi"), None, None, None),
        P(("tile", "phi")),
        P(("tile", "phi")),
        P(("tile", "phi")),
        P(("tile", "phi")),
    )
    out_specs = P(None, "tile", "phi", None)
    return jax.shard_map(local, mesh=mesh, in_specs=in_specs, out_specs=out_specs, check_vma=False)
```

time: 778 us -> 312 us (0.40)
  waiting for transfers between devices: 454 us -> 173 us
  local copies, waits for them, and re-layouts: 198 us -> 0.44 us
  Pallas kernels: 0 us -> 85.3 us
  matrix products: 85.2 us -> 0 us
  starting transfers between devices: 21.4 us -> 34.4 us
    all_to_all x4 -> x3, waiting for transfers between devices: 454 us -> 0.01 us  [over_tile(): return lax.all_to_all(box, 'tile', split_axis=0, concat_axis=0, tiled=True)]
    ppermute x0 -> x12, waiting for transfers between devices: none -> 173 us  [over_phi(): moved.append(lax.ppermute(parts[d], 'phi', pairs))]
    reshape x3 -> x2, local copies, waits for them, and re-layouts: 87.6 us -> 0.01 us  [as_note(): jnp.pad(c.reshape(-1), (0, pad)).reshape(each, width)]
    pallas_call x0 -> x10, Pallas kernels: none -> 85.3 us  [the longest x4 48 us: transform(): pl.pallas_call(kernel, in_specs=specs, out_specs=HBM, out_shape=pltpu.HBM...]
    dot_general x1 -> x0, matrix products: 85.2 us -> none  [local(): jnp.einsum('pnagbc,pabk->ngck', shaped, basis_table, preferred_element_ty...]
    scatter x4 -> x0, local copies, waits for them, and re-layouts: 69.9 us -> none  [the longest x1 43.8 us: local(): arranged = jnp.zeros((slot_count,) + blocks.shape[1:], jnp.bfloat16).at[r...]
    ppermute x0 -> x12, starting transfers between devices: none -> 19 us  [over_phi(): moved.append(lax.ppermute(parts[d], 'phi', pairs))]
    transpose x1 -> x0, local copies, waits for them, and re-layouts: 18.9 us -> none  [local(): jnp.transpose(arranged, (4, 2, 0, 1, 3, 5))]
  transfers between devices with their start and end apart: 4 -> 15, of which waited for: 3 -> 8; matrix products, arithmetic and copies ran while one was open for 6% -> 5% of each run, Pallas kernels for 0% -> 19%
where the time goes in v2:
time: 312 us
  waiting for transfers between devices  173 us (55%)
  Pallas kernels  85.3 us (27%)
  starting transfers between devices  34.4 us (11%)
  other arithmetic  17.6 us (6%)
    ppermute x12, waiting for transfers between devices, over_phi(): moved.append(lax.ppermute(parts[d], 'phi', pairs))  173 us
    pallas_call x4, Pallas kernels, transform(): pl.pallas_call(kernel, in_specs=specs, out_specs=HBM, out_shape=pltpu.HBM...  48 us
    ppermute x12, starting transfers between devices, over_phi(): moved.append(lax.ppermute(parts[d], 'phi', pairs))  19 us
    all_to_all x3, starting transfers between devices, over_tile(): return lax.all_to_all(box, 'tile', split_axis=0, concat_axis=0, tiled=True)  15.4 us
    pallas_call x2, Pallas kernels, sort(): pl.pallas_call(functools.partial(sort_kernel, planes, count, capacity), i...  13 us
    pallas_call x2, Pallas kernels, post(): pl.pallas_call(functools.partial(post_kernel, fields, tiles, capacity), i...  11 us
    pallas_call x1, Pallas kernels, mail(): pl.pallas_call(functools.partial(mail_kernel, planes, tiles, capacity), i...  7.45 us
    convert_element_type x1, other arithmetic, rotated_basis(): return table.reshape(SPANS, length, length // SPANS).astype(jnp.bfloat16)  6.74 us
  transfers between devices with their start and end apart: 15, of which 8 were waited for; matrix products, arithmetic and copies ran while one was open for 5% of the time, Pallas kernels for 19%

profile of v2, /device:TPU:10, one launch (start us, length us, event | category | flops | bytes accessed | tf_op | source)
XLA Modules:
  0.0 311.5 jit_solution(17367933384098703743)
XLA Ops:
  0.0 0.9 convert_reduce_fusion.3
  0.9 0.7 fusion.31
  1.6 0.7 fusion.33
  2.4 6.4 %post.3 = bf16[8,2064,256]{2,1,0:T(8,128)(2,1)} custom-call(s32[64]{0:T(128)S(1)} %get-tuple-element.72.slot_ref, bf16[16,256]{1,0:T(8,128)(2,1)S(1)} %fusion.21.note_ref, bf16[64,5,64,256]{3,2,1,0:T(8,128)(2,1)} %x_ref.5), custom_call_target="tpu_custom_call" | custom-call | tf_op jit(solution)/shard_map/post/pallas_call | solution.py:136
  8.8 5.4 %all-to-all-start = ((bf16[8,2064,256]{2,1,0:T(8,128)(2,1)}), bf16[8,2064,256]{2,1,0:T(8,128)(2,1)}, u32[]{:S(2)}, u32[]{:S(2)}) async-start(bf16[8,2064,256]{2,1,0:T(8,128)(2,1)} %post.3), calls=%async_computation | async-start | bytes 16908288 | tf_op jit(solution)/shard_map/all_to_all | solution.py:423
  14.2 5.8 %cut.1 = (bf16[64,64,128]{2,1,0:T(8,128)(2,1)}, bf16[64,64,128]{2,1,0:T(8,128)(2,1)}, bf16[64,64,128]{2,1,0:T(8,128)(2,1)}, bf16[64,64,128]{2,1,0:T(8,128)(2,1)}) custom-call(s32[1]{0:T(128)} %bitcast.me_ref, f32[64]{0:T(128)S(1)} %convert_divide_fusion.1.weight_ref, bf16[64,5,64,256]{3,2,1,0:T(8,128)(2,1)} %x_ref.5), custom_call_target="tpu_custom_call" | custom-call | tf_op jit(solution)/shard_map/cut/pallas_call | solution.py:92
  20.0 3.0 collective-permute-start.1
  23.1 2.5 collective-permute-start
  25.6 1.9 collective-permute-start.4
  27.6 0.1 add.210
  27.7 1.1 select_multiply_fusion
  28.8 2.0 fusion.10
  30.9 1.1 collective-permute-start.5
  31.9 6.7 %add_convert_fusion = bf16[4,32,64,512]{3,2,1,0:T(8,128)(2,1)} fusion(f32[4,64,512]{2,1,0:T(8,128)S(1)} %bitcast.20, f32[4,32,512]{2,1,0:T(8,128)S(1)} %bitcast.22, f32[4,64,512]{2,1,0:T(8,128)S(1)} %bitcast.21, f32[4,32,512]{2,1,0:T(8,128)S(1)} %bitcast.23), kind=kLoop, calls=%fused_computation | loop fusion | flops 16777216 | bytes 9961472 | tf_op jit(solution)/shard_map/convert_element_type | solution.py:57
  38.7 0.1 stack.22
  38.8 4.6 %post.2 = bf16[8,1040,256]{2,1,0:T(8,128)(2,1)} custom-call(s32[64]{0:T(128)S(1)} %get-tuple-element.72.slot_ref, bf16[16,256]{1,0:T(8,128)(2,1)S(1)} %fusion.20.note_ref, bf16[64,5,64,256]{3,2,1,0:T(8,128)(2,1)} %x_ref.5), custom_call_target="tpu_custom_call" | custom-call | tf_op jit(solution)/shard_map/post/pallas_call | solution.py:136
  43.4 8.5 %collective-permute-done.3.rest_1_ = bf16[64,64,128]{2,1,0:T(8,128)(2,1)S(1)} collective-permute-done((bf16[64,64,128]{2,1,0:T(8,128)(2,1)}, bf16[64,64,128]{2,1,0:T(8,128)(2,1)S(1)}, u32[]{:S(2)}, u32[]{:S(2)}) %collective-permute-start.3) | collective-permute-done | bytes 1048608 | tf_op jit(solution)/shard_map/ppermute | solution.py:419
  51.9 63.6 %collective-permute-done.4.rest_2_ = bf16[64,64,128]{2,1,0:T(8,128)(2,1)S(1)} collective-permute-done((bf16[64,64,128]{2,1,0:T(8,128)(2,1)}, bf16[64,64,128]{2,1,0:T(8,128)(2,1)S(1)}, u32[]{:S(2)}, u32[]{:S(2)}) %collective-permute-start.4) | collective-permute-done | bytes 1048608 | tf_op jit(solution)/shard_map/ppermute | solution.py:419
  115.5 2.0 collective-permute-done.5.rest_3_
  117.5 4.8 %all-to-all-start.1 = ((bf16[8,1040,256]{2,1,0:T(8,128)(2,1)}), bf16[8,1040,256]{2,1,0:T(8,128)(2,1)}, u32[]{:S(2)}, u32[]{:S(2)}) async-start(bf16[8,1040,256]{2,1,0:T(8,128)(2,1)} %post.2), calls=%async_computation.1 | async-start | bytes 8519680 | tf_op jit(solution)/shard_map/all_to_all | solution.py:423
  122.3 0.9 convert_convert_fusion
  123.3 0.3 convert_reduce_fusion.1
  123.7 0.3 select_reduce_fusion.1
  124.1 7.8 %sort.2 = (bf16[2,512,512]{2,1,0:T(8,128)(2,1)}, bf16[2,512,512]{2,1,0:T(8,128)(2,1)}, bf16[2,512,512]{2,1,0:T(8,128)(2,1)}, bf16[2,512,512]{2,1,0:T(8,128)(2,1)}) custom-call(s32[1]{0:T(128)} %bitcast.me_ref, s32[64]{0:T(128)S(1)} %get-tuple-element.56.slot_ref, f32[64]{0:T(128)S(1)} %convert_divide_fusion.weight_ref, bf16[8,2064,256]{2,1,0:T(8,128)(2,1)} %all-to-all-done.x_ref), custom_call_target="tpu_custom_call" | custom-call | tf_op jit(solution)/shard_map/sort/pallas_call | solution.py:198
  131.9 2.0 collective-permute-start.7
  133.9 0.2 convert_reduce_fusion.2
  134.2 7.5 %mail.1 = bf16[8,4096,128]{2,1,0:T(8,128)(2,1)} custom-call(s32[4,64]{1,0:T(4,128)S(1)} %multiply_add_fusion.1.slot_ref, bf16[64,64,128]{2,1,0:T(8,128)(2,1)} %get-tuple-element.29.rest_0_, bf16[64,64,128]{2,1,0:T(8,128)(2,1)} %copy-done.3, bf16[64,64,128]{2,1,0:T(8,128)(2,1)} %copy-done.4, bf16[64,64,128]{2,1,0:T(8,128)(2,1)} %copy-done.5), custom_call_target="tpu_custom_call" | custom-call | tf_op jit(solution)/shard_map/mail/pallas_call | solution.py:240
  141.6 16.5 %collective-permute-done.6.refs_1_ = bf16[2,512,512]{2,1,0:T(8,128)(2,1)S(1)} collective-permute-done((bf16[2,512,512]{2,1,0:T(8,128)(2,1)}, bf16[2,512,512]{2,1,0:T(8,128)(2,1)S(1)}, u32[]{:S(2)}, u32[]{:S(2)}) %collective-permute-start.6) | collective-permute-done | bytes 1048608 | tf_op jit(solution)/shard_map/ppermute | solution.py:419
  158.1 21.2 %collective-permute-done.7.refs_3_ = bf16[2,512,512]{2,1,0:T(8,128)(2,1)S(1)} collective-permute-done((bf16[2,512,512]{2,1,0:T(8,128)(2,1)}, bf16[2,512,512]{2,1,0:T(8,128)(2,1)S(1)}, u32[]{:S(2)}, u32[]{:S(2)}) %collective-permute-start.7) | collective-permute-done | bytes 1048608 | tf_op jit(solution)/shard_map/ppermute | solution.py:419
  179.4 5.2 %all-to-all-start.2 = ((bf16[8,4096,128]{2,1,0:T(8,128)(2,1)}), bf16[8,4096,128]{2,1,0:T(8,128)(2,1)}, u32[]{:S(2)}, u32[]{:S(2)}) async-start(bf16[8,4096,128]{2,1,0:T(8,128)(2,1)} %mail.1), calls=%async_computation.2 | async-start | bytes 16777216 | tf_op jit(solution)/shard_map/all_to_all | solution.py:423
  184.6 2.8 collective-permute-start.8
  187.4 0.1 add_multiply_fusion
  187.4 0.9 convert_convert_fusion.1
  188.3 0.1 reshape_reshape.6
  188.4 5.3 %sort.3 = (bf16[1,512,512]{2,1,0:T(8,128)(2,1)}, bf16[1,512,512]{2,1,0:T(8,128)(2,1)}, bf16[1,512,512]{2,1,0:T(8,128)(2,1)}, bf16[1,512,512]{2,1,0:T(8,128)(2,1)}) custom-call(s32[1]{0:T(128)} %bitcast.me_ref, s32[64]{0:T(128)S(1)} %get-tuple-element.56.slot_ref, f32[64]{0:T(128)S(1)} %convert_divide_fusion.weight_ref, ...), custom_call_target="tpu_custom_call" | custom-call | tf_op jit(solution)/shard_map/sort/pallas_call | solution.py:198
  193.7 37.9 %collective-permute-done.8.refs_2_ = bf16[2,512,512]{2,1,0:T(8,128)(2,1)S(1)} collective-permute-done((bf16[2,512,512]{2,1,0:T(8,128)(2,1)}, bf16[2,512,512]{2,1,0:T(8,128)(2,1)S(1)}, u32[]{:S(2)}, u32[]{:S(2)}) %collective-permute-start.8) | collective-permute-done | bytes 1048608 | tf_op jit(solution)/shard_map/ppermute | solution.py:419
  231.6 1.4 collective-permute-start.9
  233.0 4.2 %collective-permute-start.10 = (bf16[1,512,512]{2,1,0:T(8,128)(2,1)}, bf16[1,512,512]{2,1,0:T(8,128)(2,1)}, u32[]{:S(2)}, u32[]{:S(2)}) collective-permute-start(bf16[1,512,512]{2,1,0:T(8,128)(2,1)} %get-tuple-element.50), channel_id=1, source_target_pairs={{0,2},{1,3},{2,0},{3,1},{4,6},{5,7},{6,4},{7,5},{8,10},{9,11},{10,... | collective-permute-start | bytes 1572872 | tf_op jit(solution)/shard_map/ppermute | solution.py:419
  237.2 0.1 reshape_reshape.7
  237.3 9.4 %rows.3.refs_5_ = f32[5,8,64,2048]{3,2,1,0:T(8,128)} custom-call(bf16[2,512,512]{2,1,0:T(8,128)(2,1)} %get-tuple-element.52.refs_0_, bf16[2,512,512]{2,1,0:T(8,128)(2,1)} %copy-done, bf16[2,512,512]{2,1,0:T(8,128)(2,1)} %copy-done.2, bf16[2,512,512]{2,1,0:T(8,128)(2,1)} %copy-done.1, bf16[4,2048,512]{2,1,0:T(8,128)(2,1)} %bitcast.16), custom_call_target="tpu_custom_call" | custom-call | tf_op jit(solution)/shard_map/rows/pallas_call | solution.py:341
  246.7 9.4 %rows.4.refs_5_ = f32[5,8,64,2048]{3,2,1,0:T(8,128)} custom-call(bf16[2,512,512]{2,1,0:T(8,128)(2,1)} %get-tuple-element.52.refs_0_, bf16[2,512,512]{2,1,0:T(8,128)(2,1)} %copy-done, bf16[2,512,512]{2,1,0:T(8,128)(2,1)} %copy-done.2, bf16[2,512,512]{2,1,0:T(8,128)(2,1)} %copy-done.1, bf16[4,2048,512]{2,1,0:T(8,128)(2,1)} %bitcast.17, ...), custom_call_target="tpu_custom_call", output_to_operand_aliasing={{}: (5, {})} | custom-call | tf_op jit(solution)/shard_map/rows/pallas_call | solution.py:341
  256.2 1.0 convert_reduce_fusion
  257.1 0.1 add_select_fusion.2
  257.2 1.3 select_reduce_fusion.refs_0_
  258.5 19.7 %collective-permute-done.10.refs_2_ = bf16[1,512,512]{2,1,0:T(8,128)(2,1)} collective-permute-done((bf16[1,512,512]{2,1,0:T(8,128)(2,1)}, bf16[1,512,512]{2,1,0:T(8,128)(2,1)}, u32[]{:S(2)}, u32[]{:S(2)}) %collective-permute-start.10) | collective-permute-done | bytes 524320 | tf_op jit(solution)/shard_map/ppermute | solution.py:419
  278.3 3.9 %collective-permute-done.11.refs_3_ = bf16[1,512,512]{2,1,0:T(8,128)(2,1)} collective-permute-done((bf16[1,512,512]{2,1,0:T(8,128)(2,1)}, bf16[1,512,512]{2,1,0:T(8,128)(2,1)}, u32[]{:S(2)}, u32[]{:S(2)}) %collective-permute-start.11) | collective-permute-done | bytes 524320 | tf_op jit(solution)/shard_map/ppermute | solution.py:419
  282.2 9.4 %rows.5.refs_3_ = f32[5,8,64,2048]{3,2,1,0:T(8,128)} custom-call(bf16[1,512,512]{2,1,0:T(8,128)(2,1)} %get-tuple-element.48.refs_0_, bf16[1,512,512]{2,1,0:T(8,128)(2,1)} %collective-permute-done.9.refs_1_, bf16[1,512,512]{2,1,0:T(8,128)(2,1)} %collective-permute-done.10.refs_2_, ...), custom_call_target="tpu_custom_call", output_to_operand_aliasing={{}: (5, {})} | custom-call | tf_op jit(solution)/shard_map/rows/pallas_call | solution.py:341
  291.6 19.8 %box.1 = f32[5,8,64,2048]{3,2,1,0:T(8,128)} custom-call(s32[4,64]{1,0:T(4,128)S(1)} %select_reduce_fusion.refs_0_, bf16[8,4096,128]{2,1,0:T(8,128)(2,1)} %all-to-all-done.2.refs_1_, bf16[4,2048,512]{2,1,0:T(8,128)(2,1)} %bitcast.19, f32[5,8,64,2048]{3,2,1,0:T(8,128)} %rows.5.refs_3_), custom_call_target="tpu_custom_call", output_to_operand_aliasing={{}: (3, {})} | custom-call | tf_op jit(solution)/shard_map/box/pallas_call | solution.py:341
  (54 shorter events, 0.5 us)
Async XLA Ops:
  2.4 11.8 %copy-start.6 = (s32[64]{0:T(128)S(1)}, s32[64]{0:T(128)}, u32[]{:S(2)}) copy-start(s32[64]{0:T(128)} %param.6) | copy-start | bytes 772
  8.8 108.7 %all-to-all-start = ((bf16[8,2064,256]{2,1,0:T(8,128)(2,1)}), bf16[8,2064,256]{2,1,0:T(8,128)(2,1)}, u32[]{:S(2)}, u32[]{:S(2)}) async-start(bf16[8,2064,256]{2,1,0:T(8,128)(2,1)} %post.3), calls=%async_computation | async-start | bytes 16908288 | tf_op jit(solution)/shard_map/all_to_all | solution.py:423
  20.0 10.8 %collective-permute-start.2 = (s32[64]{0:T(128)S(1)}, s32[64]{0:T(128)S(1)}, u32[]{:S(2)}, u32[]{:S(2)}) collective-permute-start(s32[64]{0:T(128)S(1)} %get-tuple-element.30), channel_id=1, source_target_pairs={{0,3},{1,0},{2,1},{3,2},{4,7},{5,4},{6,5},{7,6},{8,11},{9,8},{10,9... | collective-permute-start | bytes 776 | tf_op jit(solution)/shard_map/ppermute | solution.py:419
  20.0 18.6 %collective-permute-start.1 = (s32[64]{0:T(128)S(1)}, s32[64]{0:T(128)S(1)}, u32[]{:S(2)}, u32[]{:S(2)}) collective-permute-start(s32[64]{0:T(128)S(1)} %get-tuple-element.30), channel_id=1, source_target_pairs={{0,2},{1,3},{2,0},{3,1},{4,6},{5,7},{6,4},{7,5},{8,10},{9,11},{10,... | collective-permute-start | bytes 776 | tf_op jit(solution)/shard_map/ppermute | solution.py:419
  23.1 15.6 %collective-permute-start = (s32[64]{0:T(128)S(1)}, s32[64]{0:T(128)S(1)}, u32[]{:S(2)}, u32[]{:S(2)}) collective-permute-start(s32[64]{0:T(128)S(1)} %get-tuple-element.30), channel_id=1, source_target_pairs={{0,1},{1,2},{2,3},{3,0},{4,5},{5,6},{6,7},{7,4},{8,9},{9,10},{10,1... | collective-permute-start | bytes 776 | tf_op jit(solution)/shard_map/ppermute | solution.py:419
  25.6 26.3 %collective-permute-start.3 = (bf16[64,64,128]{2,1,0:T(8,128)(2,1)}, bf16[64,64,128]{2,1,0:T(8,128)(2,1)S(1)}, u32[]{:S(2)}, u32[]{:S(2)}) collective-permute-start(bf16[64,64,128]{2,1,0:T(8,128)(2,1)} %get-tuple-element.35), channel_id=1, source_target_pairs={{0,1},{1,2},{2,3},{3,0},{4,5},{5,6},{6,7},{7,4},{8,9},{9,10},{10,1... | collective-permute-start | bytes 3145736 | tf_op jit(solution)/shard_map/ppermute | solution.py:419
  25.6 89.9 %collective-permute-start.4 = (bf16[64,64,128]{2,1,0:T(8,128)(2,1)}, bf16[64,64,128]{2,1,0:T(8,128)(2,1)S(1)}, u32[]{:S(2)}, u32[]{:S(2)}) collective-permute-start(bf16[64,64,128]{2,1,0:T(8,128)(2,1)} %get-tuple-element.36), channel_id=1, source_target_pairs={{0,2},{1,3},{2,0},{3,1},{4,6},{5,7},{6,4},{7,5},{8,10},{9,11},{10,... | collective-permute-start | bytes 3145736 | tf_op jit(solution)/shard_map/ppermute | solution.py:419
  30.9 86.6 %collective-permute-start.5 = (bf16[64,64,128]{2,1,0:T(8,128)(2,1)}, bf16[64,64,128]{2,1,0:T(8,128)(2,1)S(1)}, u32[]{:S(2)}, u32[]{:S(2)}) collective-permute-start(bf16[64,64,128]{2,1,0:T(8,128)(2,1)} %get-tuple-element.37), channel_id=1, source_target_pairs={{0,3},{1,0},{2,1},{3,2},{4,7},{5,4},{6,5},{7,6},{8,11},{9,8},{10,9... | collective-permute-start | bytes 3145736 | tf_op jit(solution)/shard_map/ppermute | solution.py:419
  51.9 82.3 %copy-start.3 = (bf16[64,64,128]{2,1,0:T(8,128)(2,1)}, bf16[64,64,128]{2,1,0:T(8,128)(2,1)S(1)}, u32[]{:S(2)}) copy-start(bf16[64,64,128]{2,1,0:T(8,128)(2,1)S(1)} %collective-permute-done.3.rest_1_) | copy-start | bytes 3145732
  115.5 8.5 %copy-start.4 = (bf16[64,64,128]{2,1,0:T(8,128)(2,1)}, bf16[64,64,128]{2,1,0:T(8,128)(2,1)S(1)}, u32[]{:S(2)}) copy-start(bf16[64,64,128]{2,1,0:T(8,128)(2,1)S(1)} %collective-permute-done.4.rest_2_) | copy-start | bytes 3145732
  117.5 14.3 %copy-start.5 = (bf16[64,64,128]{2,1,0:T(8,128)(2,1)}, bf16[64,64,128]{2,1,0:T(8,128)(2,1)S(1)}, u32[]{:S(2)}) copy-start(bf16[64,64,128]{2,1,0:T(8,128)(2,1)S(1)} %collective-permute-done.5.rest_3_) | copy-start | bytes 3145732
  117.5 61.9 %all-to-all-start.1 = ((bf16[8,1040,256]{2,1,0:T(8,128)(2,1)}), bf16[8,1040,256]{2,1,0:T(8,128)(2,1)}, u32[]{:S(2)}, u32[]{:S(2)}) async-start(bf16[8,1040,256]{2,1,0:T(8,128)(2,1)} %post.2), calls=%async_computation.1 | async-start | bytes 8519680 | tf_op jit(solution)/shard_map/all_to_all | solution.py:423
  131.8 26.3 %collective-permute-start.6 = (bf16[2,512,512]{2,1,0:T(8,128)(2,1)}, bf16[2,512,512]{2,1,0:T(8,128)(2,1)S(1)}, u32[]{:S(2)}, u32[]{:S(2)}) collective-permute-start(bf16[2,512,512]{2,1,0:T(8,128)(2,1)} %get-tuple-element.39), channel_id=1, source_target_pairs={{0,1},{1,2},{2,3},{3,0},{4,5},{5,6},{6,7},{7,4},{8,9},{9,10},{10,1... | collective-permute-start | bytes 3145736 | tf_op jit(solution)/shard_map/ppermute | solution.py:419
  131.9 47.5 %collective-permute-start.7 = (bf16[2,512,512]{2,1,0:T(8,128)(2,1)}, bf16[2,512,512]{2,1,0:T(8,128)(2,1)S(1)}, u32[]{:S(2)}, u32[]{:S(2)}) collective-permute-start(bf16[2,512,512]{2,1,0:T(8,128)(2,1)} %get-tuple-element.40), channel_id=1, source_target_pairs={{0,3},{1,0},{2,1},{3,2},{4,7},{5,4},{6,5},{7,6},{8,11},{9,8},{10,9... | collective-permute-start | bytes 3145736 | tf_op jit(solution)/shard_map/ppermute | solution.py:419
  158.1 79.2 %copy-start = (bf16[2,512,512]{2,1,0:T(8,128)(2,1)}, bf16[2,512,512]{2,1,0:T(8,128)(2,1)S(1)}, u32[]{:S(2)}) copy-start(bf16[2,512,512]{2,1,0:T(8,128)(2,1)S(1)} %collective-permute-done.6.refs_1_) | copy-start | bytes 3145732
  179.4 57.9 %copy-start.1 = (bf16[2,512,512]{2,1,0:T(8,128)(2,1)}, bf16[2,512,512]{2,1,0:T(8,128)(2,1)S(1)}, u32[]{:S(2)}) copy-start(bf16[2,512,512]{2,1,0:T(8,128)(2,1)S(1)} %collective-permute-done.7.refs_3_) | copy-start | bytes 3145732
  179.4 112.2 %all-to-all-start.2 = ((bf16[8,4096,128]{2,1,0:T(8,128)(2,1)}), bf16[8,4096,128]{2,1,0:T(8,128)(2,1)}, u32[]{:S(2)}, u32[]{:S(2)}) async-start(bf16[8,4096,128]{2,1,0:T(8,128)(2,1)} %mail.1), calls=%async_computation.2 | async-start | bytes 16777216 | tf_op jit(solution)/shard_map/all_to_all | solution.py:423
  184.6 47.0 %collective-permute-start.8 = (bf16[2,512,512]{2,1,0:T(8,128)(2,1)}, bf16[2,512,512]{2,1,0:T(8,128)(2,1)S(1)}, u32[]{:S(2)}, u32[]{:S(2)}) collective-permute-start(bf16[2,512,512]{2,1,0:T(8,128)(2,1)} %get-tuple-element.47), channel_id=1, source_target_pairs={{0,2},{1,3},{2,0},{3,1},{4,6},{5,7},{6,4},{7,5},{8,10},{9,11},{10,... | collective-permute-start | bytes 3145736 | tf_op jit(solution)/shard_map/ppermute | solution.py:419
  231.6 5.7 %copy-start.2 = (bf16[2,512,512]{2,1,0:T(8,128)(2,1)}, bf16[2,512,512]{2,1,0:T(8,128)(2,1)S(1)}, u32[]{:S(2)}) copy-start(bf16[2,512,512]{2,1,0:T(8,128)(2,1)S(1)} %collective-permute-done.8.refs_2_) | copy-start | bytes 3145732
  231.6 26.9 %collective-permute-start.9 = (bf16[1,512,512]{2,1,0:T(8,128)(2,1)}, bf16[1,512,512]{2,1,0:T(8,128)(2,1)}, u32[]{:S(2)}, u32[]{:S(2)}) collective-permute-start(bf16[1,512,512]{2,1,0:T(8,128)(2,1)} %get-tuple-element.49), channel_id=1, source_target_pairs={{0,1},{1,2},{2,3},{3,0},{4,5},{5,6},{6,7},{7,4},{8,9},{9,10},{10,1... | collective-permute-start | bytes 1572872 | tf_op jit(solution)/shard_map/ppermute | solution.py:419
  233.0 45.2 %collective-permute-start.10 = (bf16[1,512,512]{2,1,0:T(8,128)(2,1)}, bf16[1,512,512]{2,1,0:T(8,128)(2,1)}, u32[]{:S(2)}, u32[]{:S(2)}) collective-permute-start(bf16[1,512,512]{2,1,0:T(8,128)(2,1)} %get-tuple-element.50), channel_id=1, source_target_pairs={{0,2},{1,3},{2,0},{3,1},{4,6},{5,7},{6,4},{7,5},{8,10},{9,11},{10,... | collective-permute-start | bytes 1572872 | tf_op jit(solution)/shard_map/ppermute | solution.py:419
  237.2 45.0 %collective-permute-start.11 = (bf16[1,512,512]{2,1,0:T(8,128)(2,1)}, bf16[1,512,512]{2,1,0:T(8,128)(2,1)}, u32[]{:S(2)}, u32[]{:S(2)}) collective-permute-start(bf16[1,512,512]{2,1,0:T(8,128)(2,1)} %get-tuple-element.51), channel_id=1, source_target_pairs={{0,3},{1,0},{2,1},{3,2},{4,7},{5,4},{6,5},{7,6},{8,11},{9,8},{10,9... | collective-permute-start | bytes 1572872 | tf_op jit(solution)/shard_map/ppermute | solution.py:419

commit v3 on v2

v3 whole, which is shorter than its diff:
```python
import functools
import math

import jax
import jax.numpy as jnp
from jax import lax
from jax.experimental import pallas as pl
from jax.experimental.pallas import tpu as pltpu
from jax.sharding import PartitionSpec as P

FIELDS = 5
NPHI = 2048
BPHI = 64
COLS = 256
CG_DEV = 8
LANES = 128
NOTE = 16
PAIR = (0, 1)
GROUPS = ((2, 3), (4,))
VMEM_BYTES = 32 * 1024 * 1024
SPANS = 4
LIGHT = pl.CostEstimate(flops=0, bytes_accessed=0, transcendentals=0)
SLOW = pl.CostEstimate(flops=20_000_000_000, bytes_accessed=0, transcendentals=0)
SLOWER = pl.CostEstimate(flops=30_000_000_000, bytes_accessed=0, transcendentals=0)

ANY = pl.BlockSpec(memory_space=pl.ANY)
HBM = pl.BlockSpec(memory_space=pltpu.HBM)
SMEM = pl.BlockSpec(memory_space=pltpu.SMEM)
VMEM = pl.BlockSpec(memory_space=pltpu.VMEM)


def rotated_basis(length, back):
    planes = back.shape[0]
    per = length // planes
    column = jnp.arange(length, dtype=jnp.int32)
    half = length // 2
    mode = jnp.where(column <= half, column, column - half)
    coarse = (back[:, None] * per + jnp.arange(0, per, BPHI, dtype=jnp.int32)[None, :]).reshape(-1)
    fine = jnp.arange(BPHI, dtype=jnp.int32)

    def angle(row):
        phase = row[:, None] * mode[None, :] % length
        return phase.astype(jnp.float32) * jnp.float32(2.0 * math.pi / length)

    even = (column <= half)[None, :]
    scale = jnp.float32(1.0 / math.sqrt(length))
    far, near = angle(coarse), angle(fine)
    by_cos = jnp.where(even, jnp.cos(far), jnp.sin(far)) * scale
    by_sin = jnp.where(even, -jnp.sin(far), jnp.cos(far)) * scale
    near_cos, near_sin = jnp.cos(near), jnp.sin(near)

    def spans(x):
        return x.reshape(x.shape[0], SPANS, length // SPANS).transpose(1, 0, 2)

    by_cos, by_sin = spans(by_cos)[:, :, None], spans(by_sin)[:, :, None]
    near_cos, near_sin = spans(near_cos)[:, None], spans(near_sin)[:, None]
    by_cos, by_sin, near_cos, near_sin = lax.optimization_barrier((by_cos, by_sin, near_cos, near_sin))
    table = by_cos * near_cos + by_sin * near_sin
    return table.reshape(SPANS, length, length // SPANS).astype(jnp.bfloat16)


def in_hbm(*arrays):
    return [pltpu.with_memory_space_constraint(a, pltpu.HBM) for a in arrays]


def params():
    return pltpu.CompilerParams(vmem_limit_bytes=VMEM_BYTES)


def scaled(block, weight):
    return block * jnp.full((1, 1), weight, jnp.float32).astype(jnp.bfloat16)


def cut_kernel(planes, me_ref, weight_ref, note_ref, x_ref, *refs):
    outs, (buf, made, sems, out_sems) = refs[:planes], refs[planes:]
    slots = buf.shape[0]
    sliver = COLS // planes
    parts = sems.shape[0]
    some = slots // parts
    me = me_ref[0]
    for k in range(parts):
        span = pl.ds(k * some, some)
        source = x_ref.at[span, pl.ds(PAIR[0], 2)]
        pltpu.make_async_copy(source, buf.at[span], sems.at[k]).start()
    for d in range(planes):
        made[d, pl.ds(slots * sliver, NOTE)] = note_ref[...]

    def leave(k, d):
        rows = some * sliver + (NOTE if k == parts - 1 else 0)
        span = pl.ds(k * some * sliver, rows)
        return pltpu.make_async_copy(made.at[d, span], outs[d].at[span], out_sems.at[k, d])

    for k in range(parts):
        span = pl.ds(k * some, some)
        pltpu.make_async_copy(buf.at[span], buf.at[span], sems.at[k]).wait()

        def body(i, carry):
            x = scaled(buf[i].reshape(LANES, COLS), weight_ref[i]).T
            to = pl.ds(pl.multiple_of(i * sliver, sliver), sliver)
            for p in range(planes):
                made[(p - me + planes) % planes, to] = x[p * sliver : (p + 1) * sliver]
            return carry

        lax.fori_loop(k * some, (k + 1) * some, body, 0, unroll=4)
        for d in range(planes):
            leave(k, d).start()
    for k in range(parts):
        for d in range(planes):
            leave(k, d).wait()


def cut(blocks, weight, note, me, planes):
    slots = blocks.shape[0]
    parts = 4
    rows = slots * (COLS // planes) + NOTE
    return pl.pallas_call(
        functools.partial(cut_kernel, planes),
        in_specs=[SMEM, SMEM, VMEM, ANY],
        out_specs=[HBM] * planes,
        out_shape=[pltpu.HBM((rows, LANES), jnp.bfloat16)] * planes,
        scratch_shapes=[
            pltpu.VMEM((slots, 2, BPHI, COLS), jnp.bfloat16),
            pltpu.VMEM((planes, rows, LANES), jnp.bfloat16),
            pltpu.SemaphoreType.DMA((parts,)),
            pltpu.SemaphoreType.DMA((parts, planes)),
        ],
        compiler_params=params(),
        cost_estimate=LIGHT,
        name="cut",
    )(me, weight, note, *in_hbm(blocks))


def post_kernel(
    fields, tiles, capacity, dest_ref, note_ref, x_ref, out_ref, box_ref, buf, filled, sems, out_sems
):
    slots = dest_ref.shape[0]
    count = len(fields)
    rows = count * BPHI
    parts = sems.shape[0]
    some = slots // parts
    for k in range(parts):
        span = pl.ds(k * some, some)
        source = x_ref.at[span, pl.ds(fields[0], count)]
        pltpu.make_async_copy(source, buf.at[span], sems.at[k]).start()
    for t in range(tiles):
        filled[t] = 0
        box_ref[t, pl.ds(capacity * rows, NOTE)] = note_ref[...]
    for k in range(parts):
        span = pl.ds(k * some, some)
        pltpu.make_async_copy(buf.at[span], buf.at[span], sems.at[k]).wait()

        def body(i, carry):
            tile = dest_ref[i]
            slot = filled[tile]
            filled[tile] = slot + 1
            row = pl.multiple_of(slot * rows, rows)
            box_ref[tile, pl.ds(row, rows)] = buf[i].reshape(rows, COLS)
            return carry

        lax.fori_loop(k * some, (k + 1) * some, body, 0)
    for t in range(tiles):
        pltpu.make_async_copy(box_ref.at[t], out_ref.at[t], out_sems.at[t]).start()
    for t in range(tiles):
        pltpu.make_async_copy(box_ref.at[t], out_ref.at[t], out_sems.at[t]).wait()


def post(blocks, dest, note, fields, tiles, capacity):
    slots = blocks.shape[0]
    rows = capacity * len(fields) * BPHI + NOTE
    return pl.pallas_call(
        functools.partial(post_kernel, fields, tiles, capacity),
        in_specs=[SMEM, VMEM, ANY],
        out_specs=HBM,
        out_shape=pltpu.HBM((tiles, rows, COLS), jnp.bfloat16),
        scratch_shapes=[
            pltpu.VMEM((tiles, rows, COLS), jnp.bfloat16),
            pltpu.VMEM((slots, len(fields), BPHI, COLS), jnp.bfloat16),
            pltpu.SMEM((tiles,), jnp.int32),
            pltpu.SemaphoreType.DMA((4,)),
            pltpu.SemaphoreType.DMA((tiles,)),
        ],
        compiler_params=params(),
        cost_estimate=LIGHT,
        name="post",
    )(dest, note, *in_hbm(blocks))


def sort_kernel(planes, count, capacity, me_ref, slot_ref, weight_ref, note_ref, x_ref, *rest):
    outs, (buf, made, sems, out_sems) = rest[:-4], rest[-4:]
    tiles = buf.shape[0]
    per_plane = slot_ref.shape[0] // CG_DEV
    sliver = COLS // planes
    rows = count * BPHI
    side = CG_DEV * sliver
    me = me_ref[0]
    for d in range(planes):
        made[d, pl.ds(count * side, NOTE)] = note_ref[...]
    for t in range(tiles):
        pltpu.make_async_copy(x_ref.at[t], buf.at[t], sems.at[t]).start()
    for t in range(tiles):
        pltpu.make_async_copy(buf.at[t], buf.at[t], sems.at[t]).wait()

    def leave(f, d):
        span = pl.ds(f * side, side + (NOTE if f == count - 1 else 0))
        return pltpu.make_async_copy(made.at[d, span], outs[d].at[span], out_sems.at[f, d])

    def block(place, f):
        at = slot_ref[place]
        row = pl.multiple_of((at % capacity) * rows + f * BPHI, BPHI)
        return scaled(buf[at // capacity, pl.ds(row, BPHI)], weight_ref[place])

    for f in range(count):
        for j in range(per_plane // 2):

            def body(g, carry):
                even = block(2 * j * CG_DEV + g, f)
                odd = block((2 * j + 1) * CG_DEV + g, f)
                x = jnp.concatenate([even, odd], axis=0).T
                to = pl.ds(pl.multiple_of(f * side + g * sliver, sliver), sliver)
                for p in range(planes):
                    distance = (p - me + planes) % planes
                    made[distance, to, pl.ds(j * LANES, LANES)] = x[p * sliver : (p + 1) * sliver]
                return carry

            lax.fori_loop(0, CG_DEV, body, 0, unroll=4)
        for d in range(planes):
            leave(f, d).start()
    for f in range(count):
        for d in range(planes):
            leave(f, d).wait()


def sort(arrived, slot, weight, note, me, planes, count, capacity):
    cells = slot.shape[0] // CG_DEV * BPHI
    rows = count * CG_DEV * (COLS // planes) + NOTE
    return pl.pallas_call(
        functools.partial(sort_kernel, planes, count, capacity),
        in_specs=[SMEM, SMEM, SMEM, VMEM, ANY],
        out_specs=[HBM] * planes,
        out_shape=[pltpu.HBM((rows, cells), jnp.bfloat16)] * planes,
        scratch_shapes=[
            pltpu.VMEM(arrived.shape, jnp.bfloat16),
            pltpu.VMEM((planes, rows, cells), jnp.bfloat16),
            pltpu.SemaphoreType.DMA((arrived.shape[0],)),
            pltpu.SemaphoreType.DMA((count, planes)),
        ],
        compiler_params=params(),
        cost_estimate=LIGHT,
        name="sort",
    )(me, slot, weight, note, *in_hbm(arrived))


def mail_kernel(planes, tiles, capacity, slot_ref, *refs):
    ins, (out_ref, box_ref, buf, sems, out_sems) = refs[:planes], refs[planes:]
    slots = slot_ref.shape[1]
    sliver = box_ref.shape[1] // (planes * capacity)
    for d in range(planes):
        source = ins[d].at[pl.ds(0, slots * sliver)]
        pltpu.make_async_copy(source, buf.at[d], sems.at[d]).start()
    for d in range(planes):
        pltpu.make_async_copy(buf.at[d], buf.at[d], sems.at[d]).wait()

        def body(i, carry):
            to = slot_ref[d, i]
            row = pl.multiple_of((to % (planes * capacity)) * sliver, sliver)
            source = pl.ds(pl.multiple_of(i * sliver, sliver), sliver)
            box_ref[to // (planes * capacity), pl.ds(row, sliver)] = buf[d, source]
            return carry

        lax.fori_loop(0, slots, body, 0, unroll=4)
    for t in range(tiles):
        pltpu.make_async_copy(box_ref.at[t], out_ref.at[t], out_sems.at[t]).start()
    for t in range(tiles):
        pltpu.make_async_copy(box_ref.at[t], out_ref.at[t], out_sems.at[t]).wait()


def mail(parts, slot, tiles, capacity):
    planes, slots = slot.shape
    sliver = COLS // planes
    rows = planes * capacity * sliver
    return pl.pallas_call(
        functools.partial(mail_kernel, planes, tiles, capacity),
        in_specs=[SMEM] + [ANY] * planes,
        out_specs=HBM,
        out_shape=pltpu.HBM((tiles, rows, LANES), jnp.bfloat16),
        scratch_shapes=[
            pltpu.VMEM((tiles, rows, LANES), jnp.bfloat16),
            pltpu.VMEM((planes, slots * sliver, LANES), jnp.bfloat16),
            pltpu.SemaphoreType.DMA((planes,)),
            pltpu.SemaphoreType.DMA((tiles,)),
        ],
        compiler_params=params(),
        cost_estimate=SLOW,
        name="mail",
    )(slot, *in_hbm(*parts))


def load_basis(basis_hbm, basis, sems, spans):
    for j in spans:
        pltpu.make_async_copy(basis_hbm.at[j], basis.at[j], sems.at[j]).start()


def multiply(order, basis, out_hbm, rows, acc, basis_sems, sems, beside=None):
    wide = acc.shape[-1]
    copies = []
    for f, field in enumerate(order):
        for j in range(SPANS):
            n = len(copies)
            if f == 0:
                pltpu.make_async_copy(basis.at[j], basis.at[j], basis_sems.at[j]).wait()
            if beside is not None:
                beside(n)
            if n >= 2:
                copies[n - 2].wait()
            acc[n % 2] = jnp.dot(
                rows[f][...], basis[j], preferred_element_type=jnp.float32
            ).reshape(acc.shape[1:])
            copy = pltpu.make_async_copy(
                acc.at[n % 2], out_hbm.at[field, :, :, pl.ds(j * wide, wide)], sems.at[n % 2]
            )
            copy.start()
            copies.append(copy)
    for copy in copies[-2:]:
        copy.wait()


def load_rows(ins, take, rows, sems):
    cells = ins[0].shape[1]
    side = rows.shape[0]
    for d in range(len(ins)):
        to = rows.at[:, pl.ds(d * cells, cells)]
        pltpu.make_async_copy(ins[d].at[pl.ds(take * side, side)], to, sems.at[d]).start()


def wait_rows(planes, rows, sems):
    cells = rows.shape[1] // planes
    for d in range(planes):
        to = rows.at[:, pl.ds(d * cells, cells)]
        pltpu.make_async_copy(to, to, sems.at[d]).wait()


def rows_kernel(planes, take, field, chained, *refs):
    ins, basis_hbm = refs[:planes], refs[planes]
    out_hbm, rows, basis, acc, in_sems, basis_sems, out_sems = refs[planes + 1 + chained :]
    load_rows(ins, take, rows, in_sems)
    load_basis(basis_hbm, basis, basis_sems, range(SPANS))
    wait_rows(planes, rows, in_sems)
    multiply((field,), basis, out_hbm, (rows,), acc, basis_sems, out_sems)


def last_kernel(planes, per_plane, capacity, order, *refs):
    slot_ref, ins, (box_hbm, basis_hbm, _, out_hbm) = refs[0], refs[1 : 1 + planes], refs[1 + planes : 5 + planes]
    rows, one, two, basis, acc, box, in_sems, box_sems, basis_sems, out_sems = refs[5 + planes :]
    tiles = box.shape[0]
    sliver = COLS // planes
    load_rows(ins, 0, rows, in_sems)
    load_basis(basis_hbm, basis, basis_sems, range(1))
    for t in range(tiles):
        pltpu.make_async_copy(box_hbm.at[t], box.at[t], box_sems.at[t]).start()
    load_basis(basis_hbm, basis, basis_sems, range(1, SPANS))

    def piece(d, place):
        at = slot_ref[d, place]
        row = pl.multiple_of((at % (planes * capacity)) * sliver, sliver)
        return box[at // (planes * capacity), pl.ds(row, sliver)]

    def gather(rows, cells, d):
        for j in range(per_plane // 2):
            lanes = pl.ds((d * per_plane + 2 * j) * BPHI, LANES)
            for g in range(CG_DEV):
                even = piece(d, 2 * j * CG_DEV + g)
                odd = piece(d, (2 * j + 1) * CG_DEV + g)
                both = jnp.concatenate([even[:, cells], odd[:, cells]], axis=1)
                rows[pl.ds(g * sliver, sliver), lanes] = both

    def beside(n):
        if n == 1:
            for t in range(tiles):
                pltpu.make_async_copy(box.at[t], box.at[t], box_sems.at[t]).wait()
        first = SPANS - 1
        for d in range(planes):
            if n == 1 + d * first // planes:
                gather(one, slice(0, BPHI), d)
            if n == SPANS + d * SPANS // planes:
                gather(two, slice(BPHI, LANES), d)

    wait_rows(planes, rows, in_sems)
    multiply(order, basis, out_hbm, (rows, one, two), acc, basis_sems, out_sems, beside)


def transform(kernel, operands, specs, total, basis, planes, extra, name):
    sliver = COLS // planes
    operands = operands + in_hbm(basis)
    specs = specs + [ANY]
    aliases = {}
    if total is not None:
        aliases = {len(operands): 0}
        operands, specs = operands + [total], specs + [ANY]
    rows = pltpu.VMEM((CG_DEV * sliver, NPHI), jnp.bfloat16)
    more, sems = extra
    return pl.pallas_call(
        kernel,
        in_specs=specs,
        out_specs=HBM,
        out_shape=pltpu.HBM((FIELDS, CG_DEV, sliver, NPHI), jnp.float32),
        scratch_shapes=[rows] * (3 if more else 1)
        + [
            pltpu.VMEM((SPANS, NPHI, NPHI // SPANS), jnp.bfloat16),
            pltpu.VMEM((2, CG_DEV, sliver, NPHI // SPANS), jnp.float32),
        ]
        + more
        + [pltpu.SemaphoreType.DMA((planes,))]
        + sems
        + [pltpu.SemaphoreType.DMA((SPANS,)), pltpu.SemaphoreType.DMA((2,))],
        input_output_aliases=aliases,
        compiler_params=params(),
        cost_estimate=SLOWER if name == "rows" else LIGHT,
        name=name,
    )(*operands)


def transform_rows(slabs, take, basis, total, field):
    planes = len(slabs)
    kernel = functools.partial(rows_kernel, planes, take, field, int(total is not None))
    return transform(kernel, in_hbm(*slabs), [ANY] * planes, total, basis, planes, ([], []), "rows")


def transform_last(slabs, box, slot, basis, total, order, per_plane, capacity):
    planes = slot.shape[0]
    kernel = functools.partial(last_kernel, planes, per_plane, capacity, order)
    extra = ([pltpu.VMEM(box.shape, jnp.bfloat16)], [pltpu.SemaphoreType.DMA((box.shape[0],))])
    operands, specs = [slot] + in_hbm(*slabs, box), [SMEM] + [ANY] * (planes + 1)
    return transform(kernel, operands, specs, total, basis, planes, extra, "last")


def rank_of(dest):
    slots = dest.shape[-1]
    at = jnp.arange(slots, dtype=jnp.int32)
    same = (dest[..., :, None] == dest[..., None, :]) & (at[None, :] < at[:, None])
    return jnp.sum(same.astype(jnp.int32), axis=-1)


def as_note(dest, place_level, width):
    count = dest.size
    pad = -count % width
    each = (count + pad) // width
    codes = [jnp.pad(c.reshape(-1), (0, pad)).reshape(each, width) for c in (dest, place_level)]
    both = jnp.concatenate(codes, axis=0)
    return jnp.pad(both, ((0, NOTE - 2 * each), (0, 0))).astype(jnp.bfloat16)


def from_note(note, count):
    width = note.shape[2]
    each = -(-count // width)
    note = note.astype(jnp.float32).astype(jnp.int32)
    dest = note[:, :each].reshape(-1, each * width)[:, :count]
    place_level = note[:, each : 2 * each].reshape(-1, each * width)[:, :count]
    return dest, place_level


def local(blocks, levels, block_dest, block_phi, block_group):
    tiles = lax.axis_size("tile")
    planes = lax.axis_size("phi")
    tile = lax.axis_index("tile")
    plane = lax.axis_index("phi")
    slots = blocks.shape[0]
    per_plane = NPHI // BPHI // planes
    places = per_plane * CG_DEV
    capacity = 2 * slots // tiles
    me = plane.astype(jnp.int32).reshape(1)
    weight = 1.0 / jnp.left_shift(1, levels).astype(jnp.float32)
    place_iota = jnp.arange(places, dtype=jnp.int32)

    def over_phi(parts):
        moved = [parts[0]]
        for d in range(1, planes):
            pairs = [(s, (s + d) % planes) for s in range(planes)]
            moved.append(lax.ppermute(parts[d], "phi", pairs))
        return moved

    def over_tile(box):
        return lax.all_to_all(box, "tile", split_axis=0, concat_axis=0, tiled=True)

    def tie(value, *others):
        return lax.optimization_barrier((value,) + others)[0]

    place_level = levels * places + block_phi * CG_DEV + block_group
    distance = jnp.arange(planes, dtype=jnp.int32)[:, None]
    box_note = as_note(block_dest, place_level, COLS)
    box = post(blocks, block_dest, box_note, GROUPS[0], tiles, capacity)
    pieces = cut(blocks, weight, as_note(block_dest, place_level, LANES), me, planes)
    next_box = post(tie(blocks, pieces[0]), block_dest, box_note, GROUPS[1], tiles, capacity)

    back = (plane - jnp.arange(planes, dtype=jnp.int32)) % planes
    basis = rotated_basis(NPHI, back)

    first = over_tile(box)
    sent = over_phi(pieces)
    second = over_tile(tie(next_box, first, basis, sent[1], sent[planes - 1]))

    got_dest, got_code = from_note(first[:, -NOTE:], slots)
    got_slot = jnp.arange(tiles, dtype=jnp.int32)[:, None] * capacity + rank_of(got_dest)
    here = (got_dest == tile)[..., None] & ((got_code % places)[..., None] == place_iota)
    slot = jnp.sum(jnp.where(here, got_slot[..., None], 0), axis=(0, 1))
    level = jnp.sum(jnp.where(here, (got_code // places)[..., None], 0), axis=(0, 1))
    got_weight = 1.0 / jnp.left_shift(1, level).astype(jnp.float32)
    note = as_note(got_dest, got_code, per_plane * BPHI)

    dest, _ = from_note(jnp.stack([part[-NOTE:] for part in sent]), slots)
    out_slot = (dest * planes + distance) * capacity + rank_of(dest)

    arrived = tie(first, *sent[1:])
    early = over_phi(sort(arrived, slot, got_weight, note, me, planes, 2, capacity))
    outbox = mail(sent, out_slot, tiles, capacity)
    last = over_tile(tie(outbox, second))
    rest = sort(second, slot, got_weight, note, me, planes, 1, capacity)
    early = [tie(early[0], *rest)] + early[1:]
    rest = over_phi(rest)

    from_dest, from_code = from_note(jnp.stack([part[-NOTE:] for part in early]), tiles * slots)
    from_dest = from_dest.reshape(planes, tiles, slots)
    from_place = from_code.reshape(planes, tiles, slots) % places
    start = jnp.arange(tiles, dtype=jnp.int32)[None, :, None] * planes + distance[..., None]
    from_slot = start * capacity + rank_of(from_dest)
    here = (from_dest == tile)[..., None] & (from_place[..., None] == place_iota)
    routed = jnp.sum(jnp.where(here, from_slot[..., None], 0), axis=(1, 2))

    total = transform_rows(early, 0, basis, None, GROUPS[0][0])
    total = transform_rows(early, 1, basis, total, GROUPS[0][1])
    order = GROUPS[1] + PAIR
    return transform_last(rest, last, routed, basis, total, order, per_plane, capacity)


def solution(mesh):
    in_specs = (
        P(("tile", "phi"), None, None, None),
        P(("tile", "phi")),
        P(("tile", "phi")),
        P(("tile", "phi")),
        P(("tile", "phi")),
    )
    out_specs = P(None, "tile", "phi", None)
    return jax.shard_map(local, mesh=mesh, in_specs=in_specs, out_specs=out_specs, check_vma=False)
```

time: 312 us -> 304 us (0.974)
  starting transfers between devices: 34.4 us -> 28.3 us
  Pallas kernels: 85.3 us -> 79.7 us
  local copies, waits for them, and re-layouts: 0.44 us -> 4.75 us
    all_to_all x3, waiting for transfers between devices: 0.01 us -> 27.4 us  [over_tile(): return lax.all_to_all(box, 'tile', split_axis=0, concat_axis=0, tiled=True)]
    ppermute x12 -> x9, waiting for transfers between devices: 173 us -> 147 us  [over_phi(): moved.append(lax.ppermute(parts[d], 'phi', pairs))]
    ppermute x12 -> x9, starting transfers between devices: 19 us -> 11.6 us  [over_phi(): moved.append(lax.ppermute(parts[d], 'phi', pairs))]
    pallas_call x4 -> x3, Pallas kernels: 48 us -> 43 us  [transform(): pl.pallas_call(kernel, in_specs=specs, out_specs=HBM, out_shape=pltpu.HBM...]
  transfers between devices with their start and end apart: 15 -> 12, of which waited for: 8 -> 8; matrix products, arithmetic and copies ran while one was open for 5% -> 6% of each run, Pallas kernels for 19% -> 16%
where the time goes in v3:
time: 304 us; the launch traced here: 303 us
  waiting for transfers between devices  174 us (57%)
  Pallas kernels  79.7 us (26%)
  starting transfers between devices  28.3 us (9%)
  other arithmetic  15.7 us (5%)
  local copies, waits for them, and re-layouts  4.75 us (2%)
    ppermute x9, waiting for transfers between devices, over_phi(): moved.append(lax.ppermute(parts[d], 'phi', pairs))  147 us
    pallas_call x3, Pallas kernels, transform(): pl.pallas_call(kernel, in_specs=specs, out_specs=HBM, out_shape=pltpu.HBM...  43 us
    all_to_all x3, waiting for transfers between devices, over_tile(): return lax.all_to_all(box, 'tile', split_axis=0, concat_axis=0, tiled=True)  27.4 us
    all_to_all x3, starting transfers between devices, over_tile(): return lax.all_to_all(box, 'tile', split_axis=0, concat_axis=0, tiled=True)  16.7 us
    pallas_call x2, Pallas kernels, sort(): pl.pallas_call(functools.partial(sort_kernel, planes, count, capacity), i...  13.2 us
    ppermute x9, starting transfers between devices, over_phi(): moved.append(lax.ppermute(parts[d], 'phi', pairs))  11.6 us
    pallas_call x2, Pallas kernels, post(): pl.pallas_call(functools.partial(post_kernel, fields, tiles, capacity), i...  10.7 us
    pallas_call x1, Pallas kernels, mail(): pl.pallas_call(functools.partial(mail_kernel, planes, tiles, capacity), i...  7.73 us
  transfers between devices with their start and end apart: 12, of which 8 were waited for; matrix products, arithmetic and copies ran while one was open for 6% of the time, Pallas kernels for 16%

profile of v3, /device:TPU:10, one launch (start us, length us, event | category | flops | bytes accessed | tf_op | source)
XLA Modules:
  0.0 302.8 jit_solution(11606511755021329885)
XLA Ops:
  0.0 0.7 convert.34
  0.7 0.7 add_convert_fusion.1
  1.4 0.6 copy-done
  2.1 6.3 %post.2 = bf16[8,2064,256]{2,1,0:T(8,128)(2,1)} custom-call(s32[64]{0:T(128)S(1)} %copy-done, bf16[16,256]{1,0:T(8,128)(2,1)S(1)} %fusion.21.note_ref, bf16[64,5,64,256]{3,2,1,0:T(8,128)(2,1)} %x_ref.4), custom_call_target="tpu_custom_call" | custom-call | tf_op jit(solution)/shard_map/post/pallas_call | solution.py:170
  8.4 5.5 %all-to-all-start = ((bf16[8,2064,256]{2,1,0:T(8,128)(2,1)}), bf16[8,2064,256]{2,1,0:T(8,128)(2,1)}, u32[]{:S(2)}, u32[]{:S(2)}) async-start(bf16[8,2064,256]{2,1,0:T(8,128)(2,1)} %post.2), calls=%async_computation | async-start | bytes 16908288 | tf_op jit(solution)/shard_map/all_to_all | solution.py:482
  13.9 5.1 %cut.1 = (bf16[4112,128]{1,0:T(8,128)(2,1)}, bf16[4112,128]{1,0:T(8,128)(2,1)}, bf16[4112,128]{1,0:T(8,128)(2,1)}, bf16[4112,128]{1,0:T(8,128)(2,1)}) custom-call(s32[1]{0:T(128)} %bitcast.me_ref, f32[64]{0:T(128)S(1)} %convert_divide_fusion.weight_ref, bf16[16,128]{1,0:T(8,128)(2,1)S(1)} %fusion.28.note_ref, bf16[64,5,64,256]{3,2,1,0:T(8,128)(2,1)} %x_ref.4), custom_call_target="tpu_custom_call" | custom-call | tf_op jit(solution)/shard_map/cut/pallas_call | solution.py:116
  19.0 1.6 collective-permute-start
  20.7 1.1 collective-permute-start.1
  21.7 1.9 collective-permute-start.2
  23.8 0.1 add.181
  23.9 1.1 select_multiply_fusion
  25.0 2.0 fusion.10
  27.1 4.4 %post.3 = bf16[8,1040,256]{2,1,0:T(8,128)(2,1)} custom-call(s32[64]{0:T(128)S(1)} %copy-done.1, bf16[16,256]{1,0:T(8,128)(2,1)S(1)} %fusion.21.note_ref, bf16[64,5,64,256]{3,2,1,0:T(8,128)(2,1)} %x_ref.4), custom_call_target="tpu_custom_call" | custom-call | tf_op jit(solution)/shard_map/post/pallas_call | solution.py:170
  31.5 0.7 slice_bitcast_fusion.7
  32.2 6.7 %add_convert_fusion = bf16[4,32,64,512]{3,2,1,0:T(8,128)(2,1)} fusion(f32[4,64,512]{2,1,0:T(8,128)S(1)} %bitcast.35, f32[4,32,512]{2,1,0:T(8,128)S(1)} %bitcast.37, f32[4,64,512]{2,1,0:T(8,128)S(1)} %bitcast.36, f32[4,32,512]{2,1,0:T(8,128)S(1)} %bitcast.38), kind=kLoop, calls=%fused_computation | loop fusion | flops 16777216 | bytes 9961472 | tf_op jit(solution)/shard_map/convert_element_type | solution.py:59
  38.9 50.8 %collective-permute-done.refs_1_ = bf16[4112,128]{1,0:T(8,128)(2,1)S(1)} collective-permute-done((bf16[4112,128]{1,0:T(8,128)(2,1)}, bf16[4112,128]{1,0:T(8,128)(2,1)S(1)}, u32[]{:S(2)}, u32[]{:S(2)}) %collective-permute-start) | collective-permute-done | bytes 1052704 | tf_op jit(solution)/shard_map/ppermute | solution.py:478
  89.7 21.8 %collective-permute-done.1.refs_2_ = bf16[4112,128]{1,0:T(8,128)(2,1)S(1)} collective-permute-done((bf16[4112,128]{1,0:T(8,128)(2,1)}, bf16[4112,128]{1,0:T(8,128)(2,1)S(1)}, u32[]{:S(2)}, u32[]{:S(2)}) %collective-permute-start.1) | collective-permute-done | bytes 1052704 | tf_op jit(solution)/shard_map/ppermute | solution.py:478
  111.5 1.8 collective-permute-done.2.refs_3_
  113.3 0.7 slice_bitcast_fusion.4
  114.0 0.2 convert_reduce_fusion.2
  114.2 4.8 %all-to-all-start.1 = ((bf16[8,1040,256]{2,1,0:T(8,128)(2,1)}), bf16[8,1040,256]{2,1,0:T(8,128)(2,1)}, u32[]{:S(2)}, u32[]{:S(2)}) async-start(bf16[8,1040,256]{2,1,0:T(8,128)(2,1)} %post.3), calls=%async_computation.1 | async-start | bytes 8519680 | tf_op jit(solution)/shard_map/all_to_all | solution.py:482
  119.0 0.9 convert_convert_fusion
  119.9 0.1 reshape.343
  120.0 0.1 reshape.344
  120.1 0.3 convert_reduce_fusion.1
  120.6 0.3 select_reduce_fusion.1
  120.9 7.8 %sort.2 = (bf16[1040,512]{1,0:T(8,128)(2,1)}, bf16[1040,512]{1,0:T(8,128)(2,1)}, bf16[1040,512]{1,0:T(8,128)(2,1)}, bf16[1040,512]{1,0:T(8,128)(2,1)}) custom-call(s32[1]{0:T(128)} %bitcast.me_ref, s32[64]{0:T(128)S(1)} %get-tuple-element.50.slot_ref, f32[64]{0:T(128)S(1)} %convert_divide_fusion.1.weight_ref, bf16[16,512]{1,0:T(8,128)(2,1)S(1)} %fusion.18.note_ref, ...), custom_call_target="tpu_custom_call" | custom-call | tf_op jit(solution)/shard_map/sort/pallas_call | solution.py:236
  128.8 1.6 collective-permute-start.4
  130.4 1.9 collective-permute-start.5
  132.4 7.7 %mail.1 = bf16[8,4096,128]{2,1,0:T(8,128)(2,1)} custom-call(s32[4,64]{1,0:T(4,128)S(1)} %multiply_add_fusion.1.slot_ref, bf16[4112,128]{1,0:T(8,128)(2,1)} %get-tuple-element.31.refs_0_, bf16[4112,128]{1,0:T(8,128)(2,1)} %copy-done.8, bf16[4112,128]{1,0:T(8,128)(2,1)} %copy-done.9, bf16[4112,128]{1,0:T(8,128)(2,1)} %collective-permute-done.2.refs_3_), custom_call_target="tpu_custom_call" | custom-call | flops 20000000000 | tf_op jit(solution)/shard_map/mail/pallas_call | solution.py:281
  140.1 27.4 %all-to-all-done.1.x_ref = bf16[8,1040,256]{2,1,0:T(8,128)(2,1)} async-done(((bf16[8,1040,256]{2,1,0:T(8,128)(2,1)}), bf16[8,1040,256]{2,1,0:T(8,128)(2,1)}, u32[]{:S(2)}, u32[]{:S(2)}) %all-to-all-start.1) | async-done | bytes 4259872 | tf_op jit(solution)/shard_map/all_to_all | solution.py:482
  167.5 6.3 %all-to-all-start.2 = ((bf16[8,4096,128]{2,1,0:T(8,128)(2,1)}), bf16[8,4096,128]{2,1,0:T(8,128)(2,1)}, u32[]{:S(2)}, u32[]{:S(2)}) async-start(bf16[8,4096,128]{2,1,0:T(8,128)(2,1)} %mail.1), calls=%async_computation.2 | async-start | bytes 16777216 | tf_op jit(solution)/shard_map/all_to_all | solution.py:482
  173.8 47.1 %collective-permute-done.4.refs_2_ = bf16[1040,512]{1,0:T(8,128)(2,1)S(1)} collective-permute-done((bf16[1040,512]{1,0:T(8,128)(2,1)}, bf16[1040,512]{1,0:T(8,128)(2,1)S(1)}, u32[]{:S(2)}, u32[]{:S(2)}) %collective-permute-start.4) | collective-permute-done | bytes 1064992 | tf_op jit(solution)/shard_map/ppermute | solution.py:478
  221.0 2.0 collective-permute-done.5.refs_3_
  223.0 0.7 slice_bitcast_fusion
  223.7 5.4 %sort.3 = (bf16[528,512]{1,0:T(8,128)(2,1)}, bf16[528,512]{1,0:T(8,128)(2,1)}, bf16[528,512]{1,0:T(8,128)(2,1)}, bf16[528,512]{1,0:T(8,128)(2,1)}) custom-call(s32[1]{0:T(128)} %bitcast.me_ref, s32[64]{0:T(128)S(1)} %get-tuple-element.50.slot_ref, f32[64]{0:T(128)S(1)} %convert_divide_fusion.1.weight_ref, bf16[16,512]{1,0:T(8,128)(2,1)S(1)} %fusion.18.note_ref, ...), custom_call_target="tpu_custom_call" | custom-call | tf_op jit(solution)/shard_map/sort/pallas_call | solution.py:236
  229.2 1.4 collective-permute-start.7
  230.5 1.9 collective-permute-start.8
  232.5 0.7 slice_bitcast_fusion.3
  233.2 0.1 reshape_reshape.7
  233.4 9.4 %rows.2.refs_5_ = f32[5,8,64,2048]{3,2,1,0:T(8,128)} custom-call(bf16[1040,512]{1,0:T(8,128)(2,1)} %get-tuple-element.42.refs_0_, bf16[1040,512]{1,0:T(8,128)(2,1)} %copy-done.6, bf16[1040,512]{1,0:T(8,128)(2,1)} %copy-done.7, bf16[1040,512]{1,0:T(8,128)(2,1)} %collective-permute-done.5.refs_3_, bf16[4,2048,512]{2,1,0:T(8,128)(2,1)} %bitcast.32), custom_call_target="tpu_custom_call" | custom-call | flops 30000001024 | tf_op jit(solution)/shard_map/rows/pallas_call | solution.py:401
  242.8 9.4 %rows.3.refs_7_ = f32[5,8,64,2048]{3,2,1,0:T(8,128)} custom-call(bf16[1040,512]{1,0:T(8,128)(2,1)} %get-tuple-element.42.refs_0_, bf16[1040,512]{1,0:T(8,128)(2,1)} %copy-done.6, bf16[1040,512]{1,0:T(8,128)(2,1)} %copy-done.7, bf16[1040,512]{1,0:T(8,128)(2,1)} %collective-permute-done.5.refs_3_, ...), custom_call_target="tpu_custom_call", output_to_operand_aliasing={{}: (5, {})} | custom-call | flops 30000001024 | tf_op jit(solution)/shard_map/rows/pallas_call | solution.py:401
  252.3 0.9 convert_reduce_fusion
  253.3 1.3 select_reduce_fusion.refs_0_
  254.6 21.6 %collective-permute-done.7.refs_3_ = bf16[528,512]{1,0:T(8,128)(2,1)S(1)} collective-permute-done((bf16[528,512]{1,0:T(8,128)(2,1)}, bf16[528,512]{1,0:T(8,128)(2,1)S(1)}, u32[]{:S(2)}, u32[]{:S(2)}) %collective-permute-start.7) | collective-permute-done | bytes 540704 | tf_op jit(solution)/shard_map/ppermute | solution.py:478
  276.2 1.4 collective-permute-done.8.refs_4_
  277.7 0.8 copy-done.4
  278.4 24.2 %last.1 = f32[5,8,64,2048]{3,2,1,0:T(8,128)} custom-call(s32[4,64]{1,0:T(4,128)S(1)} %select_reduce_fusion.refs_0_, bf16[528,512]{1,0:T(8,128)(2,1)} %get-tuple-element.38.refs_1_, bf16[528,512]{1,0:T(8,128)(2,1)} %copy-done.2, bf16[528,512]{1,0:T(8,128)(2,1)} %copy-done.3, bf16[528,512]{1,0:T(8,128)(2,1)} %copy-done.4, ...), custom_call_target="tpu_custom_call", output_to_operand_aliasing={{}: (7, {})} | custom-call | tf_op jit(solution)/shard_map/last/pallas_call | solution.py:401
  (62 shorter events, 0.8 us)
Async XLA Ops:
  1.4 0.7 copy-start
  8.4 5.5 %copy-start.5 = (s32[64]{0:T(128)S(1)}, s32[64]{0:T(128)}, u32[]{:S(2)}) copy-start(s32[64]{0:T(128)} %param.6) | copy-start | bytes 772
  8.4 105.8 %all-to-all-start = ((bf16[8,2064,256]{2,1,0:T(8,128)(2,1)}), bf16[8,2064,256]{2,1,0:T(8,128)(2,1)}, u32[]{:S(2)}, u32[]{:S(2)}) async-start(bf16[8,2064,256]{2,1,0:T(8,128)(2,1)} %post.2), calls=%async_computation | async-start | bytes 16908288 | tf_op jit(solution)/shard_map/all_to_all | solution.py:482
  19.0 8.1 %copy-start.1 = (s32[64]{0:T(128)S(1)}, s32[64]{0:T(128)}, u32[]{:S(2)}) copy-start(s32[64]{0:T(128)} %dest_ref.3) | copy-start | bytes 772
  19.0 70.7 %collective-permute-start = (bf16[4112,128]{1,0:T(8,128)(2,1)}, bf16[4112,128]{1,0:T(8,128)(2,1)S(1)}, u32[]{:S(2)}, u32[]{:S(2)}) collective-permute-start(bf16[4112,128]{1,0:T(8,128)(2,1)} %get-tuple-element.26), channel_id=1, source_target_pairs={{0,1},{1,2},{2,3},{3,0},{4,5},{5,6},{6,7},{7,4},{8,9},{9,10},{10,1... | collective-permute-start | bytes 3158024 | tf_op jit(solution)/shard_map/ppermute | solution.py:478
  20.7 90.8 %collective-permute-start.1 = (bf16[4112,128]{1,0:T(8,128)(2,1)}, bf16[4112,128]{1,0:T(8,128)(2,1)S(1)}, u32[]{:S(2)}, u32[]{:S(2)}) collective-permute-start(bf16[4112,128]{1,0:T(8,128)(2,1)} %get-tuple-element.27), channel_id=1, source_target_pairs={{0,2},{1,3},{2,0},{3,1},{4,6},{5,7},{6,4},{7,5},{8,10},{9,11},{10,... | collective-permute-start | bytes 3158024 | tf_op jit(solution)/shard_map/ppermute | solution.py:478
  21.7 91.5 %collective-permute-start.2 = (bf16[4112,128]{1,0:T(8,128)(2,1)}, bf16[4112,128]{1,0:T(8,128)(2,1)}, u32[]{:S(2)}, u32[]{:S(2)}) collective-permute-start(bf16[4112,128]{1,0:T(8,128)(2,1)} %get-tuple-element.28), channel_id=1, source_target_pairs={{0,3},{1,0},{2,1},{3,2},{4,7},{5,4},{6,5},{7,6},{8,11},{9,8},{10,9... | collective-permute-start | bytes 3158024 | tf_op jit(solution)/shard_map/ppermute | solution.py:478
  89.7 21.8 %copy-start.8 = (bf16[4112,128]{1,0:T(8,128)(2,1)}, bf16[4112,128]{1,0:T(8,128)(2,1)S(1)}, u32[]{:S(2)}) copy-start(bf16[4112,128]{1,0:T(8,128)(2,1)S(1)} %collective-permute-done.refs_1_) | copy-start | bytes 3158020
  111.5 2.7 copy-start.9
  114.2 53.3 %all-to-all-start.1 = ((bf16[8,1040,256]{2,1,0:T(8,128)(2,1)}), bf16[8,1040,256]{2,1,0:T(8,128)(2,1)}, u32[]{:S(2)}, u32[]{:S(2)}) async-start(bf16[8,1040,256]{2,1,0:T(8,128)(2,1)} %post.3), calls=%async_computation.1 | async-start | bytes 8519680 | tf_op jit(solution)/shard_map/all_to_all | solution.py:482
  128.8 45.1 %collective-permute-start.3 = (bf16[1040,512]{1,0:T(8,128)(2,1)}, bf16[1040,512]{1,0:T(8,128)(2,1)S(1)}, u32[]{:S(2)}, u32[]{:S(2)}) collective-permute-start(bf16[1040,512]{1,0:T(8,128)(2,1)} %get-tuple-element.43), channel_id=1, source_target_pairs={{0,1},{1,2},{2,3},{3,0},{4,5},{5,6},{6,7},{7,4},{8,9},{9,10},{10,1... | collective-permute-start | bytes 3194888 | tf_op jit(solution)/shard_map/ppermute | solution.py:478
  128.8 92.1 %collective-permute-start.4 = (bf16[1040,512]{1,0:T(8,128)(2,1)}, bf16[1040,512]{1,0:T(8,128)(2,1)S(1)}, u32[]{:S(2)}, u32[]{:S(2)}) collective-permute-start(bf16[1040,512]{1,0:T(8,128)(2,1)} %get-tuple-element.44), channel_id=1, source_target_pairs={{0,2},{1,3},{2,0},{3,1},{4,6},{5,7},{6,4},{7,5},{8,10},{9,11},{10,... | collective-permute-start | bytes 3194888 | tf_op jit(solution)/shard_map/ppermute | solution.py:478
  130.4 92.6 %collective-permute-start.5 = (bf16[1040,512]{1,0:T(8,128)(2,1)}, bf16[1040,512]{1,0:T(8,128)(2,1)}, u32[]{:S(2)}, u32[]{:S(2)}) collective-permute-start(bf16[1040,512]{1,0:T(8,128)(2,1)} %get-tuple-element.45), channel_id=1, source_target_pairs={{0,3},{1,0},{2,1},{3,2},{4,7},{5,4},{6,5},{7,6},{8,11},{9,8},{10,9... | collective-permute-start | bytes 3194888 | tf_op jit(solution)/shard_map/ppermute | solution.py:478
  167.5 110.2 %all-to-all-start.2 = ((bf16[8,4096,128]{2,1,0:T(8,128)(2,1)}), bf16[8,4096,128]{2,1,0:T(8,128)(2,1)}, u32[]{:S(2)}, u32[]{:S(2)}) async-start(bf16[8,4096,128]{2,1,0:T(8,128)(2,1)} %mail.1), calls=%async_computation.2 | async-start | bytes 16777216 | tf_op jit(solution)/shard_map/all_to_all | solution.py:482
  173.8 55.2 %copy-start.6 = (bf16[1040,512]{1,0:T(8,128)(2,1)}, bf16[1040,512]{1,0:T(8,128)(2,1)S(1)}, u32[]{:S(2)}) copy-start(bf16[1040,512]{1,0:T(8,128)(2,1)S(1)} %collective-permute-done.3.refs_1_) | copy-start | bytes 3194884
  221.0 8.1 %copy-start.7 = (bf16[1040,512]{1,0:T(8,128)(2,1)}, bf16[1040,512]{1,0:T(8,128)(2,1)S(1)}, u32[]{:S(2)}) copy-start(bf16[1040,512]{1,0:T(8,128)(2,1)S(1)} %collective-permute-done.4.refs_2_) | copy-start | bytes 3194884
  229.1 25.5 %collective-permute-start.6 = (bf16[528,512]{1,0:T(8,128)(2,1)}, bf16[528,512]{1,0:T(8,128)(2,1)S(1)}, u32[]{:S(2)}, u32[]{:S(2)}) collective-permute-start(bf16[528,512]{1,0:T(8,128)(2,1)} %get-tuple-element.39), channel_id=1, source_target_pairs={{0,1},{1,2},{2,3},{3,0},{4,5},{5,6},{6,7},{7,4},{8,9},{9,10},{10,1... | collective-permute-start | bytes 1622024 | tf_op jit(solution)/shard_map/ppermute | solution.py:478
  229.2 47.1 %collective-permute-start.7 = (bf16[528,512]{1,0:T(8,128)(2,1)}, bf16[528,512]{1,0:T(8,128)(2,1)S(1)}, u32[]{:S(2)}, u32[]{:S(2)}) collective-permute-start(bf16[528,512]{1,0:T(8,128)(2,1)} %get-tuple-element.40), channel_id=1, source_target_pairs={{0,2},{1,3},{2,0},{3,1},{4,6},{5,7},{6,4},{7,5},{8,10},{9,11},{10,... | collective-permute-start | bytes 1622024 | tf_op jit(solution)/shard_map/ppermute | solution.py:478
  230.5 47.1 %collective-permute-start.8 = (bf16[528,512]{1,0:T(8,128)(2,1)}, bf16[528,512]{1,0:T(8,128)(2,1)S(1)}, u32[]{:S(2)}, u32[]{:S(2)}) collective-permute-start(bf16[528,512]{1,0:T(8,128)(2,1)} %get-tuple-element.41), channel_id=1, source_target_pairs={{0,3},{1,0},{2,1},{3,2},{4,7},{5,4},{6,5},{7,6},{8,11},{9,8},{10,9... | collective-permute-start | bytes 1622024 | tf_op jit(solution)/shard_map/ppermute | solution.py:478
  254.6 23.0 %copy-start.2 = (bf16[528,512]{1,0:T(8,128)(2,1)}, bf16[528,512]{1,0:T(8,128)(2,1)S(1)}, u32[]{:S(2)}) copy-start(bf16[528,512]{1,0:T(8,128)(2,1)S(1)} %collective-permute-done.6.refs_2_) | copy-start | bytes 1622020
  276.2 1.4 copy-start.3
  277.6 0.8 copy-start.4

commit v4 on v3

--- a/solution.py
+++ b/solution.py
@@ -164,7 +164,7 @@
         pltpu.make_async_copy(box_ref.at[t], out_ref.at[t], out_sems.at[t]).wait()
 
 
-def post(blocks, dest, note, fields, tiles, capacity):
+def post(blocks, dest, note, fields, tiles, capacity, cost):
     slots = blocks.shape[0]
     rows = capacity * len(fields) * BPHI + NOTE
     return pl.pallas_call(
@@ -180,7 +180,7 @@
             pltpu.SemaphoreType.DMA((tiles,)),
         ],
         compiler_params=params(),
-        cost_estimate=LIGHT,
+        cost_estimate=cost,
         name="post",
     )(dest, note, *in_hbm(blocks))
 
@@ -343,20 +343,22 @@
     ins, basis_hbm = refs[:planes], refs[planes]
     out_hbm, rows, basis, acc, in_sems, basis_sems, out_sems = refs[planes + 1 + chained :]
     load_rows(ins, take, rows, in_sems)
-    load_basis(basis_hbm, basis, basis_sems, range(SPANS))
+    load_basis(basis_hbm, basis, basis_sems, range(1))
     wait_rows(planes, rows, in_sems)
+    load_basis(basis_hbm, basis, basis_sems, range(1, SPANS))
     multiply((field,), basis, out_hbm, (rows,), acc, basis_sems, out_sems)
 
 
-def last_kernel(planes, per_plane, capacity, order, *refs):
-    slot_ref, ins, (box_hbm, basis_hbm, _, out_hbm) = refs[0], refs[1 : 1 + planes], refs[1 + planes : 5 + planes]
-    rows, one, two, basis, acc, box, in_sems, box_sems, basis_sems, out_sems = refs[5 + planes :]
+def box_kernel(planes, per_plane, capacity, *refs):
+    slot_ref, box_hbm, basis_hbm, _, out_hbm = refs[:5]
+    one, two, basis, acc, box, box_sems, basis_sems, out_sems = refs[5:]
     tiles = box.shape[0]
     sliver = COLS // planes
-    load_rows(ins, 0, rows, in_sems)
+    for t in range(tiles):
+        pltpu.make_async_copy(box_hbm.at[t], box.at[t], box_sems.at[t]).start()
     load_basis(basis_hbm, basis, basis_sems, range(1))
     for t in range(tiles):
-        pltpu.make_async_copy(box_hbm.at[t], box.at[t], box_sems.at[t]).start()
+        pltpu.make_async_copy(box.at[t], box.at[t], box_sems.at[t]).wait()
     load_basis(basis_hbm, basis, basis_sems, range(1, SPANS))
 
     def piece(d, place):
@@ -374,21 +376,16 @@
                 rows[pl.ds(g * sliver, sliver), lanes] = both
 
     def beside(n):
-        if n == 1:
-            for t in range(tiles):
-                pltpu.make_async_copy(box.at[t], box.at[t], box_sems.at[t]).wait()
-        first = SPANS - 1
         for d in range(planes):
-            if n == 1 + d * first // planes:
-                gather(one, slice(0, BPHI), d)
-            if n == SPANS + d * SPANS // planes:
+            if n == d * SPANS // planes:
                 gather(two, slice(BPHI, LANES), d)
 
-    wait_rows(planes, rows, in_sems)
-    multiply(order, basis, out_hbm, (rows, one, two), acc, basis_sems, out_sems, beside)
-
-
-def transform(kernel, operands, specs, total, basis, planes, extra, name):
+    for d in range(planes):
+        gather(one, slice(0, BPHI), d)
+    multiply(PAIR, basis, out_hbm, (one, two), acc, basis_sems, out_sems, beside)
+
+
+def transform(kernel, operands, specs, total, basis, planes, fields, extra, sems, cost, name):
     sliver = COLS // planes
     operands = operands + in_hbm(basis)
     specs = specs + [ANY]
@@ -397,40 +394,39 @@
         aliases = {len(operands): 0}
         operands, specs = operands + [total], specs + [ANY]
     rows = pltpu.VMEM((CG_DEV * sliver, NPHI), jnp.bfloat16)
-    more, sems = extra
     return pl.pallas_call(
         kernel,
         in_specs=specs,
         out_specs=HBM,
         out_shape=pltpu.HBM((FIELDS, CG_DEV, sliver, NPHI), jnp.float32),
-        scratch_shapes=[rows] * (3 if more else 1)
+        scratch_shapes=[rows] * fields
         + [
             pltpu.VMEM((SPANS, NPHI, NPHI // SPANS), jnp.bfloat16),
             pltpu.VMEM((2, CG_DEV, sliver, NPHI // SPANS), jnp.float32),
         ]
-        + more
-        + [pltpu.SemaphoreType.DMA((planes,))]
-        + sems
+        + extra
+        + [pltpu.SemaphoreType.DMA((sems,))]
         + [pltpu.SemaphoreType.DMA((SPANS,)), pltpu.SemaphoreType.DMA((2,))],
         input_output_aliases=aliases,
         compiler_params=params(),
-        cost_estimate=SLOWER if name == "rows" else LIGHT,
+        cost_estimate=cost,
         name=name,
     )(*operands)
 
 
-def transform_rows(slabs, take, basis, total, field):
+def transform_rows(slabs, take, basis, total, field, cost):
     planes = len(slabs)
     kernel = functools.partial(rows_kernel, planes, take, field, int(total is not None))
-    return transform(kernel, in_hbm(*slabs), [ANY] * planes, total, basis, planes, ([], []), "rows")
-
-
-def transform_last(slabs, box, slot, basis, total, order, per_plane, capacity):
-    planes = slot.shape[0]
-    kernel = functools.partial(last_kernel, planes, per_plane, capacity, order)
-    extra = ([pltpu.VMEM(box.shape, jnp.bfloat16)], [pltpu.SemaphoreType.DMA((box.shape[0],))])
-    operands, specs = [slot] + in_hbm(*slabs, box), [SMEM] + [ANY] * (planes + 1)
-    return transform(kernel, operands, specs, total, basis, planes, extra, "last")
+    operands, specs = in_hbm(*slabs), [ANY] * planes
+    return transform(kernel, operands, specs, total, basis, planes, 1, [], planes, cost, "rows")
+
+
+def transform_box(box, slot, basis, total, per_plane, capacity):
+    planes, tiles = slot.shape[0], box.shape[0]
+    kernel = functools.partial(box_kernel, planes, per_plane, capacity)
+    operands, specs = [slot] + in_hbm(box), [SMEM, ANY]
+    extra = [pltpu.VMEM(box.shape, jnp.bfloat16)]
+    return transform(kernel, operands, specs, total, basis, planes, 2, extra, tiles, LIGHT, "box")
 
 
 def rank_of(dest):
@@ -487,16 +483,17 @@
     place_level = levels * places + block_phi * CG_DEV + block_group
     distance = jnp.arange(planes, dtype=jnp.int32)[:, None]
     box_note = as_note(block_dest, place_level, COLS)
-    box = post(blocks, block_dest, box_note, GROUPS[0], tiles, capacity)
+    box = post(blocks, block_dest, box_note, GROUPS[0], tiles, capacity, LIGHT)
     pieces = cut(blocks, weight, as_note(block_dest, place_level, LANES), me, planes)
-    next_box = post(tie(blocks, pieces[0]), block_dest, box_note, GROUPS[1], tiles, capacity)
+    source = tie(blocks, pieces[0])
+    next_box = post(source, block_dest, box_note, GROUPS[1], tiles, capacity, SLOWER)
 
     back = (plane - jnp.arange(planes, dtype=jnp.int32)) % planes
     basis = rotated_basis(NPHI, back)
 
     first = over_tile(box)
     sent = over_phi(pieces)
-    second = over_tile(tie(next_box, first, basis, sent[1], sent[planes - 1]))
+    second = over_tile(tie(next_box, first, basis))
 
     got_dest, got_code = from_note(first[:, -NOTE:], slots)
     got_slot = jnp.arange(tiles, dtype=jnp.int32)[:, None] * capacity + rank_of(got_dest)
@@ -506,11 +503,13 @@
     got_weight = 1.0 / jnp.left_shift(1, level).astype(jnp.float32)
     note = as_note(got_dest, got_code, per_plane * BPHI)
 
+    early = sort(first, slot, got_weight, note, me, planes, 2, capacity)
+    sent = list(lax.optimization_barrier((tuple(sent), early[0]))[0])
+    early = over_phi(early)
+
     dest, _ = from_note(jnp.stack([part[-NOTE:] for part in sent]), slots)
     out_slot = (dest * planes + distance) * capacity + rank_of(dest)
 
-    arrived = tie(first, *sent[1:])
-    early = over_phi(sort(arrived, slot, got_weight, note, me, planes, 2, capacity))
     outbox = mail(sent, out_slot, tiles, capacity)
     last = over_tile(tie(outbox, second))
     rest = sort(second, slot, got_weight, note, me, planes, 1, capacity)
@@ -525,10 +524,10 @@
     here = (from_dest == tile)[..., None] & (from_place[..., None] == place_iota)
     routed = jnp.sum(jnp.where(here, from_slot[..., None], 0), axis=(1, 2))
 
-    total = transform_rows(early, 0, basis, None, GROUPS[0][0])
-    total = transform_rows(early, 1, basis, total, GROUPS[0][1])
-    order = GROUPS[1] + PAIR
-    return transform_last(rest, last, routed, basis, total, order, per_plane, capacity)
+    total = transform_rows(early, 0, basis, None, GROUPS[0][0], SLOWER)
+    total = transform_rows(early, 1, basis, total, GROUPS[0][1], SLOWER)
+    total = transform_box(last, routed, basis, total, per_plane, capacity)
+    return transform_rows(rest, 0, basis, total, GROUPS[1][0], LIGHT)
 
 
 def solution(mesh):

time: 304 us -> 291 us (0.957)
  waiting for transfers between devices: 174 us -> 155 us
    ppermute x9, waiting for transfers between devices: 147 us -> 51.2 us  [over_phi(): moved.append(lax.ppermute(parts[d], 'phi', pairs))]
    all_to_all x3, waiting for transfers between devices: 27.4 us -> 104 us  [over_tile(): return lax.all_to_all(box, 'tile', split_axis=0, concat_axis=0, tiled=True)]
    pallas_call x3 -> x4, Pallas kernels: 43 us -> 43 us  [transform(): pl.pallas_call(kernel, in_specs=specs, out_specs=HBM, out_shape=pltpu.HBM...]
  transfers between devices with their start and end apart: 12 -> 12, of which waited for: 8 -> 6; matrix products, arithmetic and copies ran while one was open for 6% -> 6% of each run, Pallas kernels for 16% -> 22%
where the time goes in v4:
time: 291 us; the launch traced here: 289 us
  waiting for transfers between devices  155 us (53%)
  Pallas kernels  79.7 us (27%)
  starting transfers between devices  30.6 us (11%)
  other arithmetic  16 us (5%)
  local copies, waits for them, and re-layouts  7.33 us (3%)
    all_to_all x3, waiting for transfers between devices, over_tile(): return lax.all_to_all(box, 'tile', split_axis=0, concat_axis=0, tiled=True)  104 us
    ppermute x9, waiting for transfers between devices, over_phi(): moved.append(lax.ppermute(parts[d], 'phi', pairs))  51.2 us
    pallas_call x4, Pallas kernels, transform(): pl.pallas_call(kernel, in_specs=specs, out_specs=HBM, out_shape=pltpu.HBM...  43 us
    all_to_all x3, starting transfers between devices, over_tile(): return lax.all_to_all(box, 'tile', split_axis=0, concat_axis=0, tiled=True)  17.8 us
    pallas_call x2, Pallas kernels, sort(): pl.pallas_call(functools.partial(sort_kernel, planes, count, capacity), i...  13.1 us
    ppermute x9, starting transfers between devices, over_phi(): moved.append(lax.ppermute(parts[d], 'phi', pairs))  12.9 us
    pallas_call x2, Pallas kernels, post(): pl.pallas_call(functools.partial(post_kernel, fields, tiles, capacity), i...  10.7 us
    pallas_call x1, Pallas kernels, mail(): pl.pallas_call(functools.partial(mail_kernel, planes, tiles, capacity), i...  7.73 us
  transfers between devices with their start and end apart: 12, of which 6 were waited for; matrix products, arithmetic and copies ran while one was open for 6% of the time, Pallas kernels for 22%

profile of v4, /device:TPU:10, one launch (start us, length us, event | category | flops | bytes accessed | tf_op | source)
XLA Modules:
  0.0 289.1 jit_solution(1858071122408070522)
XLA Ops:
  0.0 0.7 convert.34
  0.7 0.7 add_convert_fusion.1
  1.4 0.6 copy-done
  2.1 6.3 %post.2 = bf16[8,2064,256]{2,1,0:T(8,128)(2,1)} custom-call(s32[64]{0:T(128)S(1)} %copy-done, bf16[16,256]{1,0:T(8,128)(2,1)S(1)} %fusion.21.note_ref, bf16[64,5,64,256]{3,2,1,0:T(8,128)(2,1)} %x_ref.4), custom_call_target="tpu_custom_call" | custom-call | tf_op jit(solution)/shard_map/post/pallas_call | solution.py:170
  8.4 5.4 %all-to-all-start = ((bf16[8,2064,256]{2,1,0:T(8,128)(2,1)}), bf16[8,2064,256]{2,1,0:T(8,128)(2,1)}, u32[]{:S(2)}, u32[]{:S(2)}) async-start(bf16[8,2064,256]{2,1,0:T(8,128)(2,1)} %post.2), calls=%async_computation | async-start | bytes 16908288 | tf_op jit(solution)/shard_map/all_to_all | solution.py:478
  13.9 5.1 %cut.1 = (bf16[4112,128]{1,0:T(8,128)(2,1)}, bf16[4112,128]{1,0:T(8,128)(2,1)}, bf16[4112,128]{1,0:T(8,128)(2,1)}, bf16[4112,128]{1,0:T(8,128)(2,1)}) custom-call(s32[1]{0:T(128)} %bitcast.me_ref, f32[64]{0:T(128)S(1)} %convert_divide_fusion.weight_ref, bf16[16,128]{1,0:T(8,128)(2,1)S(1)} %fusion.28.note_ref, bf16[64,5,64,256]{3,2,1,0:T(8,128)(2,1)} %x_ref.4), custom_call_target="tpu_custom_call" | custom-call | tf_op jit(solution)/shard_map/cut/pallas_call | solution.py:116
  18.9 1.6 collective-permute-start.6
  20.6 1.1 collective-permute-start.7
  21.7 1.9 collective-permute-start.8
  23.8 1.1 select_multiply_fusion
  25.0 2.0 fusion.10
  27.1 7.1 %add_convert_fusion = bf16[4,32,64,512]{3,2,1,0:T(8,128)(2,1)} fusion(f32[4,64,512]{2,1,0:T(8,128)S(1)} %bitcast.36, f32[4,32,512]{2,1,0:T(8,128)S(1)} %bitcast.38, f32[4,64,512]{2,1,0:T(8,128)S(1)} %bitcast.37, f32[4,32,512]{2,1,0:T(8,128)S(1)} %bitcast.39), kind=kLoop, calls=%fused_computation | loop fusion | flops 16777216 | bytes 9961472 | tf_op jit(solution)/shard_map/convert_element_type | solution.py:59
  34.1 4.4 %post.3 = bf16[8,1040,256]{2,1,0:T(8,128)(2,1)} custom-call(s32[64]{0:T(128)S(1)} %copy-done.1, bf16[16,256]{1,0:T(8,128)(2,1)S(1)} %fusion.21.note_ref, bf16[64,5,64,256]{3,2,1,0:T(8,128)(2,1)} %x_ref.4), custom_call_target="tpu_custom_call" | custom-call | flops 30000001024 | tf_op jit(solution)/shard_map/post/pallas_call | solution.py:170
  38.5 68.7 %all-to-all-done.x_ref = bf16[8,2064,256]{2,1,0:T(8,128)(2,1)} async-done(((bf16[8,2064,256]{2,1,0:T(8,128)(2,1)}), bf16[8,2064,256]{2,1,0:T(8,128)(2,1)}, u32[]{:S(2)}, u32[]{:S(2)}) %all-to-all-start) | async-done | bytes 8454176 | tf_op jit(solution)/shard_map/all_to_all | solution.py:478
  107.2 6.0 %all-to-all-start.1 = ((bf16[8,1040,256]{2,1,0:T(8,128)(2,1)}), bf16[8,1040,256]{2,1,0:T(8,128)(2,1)}, u32[]{:S(2)}, u32[]{:S(2)}) async-start(bf16[8,1040,256]{2,1,0:T(8,128)(2,1)} %post.3), calls=%async_computation.1 | async-start | bytes 8519680 | tf_op jit(solution)/shard_map/all_to_all | solution.py:478
  113.2 0.9 convert_convert_fusion
  114.1 0.3 convert_reduce_fusion.1
  114.7 0.3 select_reduce_fusion.1
  115.1 7.8 %sort.3 = (bf16[1040,512]{1,0:T(8,128)(2,1)}, bf16[1040,512]{1,0:T(8,128)(2,1)}, bf16[1040,512]{1,0:T(8,128)(2,1)}, bf16[1040,512]{1,0:T(8,128)(2,1)}) custom-call(s32[1]{0:T(128)} %bitcast.me_ref, s32[64]{0:T(128)S(1)} %get-tuple-element.56.slot_ref, f32[64]{0:T(128)S(1)} %convert_divide_fusion.1.weight_ref, bf16[16,512]{1,0:T(8,128)(2,1)S(1)} %fusion.18.note_ref, ...), custom_call_target="tpu_custom_call" | custom-call | tf_op jit(solution)/shard_map/sort/pallas_call | solution.py:236
  123.0 1.0 copy-done.9
  124.0 1.6 collective-permute-start.3
  125.5 1.4 collective-permute-start.4
  126.9 1.6 collective-permute-start.5
  128.6 0.7 slice_bitcast_fusion.7
  129.3 0.7 slice_bitcast_fusion.5
  129.9 0.7 slice_bitcast_fusion.4
  130.6 0.2 convert_reduce_fusion.2
  130.9 7.7 %mail.1 = bf16[8,4096,128]{2,1,0:T(8,128)(2,1)} custom-call(s32[4,64]{1,0:T(4,128)S(1)} %multiply_add_fusion.1.slot_ref, bf16[4112,128]{1,0:T(8,128)(2,1)} %get-tuple-element.48.refs_0_, bf16[4112,128]{1,0:T(8,128)(2,1)} %copy-done.8, bf16[4112,128]{1,0:T(8,128)(2,1)} %copy-done.9, bf16[4112,128]{1,0:T(8,128)(2,1)} %copy-done.10), custom_call_target="tpu_custom_call" | custom-call | flops 20000000000 | tf_op jit(solution)/shard_map/mail/pallas_call | solution.py:281
  138.6 23.0 %all-to-all-done.1.x_ref = bf16[8,1040,256]{2,1,0:T(8,128)(2,1)} async-done(((bf16[8,1040,256]{2,1,0:T(8,128)(2,1)}), bf16[8,1040,256]{2,1,0:T(8,128)(2,1)}, u32[]{:S(2)}, u32[]{:S(2)}) %all-to-all-start.1) | async-done | bytes 4259872 | tf_op jit(solution)/shard_map/all_to_all | solution.py:478
  161.6 6.4 %all-to-all-start.2 = ((bf16[8,4096,128]{2,1,0:T(8,128)(2,1)}), bf16[8,4096,128]{2,1,0:T(8,128)(2,1)}, u32[]{:S(2)}, u32[]{:S(2)}) async-start(bf16[8,4096,128]{2,1,0:T(8,128)(2,1)} %mail.1), calls=%async_computation.2 | async-start | bytes 16777216 | tf_op jit(solution)/shard_map/all_to_all | solution.py:478
  168.0 27.4 %collective-permute-done.3.refs_1_ = bf16[1040,512]{1,0:T(8,128)(2,1)S(1)} collective-permute-done((bf16[1040,512]{1,0:T(8,128)(2,1)}, bf16[1040,512]{1,0:T(8,128)(2,1)S(1)}, u32[]{:S(2)}, u32[]{:S(2)}) %collective-permute-start.3) | collective-permute-done | bytes 1064992 | tf_op jit(solution)/shard_map/ppermute | solution.py:474
  195.4 22.0 %collective-permute-done.4.refs_2_ = bf16[1040,512]{1,0:T(8,128)(2,1)S(1)} collective-permute-done((bf16[1040,512]{1,0:T(8,128)(2,1)}, bf16[1040,512]{1,0:T(8,128)(2,1)S(1)}, u32[]{:S(2)}, u32[]{:S(2)}) %collective-permute-start.4) | collective-permute-done | bytes 1064992 | tf_op jit(solution)/shard_map/ppermute | solution.py:474
  217.4 1.8 collective-permute-done.5.refs_3_
  219.2 0.7 slice_bitcast_fusion
  219.9 5.3 %sort.2 = (bf16[528,512]{1,0:T(8,128)(2,1)}, bf16[528,512]{1,0:T(8,128)(2,1)}, bf16[528,512]{1,0:T(8,128)(2,1)}, bf16[528,512]{1,0:T(8,128)(2,1)}) custom-call(s32[1]{0:T(128)} %bitcast.me_ref, s32[64]{0:T(128)S(1)} %get-tuple-element.56.slot_ref, f32[64]{0:T(128)S(1)} %convert_divide_fusion.1.weight_ref, bf16[16,512]{1,0:T(8,128)(2,1)S(1)} %fusion.18.note_ref, ...), custom_call_target="tpu_custom_call" | custom-call | tf_op jit(solution)/shard_map/sort/pallas_call | solution.py:236
  225.3 1.6 collective-permute-start.1
  226.9 1.9 collective-permute-start.2
  228.8 0.7 slice_bitcast_fusion.3
  229.8 8.3 %rows.3.refs_5_ = f32[5,8,64,2048]{3,2,1,0:T(8,128)} custom-call(bf16[1040,512]{1,0:T(8,128)(2,1)} %get-tuple-element.41.refs_0_, bf16[1040,512]{1,0:T(8,128)(2,1)} %copy-done.6, bf16[1040,512]{1,0:T(8,128)(2,1)} %copy-done.7, bf16[1040,512]{1,0:T(8,128)(2,1)} %collective-permute-done.5.refs_3_, bf16[4,2048,512]{2,1,0:T(8,128)(2,1)} %bitcast.32), custom_call_target="tpu_custom_call" | custom-call | flops 30000001024 | tf_op jit(solution)/shard_map/rows/pallas_call | solution.py:397
  238.1 8.3 %rows.4.refs_3_ = f32[5,8,64,2048]{3,2,1,0:T(8,128)} custom-call(bf16[1040,512]{1,0:T(8,128)(2,1)} %get-tuple-element.41.refs_0_, bf16[1040,512]{1,0:T(8,128)(2,1)} %copy-done.6, bf16[1040,512]{1,0:T(8,128)(2,1)} %copy-done.7, bf16[1040,512]{1,0:T(8,128)(2,1)} %collective-permute-done.5.refs_3_, ...), custom_call_target="tpu_custom_call", output_to_operand_aliasing={{}: (5, {})} | custom-call | flops 30000001024 | tf_op jit(solution)/shard_map/rows/pallas_call | solution.py:397
  246.4 0.9 convert_reduce_fusion
  247.4 1.3 select_reduce_fusion.refs_0_
  248.7 11.9 %all-to-all-done.2.refs_1_ = bf16[8,4096,128]{2,1,0:T(8,128)(2,1)} async-done(((bf16[8,4096,128]{2,1,0:T(8,128)(2,1)}), bf16[8,4096,128]{2,1,0:T(8,128)(2,1)}, u32[]{:S(2)}, u32[]{:S(2)}) %all-to-all-start.2) | async-done | bytes 8388640 | tf_op jit(solution)/shard_map/all_to_all | solution.py:478
  260.7 18.1 %box.1.refs_5_ = f32[5,8,64,2048]{3,2,1,0:T(8,128)} custom-call(s32[4,64]{1,0:T(4,128)S(1)} %select_reduce_fusion.refs_0_, bf16[8,4096,128]{2,1,0:T(8,128)(2,1)} %all-to-all-done.2.refs_1_, bf16[4,2048,512]{2,1,0:T(8,128)(2,1)} %bitcast.34, f32[5,8,64,2048]{3,2,1,0:T(8,128)} %rows.4.refs_3_), custom_call_target="tpu_custom_call", output_to_operand_aliasing={{}: (3, {})} | custom-call | tf_op jit(solution)/shard_map/box/pallas_call | solution.py:397
  278.9 0.8 copy-done.2
  279.6 0.2 copy-done.3
  279.8 0.8 copy-done.4
  280.6 8.3 %rows.5 = f32[5,8,64,2048]{3,2,1,0:T(8,128)} custom-call(bf16[528,512]{1,0:T(8,128)(2,1)} %get-tuple-element.36.refs_0_, bf16[528,512]{1,0:T(8,128)(2,1)} %copy-done.2, bf16[528,512]{1,0:T(8,128)(2,1)} %copy-done.3, bf16[528,512]{1,0:T(8,128)(2,1)} %copy-done.4, bf16[4,2048,512]{2,1,0:T(8,128)(2,1)} %bitcast.35, ...), custom_call_target="tpu_custom_call", output_to_operand_aliasing={{}: (5, {})} | custom-call | tf_op jit(solution)/shard_map/rows/pallas_call | solution.py:397
  (65 shorter events, 1.0 us)
Async XLA Ops:
  1.4 0.7 copy-start
  8.4 5.4 %copy-start.5 = (s32[64]{0:T(128)S(1)}, s32[64]{0:T(128)}, u32[]{:S(2)}) copy-start(s32[64]{0:T(128)} %param.6) | copy-start | bytes 772
  8.4 98.8 %all-to-all-start = ((bf16[8,2064,256]{2,1,0:T(8,128)(2,1)}), bf16[8,2064,256]{2,1,0:T(8,128)(2,1)}, u32[]{:S(2)}, u32[]{:S(2)}) async-start(bf16[8,2064,256]{2,1,0:T(8,128)(2,1)} %post.2), calls=%async_computation | async-start | bytes 16908288 | tf_op jit(solution)/shard_map/all_to_all | solution.py:478
  18.9 104.0 %collective-permute-start.6 = (bf16[4112,128]{1,0:T(8,128)(2,1)}, bf16[4112,128]{1,0:T(8,128)(2,1)S(1)}, u32[]{:S(2)}, u32[]{:S(2)}) collective-permute-start(bf16[4112,128]{1,0:T(8,128)(2,1)} %get-tuple-element.45), channel_id=1, source_target_pairs={{0,1},{1,2},{2,3},{3,0},{4,5},{5,6},{6,7},{7,4},{8,9},{9,10},{10,1... | collective-permute-start | bytes 3158024 | tf_op jit(solution)/shard_map/ppermute | solution.py:474
  20.6 102.4 %collective-permute-start.7 = (bf16[4112,128]{1,0:T(8,128)(2,1)}, bf16[4112,128]{1,0:T(8,128)(2,1)S(1)}, u32[]{:S(2)}, u32[]{:S(2)}) collective-permute-start(bf16[4112,128]{1,0:T(8,128)(2,1)} %get-tuple-element.46), channel_id=1, source_target_pairs={{0,2},{1,3},{2,0},{3,1},{4,6},{5,7},{6,4},{7,5},{8,10},{9,11},{10,... | collective-permute-start | bytes 3158024 | tf_op jit(solution)/shard_map/ppermute | solution.py:474
  21.7 101.3 %collective-permute-start.8 = (bf16[4112,128]{1,0:T(8,128)(2,1)}, bf16[4112,128]{1,0:T(8,128)(2,1)S(1)}, u32[]{:S(2)}, u32[]{:S(2)}) collective-permute-start(bf16[4112,128]{1,0:T(8,128)(2,1)} %get-tuple-element.47), channel_id=1, source_target_pairs={{0,3},{1,0},{2,1},{3,2},{4,7},{5,4},{6,5},{7,6},{8,11},{9,8},{10,9... | collective-permute-start | bytes 3158024 | tf_op jit(solution)/shard_map/ppermute | solution.py:474
  27.0 7.1 %copy-start.1 = (s32[64]{0:T(128)S(1)}, s32[64]{0:T(128)}, u32[]{:S(2)}) copy-start(s32[64]{0:T(128)} %dest_ref.3) | copy-start | bytes 772
  107.2 54.4 %all-to-all-start.1 = ((bf16[8,1040,256]{2,1,0:T(8,128)(2,1)}), bf16[8,1040,256]{2,1,0:T(8,128)(2,1)}, u32[]{:S(2)}, u32[]{:S(2)}) async-start(bf16[8,1040,256]{2,1,0:T(8,128)(2,1)} %post.3), calls=%async_computation.1 | async-start | bytes 8519680 | tf_op jit(solution)/shard_map/all_to_all | solution.py:478
  122.9 7.9 %copy-start.8 = (bf16[4112,128]{1,0:T(8,128)(2,1)}, bf16[4112,128]{1,0:T(8,128)(2,1)S(1)}, u32[]{:S(2)}) copy-start(bf16[4112,128]{1,0:T(8,128)(2,1)S(1)} %collective-permute-done.6.refs_1_) | copy-start | bytes 3158020
  123.0 1.0 copy-start.9
  123.0 2.6 copy-start.10
  124.0 71.4 %collective-permute-start.3 = (bf16[1040,512]{1,0:T(8,128)(2,1)}, bf16[1040,512]{1,0:T(8,128)(2,1)S(1)}, u32[]{:S(2)}, u32[]{:S(2)}) collective-permute-start(bf16[1040,512]{1,0:T(8,128)(2,1)} %get-tuple-element.42), channel_id=1, source_target_pairs={{0,1},{1,2},{2,3},{3,0},{4,5},{5,6},{6,7},{7,4},{8,9},{9,10},{10,1... | collective-permute-start | bytes 3194888 | tf_op jit(solution)/shard_map/ppermute | solution.py:474
  125.5 91.9 %collective-permute-start.4 = (bf16[1040,512]{1,0:T(8,128)(2,1)}, bf16[1040,512]{1,0:T(8,128)(2,1)S(1)}, u32[]{:S(2)}, u32[]{:S(2)}) collective-permute-start(bf16[1040,512]{1,0:T(8,128)(2,1)} %get-tuple-element.43), channel_id=1, source_target_pairs={{0,2},{1,3},{2,0},{3,1},{4,6},{5,7},{6,4},{7,5},{8,10},{9,11},{10,... | collective-permute-start | bytes 3194888 | tf_op jit(solution)/shard_map/ppermute | solution.py:474
  126.9 92.2 %collective-permute-start.5 = (bf16[1040,512]{1,0:T(8,128)(2,1)}, bf16[1040,512]{1,0:T(8,128)(2,1)}, u32[]{:S(2)}, u32[]{:S(2)}) collective-permute-start(bf16[1040,512]{1,0:T(8,128)(2,1)} %get-tuple-element.44), channel_id=1, source_target_pairs={{0,3},{1,0},{2,1},{3,2},{4,7},{5,4},{6,5},{7,6},{8,11},{9,8},{10,9... | collective-permute-start | bytes 3194888 | tf_op jit(solution)/shard_map/ppermute | solution.py:474
  161.6 99.0 %all-to-all-start.2 = ((bf16[8,4096,128]{2,1,0:T(8,128)(2,1)}), bf16[8,4096,128]{2,1,0:T(8,128)(2,1)}, u32[]{:S(2)}, u32[]{:S(2)}) async-start(bf16[8,4096,128]{2,1,0:T(8,128)(2,1)} %mail.1), calls=%async_computation.2 | async-start | bytes 16777216 | tf_op jit(solution)/shard_map/all_to_all | solution.py:478
  195.4 29.9 %copy-start.6 = (bf16[1040,512]{1,0:T(8,128)(2,1)}, bf16[1040,512]{1,0:T(8,128)(2,1)S(1)}, u32[]{:S(2)}) copy-start(bf16[1040,512]{1,0:T(8,128)(2,1)S(1)} %collective-permute-done.3.refs_1_) | copy-start | bytes 3194884
  217.4 7.8 %copy-start.7 = (bf16[1040,512]{1,0:T(8,128)(2,1)}, bf16[1040,512]{1,0:T(8,128)(2,1)S(1)}, u32[]{:S(2)}) copy-start(bf16[1040,512]{1,0:T(8,128)(2,1)S(1)} %collective-permute-done.4.refs_2_) | copy-start | bytes 3194884
  225.2 53.6 %collective-permute-start = (bf16[528,512]{1,0:T(8,128)(2,1)}, bf16[528,512]{1,0:T(8,128)(2,1)S(1)}, u32[]{:S(2)}, u32[]{:S(2)}) collective-permute-start(bf16[528,512]{1,0:T(8,128)(2,1)} %get-tuple-element.37), channel_id=1, source_target_pairs={{0,1},{1,2},{2,3},{3,0},{4,5},{5,6},{6,7},{7,4},{8,9},{9,10},{10,1... | collective-permute-start | bytes 1622024 | tf_op jit(solution)/shard_map/ppermute | solution.py:474
  225.3 53.5 %collective-permute-start.1 = (bf16[528,512]{1,0:T(8,128)(2,1)}, bf16[528,512]{1,0:T(8,128)(2,1)S(1)}, u32[]{:S(2)}, u32[]{:S(2)}) collective-permute-start(bf16[528,512]{1,0:T(8,128)(2,1)} %get-tuple-element.38), channel_id=1, source_target_pairs={{0,2},{1,3},{2,0},{3,1},{4,6},{5,7},{6,4},{7,5},{8,10},{9,11},{10,... | collective-permute-start | bytes 1622024 | tf_op jit(solution)/shard_map/ppermute | solution.py:474
  226.9 52.0 %collective-permute-start.2 = (bf16[528,512]{1,0:T(8,128)(2,1)}, bf16[528,512]{1,0:T(8,128)(2,1)S(1)}, u32[]{:S(2)}, u32[]{:S(2)}) collective-permute-start(bf16[528,512]{1,0:T(8,128)(2,1)} %get-tuple-element.39), channel_id=1, source_target_pairs={{0,3},{1,0},{2,1},{3,2},{4,7},{5,4},{6,5},{7,6},{8,11},{9,8},{10,9... | collective-permute-start | bytes 1622024 | tf_op jit(solution)/shard_map/ppermute | solution.py:474
  278.8 0.8 copy-start.2
  278.8 1.0 copy-start.3
  279.8 0.8 copy-start.4

commit v5 on v4

--- a/solution.py
+++ b/solution.py
@@ -417,7 +417,7 @@
 def transform_rows(slabs, take, basis, total, field, cost):
     planes = len(slabs)
     kernel = functools.partial(rows_kernel, planes, take, field, int(total is not None))
-    operands, specs = in_hbm(*slabs), [ANY] * planes
+    operands, specs = list(slabs), [ANY] * planes
     return transform(kernel, operands, specs, total, basis, planes, 1, [], planes, cost, "rows")
 
 
@@ -438,11 +438,15 @@
 
 def as_note(dest, place_level, width):
     count = dest.size
-    pad = -count % width
-    each = (count + pad) // width
-    codes = [jnp.pad(c.reshape(-1), (0, pad)).reshape(each, width) for c in (dest, place_level)]
-    both = jnp.concatenate(codes, axis=0)
-    return jnp.pad(both, ((0, NOTE - 2 * each), (0, 0))).astype(jnp.bfloat16)
+    each = -(-count // width)
+    row = jnp.arange(NOTE, dtype=jnp.int32)[:, None]
+    if each > 1:
+        codes = [c.reshape(-1) for c in (dest, place_level)]
+        codes = [jnp.pad(c, (0, each * width - count)).reshape(each, width) for c in codes]
+        both = jnp.concatenate(codes, axis=0)
+        return jnp.pad(both, ((0, NOTE - 2 * each), (0, 0))).astype(jnp.bfloat16)
+    wide = [jnp.pad(c.reshape(1, -1), ((0, 0), (0, width - count))) for c in (dest, place_level)]
+    return jnp.where(row == 0, wide[0], jnp.where(row == 1, wide[1], 0)).astype(jnp.bfloat16)
 
 
 def from_note(note, count):

time: 291 us -> 289 us (level)
  waiting for transfers between devices: 155 us -> 151 us
  local copies, waits for them, and re-layouts: 7.33 us -> 10.5 us
    all_to_all x3, waiting for transfers between devices: 104 us -> 99.6 us  [over_tile(): return lax.all_to_all(box, 'tile', split_axis=0, concat_axis=0, tiled=True)]
    unnamed x23 -> x30, local copies, waits for them, and re-layouts: 3.4 us -> 6.75 us
where the time goes in v5:
time: 289 us; the launch traced here: 287 us
  waiting for transfers between devices  151 us (52%)
  Pallas kernels  78.6 us (27%)
  starting transfers between devices  30.8 us (11%)
  other arithmetic  15.6 us (5%)
  local copies, waits for them, and re-layouts  10.5 us (4%)
    all_to_all x3, waiting for transfers between devices, over_tile(): return lax.all_to_all(box, 'tile', split_axis=0, concat_axis=0, tiled=True)  99.6 us
    ppermute x9, waiting for transfers between devices, over_phi(): moved.append(lax.ppermute(parts[d], 'phi', pairs))  51.5 us
    pallas_call x4, Pallas kernels, transform(): pl.pallas_call(kernel, in_specs=specs, out_specs=HBM, out_shape=pltpu.HBM...  42 us
    all_to_all x3, starting transfers between devices, over_tile(): return lax.all_to_all(box, 'tile', split_axis=0, concat_axis=0, tiled=True)  17.8 us
    pallas_call x2, Pallas kernels, sort(): pl.pallas_call(functools.partial(sort_kernel, planes, count, capacity), i...  13.1 us
    ppermute x9, starting transfers between devices, over_phi(): moved.append(lax.ppermute(parts[d], 'phi', pairs))  13 us
    pallas_call x2, Pallas kernels, post(): pl.pallas_call(functools.partial(post_kernel, fields, tiles, capacity), i...  10.7 us
    pallas_call x1, Pallas kernels, mail(): pl.pallas_call(functools.partial(mail_kernel, planes, tiles, capacity), i...  7.73 us
  transfers between devices with their start and end apart: 12, of which 6 were waited for; matrix products, arithmetic and copies ran while one was open for 6% of the time, Pallas kernels for 22%

profile of v5, /device:TPU:10, one launch (start us, length us, event | category | flops | bytes accessed | tf_op | source)
XLA Modules:
  0.0 287.0 jit_solution(3362387193788597089)
XLA Ops:
  0.0 0.7 add_bitcast_fusion
  0.7 0.7 pad.14
  1.4 0.7 copy-done.1
  2.1 6.3 %post.2 = bf16[8,2064,256]{2,1,0:T(8,128)(2,1)} custom-call(s32[64]{0:T(128)S(1)} %copy-done.1, bf16[16,256]{1,0:T(8,128)(2,1)S(1)} %select_convert_fusion.1.note_ref, bf16[64,5,64,256]{3,2,1,0:T(8,128)(2,1)} %x_ref.4), custom_call_target="tpu_custom_call" | custom-call | tf_op jit(solution)/shard_map/post/pallas_call | solution.py:170
  8.5 5.4 %all-to-all-start = ((bf16[8,2064,256]{2,1,0:T(8,128)(2,1)}), bf16[8,2064,256]{2,1,0:T(8,128)(2,1)}, u32[]{:S(2)}, u32[]{:S(2)}) async-start(bf16[8,2064,256]{2,1,0:T(8,128)(2,1)} %post.2), calls=%async_computation | async-start | bytes 16908288 | tf_op jit(solution)/shard_map/all_to_all | solution.py:482
  14.0 5.0 %cut.1 = (bf16[4112,128]{1,0:T(8,128)(2,1)}, bf16[4112,128]{1,0:T(8,128)(2,1)}, bf16[4112,128]{1,0:T(8,128)(2,1)}, bf16[4112,128]{1,0:T(8,128)(2,1)}) custom-call(s32[1]{0:T(128)} %bitcast.me_ref, f32[64]{0:T(128)S(1)} %convert_divide_fusion.weight_ref, bf16[16,128]{1,0:T(8,128)(2,1)S(1)} %select_convert_fusion.2.note_ref, bf16[64,5,64,256]{3,2,1,0:T(8,128)(2,1)} %x_ref.4), custom_call_target="tpu_custom_call" | custom-call | tf_op jit(solution)/shard_map/cut/pallas_call | solution.py:116
  19.0 1.6 collective-permute-start.6
  20.7 1.1 collective-permute-start.7
  21.7 1.9 collective-permute-start.8
  23.9 1.1 select_multiply_fusion
  25.0 2.0 fusion.10
  27.1 7.0 %add_convert_fusion = bf16[4,32,64,512]{3,2,1,0:T(8,128)(2,1)} fusion(f32[4,64,512]{2,1,0:T(8,128)S(1)} %bitcast.45, f32[4,32,512]{2,1,0:T(8,128)S(1)} %bitcast.47, f32[4,64,512]{2,1,0:T(8,128)S(1)} %bitcast.46, f32[4,32,512]{2,1,0:T(8,128)S(1)} %bitcast.48), kind=kLoop, calls=%fused_computation | loop fusion | flops 16777216 | bytes 9961472 | tf_op jit(solution)/shard_map/convert_element_type | solution.py:59
  34.2 4.4 %post.3 = bf16[8,1040,256]{2,1,0:T(8,128)(2,1)} custom-call(s32[64]{0:T(128)S(1)} %copy-done.2, bf16[16,256]{1,0:T(8,128)(2,1)S(1)} %select_convert_fusion.1.note_ref, bf16[64,5,64,256]{3,2,1,0:T(8,128)(2,1)} %x_ref.4), custom_call_target="tpu_custom_call" | custom-call | flops 30000001024 | tf_op jit(solution)/shard_map/post/pallas_call | solution.py:170
  38.6 68.7 %all-to-all-done.x_ref = bf16[8,2064,256]{2,1,0:T(8,128)(2,1)} async-done(((bf16[8,2064,256]{2,1,0:T(8,128)(2,1)}), bf16[8,2064,256]{2,1,0:T(8,128)(2,1)}, u32[]{:S(2)}, u32[]{:S(2)}) %all-to-all-start) | async-done | bytes 8454176 | tf_op jit(solution)/shard_map/all_to_all | solution.py:482
  107.2 6.0 %all-to-all-start.1 = ((bf16[8,1040,256]{2,1,0:T(8,128)(2,1)}), bf16[8,1040,256]{2,1,0:T(8,128)(2,1)}, u32[]{:S(2)}, u32[]{:S(2)}) async-start(bf16[8,1040,256]{2,1,0:T(8,128)(2,1)} %post.3), calls=%async_computation.1 | async-start | bytes 8519680 | tf_op jit(solution)/shard_map/all_to_all | solution.py:482
  113.3 0.9 convert_convert_fusion
  114.2 0.3 convert_reduce_fusion.1
  114.6 0.4 select_reduce_fusion.1
  115.2 7.8 %sort.3 = (bf16[1040,512]{1,0:T(8,128)(2,1)}, bf16[1040,512]{1,0:T(8,128)(2,1)}, bf16[1040,512]{1,0:T(8,128)(2,1)}, bf16[1040,512]{1,0:T(8,128)(2,1)}) custom-call(s32[1]{0:T(128)} %bitcast.me_ref, s32[64]{0:T(128)S(1)} %get-tuple-element.56.slot_ref, f32[64]{0:T(128)S(1)} %convert_divide_fusion.1.weight_ref, ...), custom_call_target="tpu_custom_call" | custom-call | tf_op jit(solution)/shard_map/sort/pallas_call | solution.py:236
  123.0 1.0 copy-done.11
  124.0 0.3 copy-done.12
  124.4 1.6 collective-permute-start.3
  125.9 1.4 collective-permute-start.4
  127.3 1.6 collective-permute-start.5
  129.0 0.7 slice_bitcast_fusion.7
  129.7 0.7 slice_bitcast_fusion.6
  130.3 0.7 slice_bitcast_fusion.5
  131.0 0.7 slice_bitcast_fusion.4
  131.9 7.7 %mail.1 = bf16[8,4096,128]{2,1,0:T(8,128)(2,1)} custom-call(s32[4,64]{1,0:T(4,128)S(1)} %multiply_add_fusion.1.slot_ref, bf16[4112,128]{1,0:T(8,128)(2,1)} %get-tuple-element.48.refs_0_, bf16[4112,128]{1,0:T(8,128)(2,1)} %copy-done.11, bf16[4112,128]{1,0:T(8,128)(2,1)} %copy-done.12, bf16[4112,128]{1,0:T(8,128)(2,1)} %copy-done.13), custom_call_target="tpu_custom_call" | custom-call | flops 20000000000 | tf_op jit(solution)/shard_map/mail/pallas_call | solution.py:281
  139.7 22.0 %all-to-all-done.1.x_ref = bf16[8,1040,256]{2,1,0:T(8,128)(2,1)} async-done(((bf16[8,1040,256]{2,1,0:T(8,128)(2,1)}), bf16[8,1040,256]{2,1,0:T(8,128)(2,1)}, u32[]{:S(2)}, u32[]{:S(2)}) %all-to-all-start.1) | async-done | bytes 4259872 | tf_op jit(solution)/shard_map/all_to_all | solution.py:482
  161.7 6.4 %all-to-all-start.2 = ((bf16[8,4096,128]{2,1,0:T(8,128)(2,1)}), bf16[8,4096,128]{2,1,0:T(8,128)(2,1)}, u32[]{:S(2)}, u32[]{:S(2)}) async-start(bf16[8,4096,128]{2,1,0:T(8,128)(2,1)} %mail.1), calls=%async_computation.2 | async-start | bytes 16777216 | tf_op jit(solution)/shard_map/all_to_all | solution.py:482
  168.0 27.7 %collective-permute-done.3.refs_1_ = bf16[1040,512]{1,0:T(8,128)(2,1)S(1)} collective-permute-done((bf16[1040,512]{1,0:T(8,128)(2,1)}, bf16[1040,512]{1,0:T(8,128)(2,1)S(1)}, u32[]{:S(2)}, u32[]{:S(2)}) %collective-permute-start.3) | collective-permute-done | bytes 1064992 | tf_op jit(solution)/shard_map/ppermute | solution.py:478
  195.8 22.0 %collective-permute-done.4.refs_2_ = bf16[1040,512]{1,0:T(8,128)(2,1)S(1)} collective-permute-done((bf16[1040,512]{1,0:T(8,128)(2,1)}, bf16[1040,512]{1,0:T(8,128)(2,1)S(1)}, u32[]{:S(2)}, u32[]{:S(2)}) %collective-permute-start.4) | collective-permute-done | bytes 1064992 | tf_op jit(solution)/shard_map/ppermute | solution.py:478
  217.8 1.7 collective-permute-done.5.refs_3_
  219.5 1.0 copy-done.8
  220.5 5.3 %sort.2 = (bf16[528,512]{1,0:T(8,128)(2,1)}, bf16[528,512]{1,0:T(8,128)(2,1)}, bf16[528,512]{1,0:T(8,128)(2,1)}, bf16[528,512]{1,0:T(8,128)(2,1)}) custom-call(s32[1]{0:T(128)} %bitcast.me_ref, s32[64]{0:T(128)S(1)} %get-tuple-element.56.slot_ref, f32[64]{0:T(128)S(1)} %convert_divide_fusion.1.weight_ref, bf16[16,512]{1,0:T(8,128)(2,1)S(1)} %select_convert_fusion.note_ref, ...), custom_call_target="tpu_custom_call" | custom-call | tf_op jit(solution)/shard_map/sort/pallas_call | solution.py:236
  225.9 1.7 collective-permute-start.1
  227.7 1.9 collective-permute-start.2
  229.9 1.2 copy-done.5
  231.1 1.2 copy-done.7
  232.3 1.2 copy-done.9
  233.5 8.0 %rows.3.refs_5_ = f32[5,8,64,2048]{3,2,1,0:T(8,128)} custom-call(bf16[1040,512]{1,0:T(8,128)(2,1)S(1)} %copy-done.3, bf16[1040,512]{1,0:T(8,128)(2,1)S(1)} %copy-done.5, bf16[1040,512]{1,0:T(8,128)(2,1)S(1)} %copy-done.7, bf16[1040,512]{1,0:T(8,128)(2,1)S(1)} %copy-done.9, bf16[4,2048,512]{2,1,0:T(8,128)(2,1)} %bitcast.41), custom_call_target="tpu_custom_call" | custom-call | flops 30000001024 | tf_op jit(solution)/shard_map/rows/pallas_call | solution.py:397
  241.5 8.0 %rows.4.refs_3_ = f32[5,8,64,2048]{3,2,1,0:T(8,128)} custom-call(bf16[1040,512]{1,0:T(8,128)(2,1)S(1)} %copy-done.3, bf16[1040,512]{1,0:T(8,128)(2,1)S(1)} %copy-done.5, bf16[1040,512]{1,0:T(8,128)(2,1)S(1)} %copy-done.7, bf16[1040,512]{1,0:T(8,128)(2,1)S(1)} %copy-done.9, bf16[4,2048,512]{2,1,0:T(8,128)(2,1)} %bitcast.42, ...), custom_call_target="tpu_custom_call", output_to_operand_aliasing={{}: (5, {})} | custom-call | flops 30000001024 | tf_op jit(solution)/shard_map/rows/pallas_call | solution.py:397
  249.5 0.9 convert_reduce_fusion
  250.5 1.4 select_reduce_fusion.refs_0_
  251.8 8.9 %all-to-all-done.2.refs_1_ = bf16[8,4096,128]{2,1,0:T(8,128)(2,1)} async-done(((bf16[8,4096,128]{2,1,0:T(8,128)(2,1)}), bf16[8,4096,128]{2,1,0:T(8,128)(2,1)}, u32[]{:S(2)}, u32[]{:S(2)}) %all-to-all-start.2) | async-done | bytes 8388640 | tf_op jit(solution)/shard_map/all_to_all | solution.py:482
  260.7 18.1 %box.1.refs_5_ = f32[5,8,64,2048]{3,2,1,0:T(8,128)} custom-call(s32[4,64]{1,0:T(4,128)S(1)} %select_reduce_fusion.refs_0_, bf16[8,4096,128]{2,1,0:T(8,128)(2,1)} %all-to-all-done.2.refs_1_, bf16[4,2048,512]{2,1,0:T(8,128)(2,1)} %bitcast.43, f32[5,8,64,2048]{3,2,1,0:T(8,128)} %rows.4.refs_3_), custom_call_target="tpu_custom_call", output_to_operand_aliasing={{}: (3, {})} | custom-call | tf_op jit(solution)/shard_map/box/pallas_call | solution.py:397
  278.9 8.0 %rows.5 = f32[5,8,64,2048]{3,2,1,0:T(8,128)} custom-call(bf16[528,512]{1,0:T(8,128)(2,1)S(1)} %copy-done, bf16[528,512]{1,0:T(8,128)(2,1)S(1)} %collective-permute-done.refs_1_, bf16[528,512]{1,0:T(8,128)(2,1)S(1)} %collective-permute-done.1.refs_2_, bf16[528,512]{1,0:T(8,128)(2,1)S(1)} %collective-permute-done.2.refs_3_, ...), custom_call_target="tpu_custom_call", output_to_operand_aliasing={{}: (5, {})} | custom-call | tf_op jit(solution)/shard_map/rows/pallas_call | solution.py:397
  (69 shorter events, 1.4 us)
Async XLA Ops:
  1.4 0.7 copy-start.1
  8.5 5.4 %copy-start.2 = (s32[64]{0:T(128)S(1)}, s32[64]{0:T(128)}, u32[]{:S(2)}) copy-start(s32[64]{0:T(128)} %dest_ref.3) | copy-start | bytes 772
  8.5 5.4 %copy-start.10 = (s32[64]{0:T(128)S(1)}, s32[64]{0:T(128)}, u32[]{:S(2)}) copy-start(s32[64]{0:T(128)} %param.6) | copy-start | bytes 772
  8.5 98.8 %all-to-all-start = ((bf16[8,2064,256]{2,1,0:T(8,128)(2,1)}), bf16[8,2064,256]{2,1,0:T(8,128)(2,1)}, u32[]{:S(2)}, u32[]{:S(2)}) async-start(bf16[8,2064,256]{2,1,0:T(8,128)(2,1)} %post.2), calls=%async_computation | async-start | bytes 16908288 | tf_op jit(solution)/shard_map/all_to_all | solution.py:482
  19.0 104.0 %collective-permute-start.6 = (bf16[4112,128]{1,0:T(8,128)(2,1)}, bf16[4112,128]{1,0:T(8,128)(2,1)S(1)}, u32[]{:S(2)}, u32[]{:S(2)}) collective-permute-start(bf16[4112,128]{1,0:T(8,128)(2,1)} %get-tuple-element.45), channel_id=1, source_target_pairs={{0,1},{1,2},{2,3},{3,0},{4,5},{5,6},{6,7},{7,4},{8,9},{9,10},{10,1... | collective-permute-start | bytes 3158024 | tf_op jit(solution)/shard_map/ppermute | solution.py:478
  20.7 102.4 %collective-permute-start.7 = (bf16[4112,128]{1,0:T(8,128)(2,1)}, bf16[4112,128]{1,0:T(8,128)(2,1)S(1)}, u32[]{:S(2)}, u32[]{:S(2)}) collective-permute-start(bf16[4112,128]{1,0:T(8,128)(2,1)} %get-tuple-element.46), channel_id=1, source_target_pairs={{0,2},{1,3},{2,0},{3,1},{4,6},{5,7},{6,4},{7,5},{8,10},{9,11},{10,... | collective-permute-start | bytes 3158024 | tf_op jit(solution)/shard_map/ppermute | solution.py:478
  21.7 101.3 %collective-permute-start.8 = (bf16[4112,128]{1,0:T(8,128)(2,1)}, bf16[4112,128]{1,0:T(8,128)(2,1)S(1)}, u32[]{:S(2)}, u32[]{:S(2)}) collective-permute-start(bf16[4112,128]{1,0:T(8,128)(2,1)} %get-tuple-element.47), channel_id=1, source_target_pairs={{0,3},{1,0},{2,1},{3,2},{4,7},{5,4},{6,5},{7,6},{8,11},{9,8},{10,9... | collective-permute-start | bytes 3158024 | tf_op jit(solution)/shard_map/ppermute | solution.py:478
  107.2 54.5 %all-to-all-start.1 = ((bf16[8,1040,256]{2,1,0:T(8,128)(2,1)}), bf16[8,1040,256]{2,1,0:T(8,128)(2,1)}, u32[]{:S(2)}, u32[]{:S(2)}) async-start(bf16[8,1040,256]{2,1,0:T(8,128)(2,1)} %post.3), calls=%async_computation.1 | async-start | bytes 8519680 | tf_op jit(solution)/shard_map/all_to_all | solution.py:482
  123.0 1.0 copy-start.11
  123.0 1.3 copy-start.12
  123.0 2.9 %copy-start.13 = (bf16[4112,128]{1,0:T(8,128)(2,1)}, bf16[4112,128]{1,0:T(8,128)(2,1)S(1)}, u32[]{:S(2)}) copy-start(bf16[4112,128]{1,0:T(8,128)(2,1)S(1)} %collective-permute-done.8.refs_3_) | copy-start | bytes 3158020
  124.4 71.4 %collective-permute-start.3 = (bf16[1040,512]{1,0:T(8,128)(2,1)}, bf16[1040,512]{1,0:T(8,128)(2,1)S(1)}, u32[]{:S(2)}, u32[]{:S(2)}) collective-permute-start(bf16[1040,512]{1,0:T(8,128)(2,1)} %get-tuple-element.42), channel_id=1, source_target_pairs={{0,1},{1,2},{2,3},{3,0},{4,5},{5,6},{6,7},{7,4},{8,9},{9,10},{10,1... | collective-permute-start | bytes 3194888 | tf_op jit(solution)/shard_map/ppermute | solution.py:478
  125.9 91.9 %collective-permute-start.4 = (bf16[1040,512]{1,0:T(8,128)(2,1)}, bf16[1040,512]{1,0:T(8,128)(2,1)S(1)}, u32[]{:S(2)}, u32[]{:S(2)}) collective-permute-start(bf16[1040,512]{1,0:T(8,128)(2,1)} %get-tuple-element.43), channel_id=1, source_target_pairs={{0,2},{1,3},{2,0},{3,1},{4,6},{5,7},{6,4},{7,5},{8,10},{9,11},{10,... | collective-permute-start | bytes 3194888 | tf_op jit(solution)/shard_map/ppermute | solution.py:478
  127.3 92.2 %collective-permute-start.5 = (bf16[1040,512]{1,0:T(8,128)(2,1)}, bf16[1040,512]{1,0:T(8,128)(2,1)S(1)}, u32[]{:S(2)}, u32[]{:S(2)}) collective-permute-start(bf16[1040,512]{1,0:T(8,128)(2,1)} %get-tuple-element.44), channel_id=1, source_target_pairs={{0,3},{1,0},{2,1},{3,2},{4,7},{5,4},{6,5},{7,6},{8,11},{9,8},{10,9... | collective-permute-start | bytes 3194888 | tf_op jit(solution)/shard_map/ppermute | solution.py:478
  161.7 99.0 %all-to-all-start.2 = ((bf16[8,4096,128]{2,1,0:T(8,128)(2,1)}), bf16[8,4096,128]{2,1,0:T(8,128)(2,1)}, u32[]{:S(2)}, u32[]{:S(2)}) async-start(bf16[8,4096,128]{2,1,0:T(8,128)(2,1)} %mail.1), calls=%async_computation.2 | async-start | bytes 16777216 | tf_op jit(solution)/shard_map/all_to_all | solution.py:482
  195.8 30.1 %copy-start.4 = (bf16[1040,512]{1,0:T(8,128)(2,1)}, bf16[1040,512]{1,0:T(8,128)(2,1)S(1)}, u32[]{:S(2)}) copy-start(bf16[1040,512]{1,0:T(8,128)(2,1)S(1)} %collective-permute-done.3.refs_1_) | copy-start | bytes 3194884
  217.8 8.1 %copy-start.6 = (bf16[1040,512]{1,0:T(8,128)(2,1)}, bf16[1040,512]{1,0:T(8,128)(2,1)S(1)}, u32[]{:S(2)}) copy-start(bf16[1040,512]{1,0:T(8,128)(2,1)S(1)} %collective-permute-done.4.refs_2_) | copy-start | bytes 3194884
  219.5 1.0 copy-start.8
  220.5 9.1 %copy-start.3 = (bf16[1040,512]{1,0:T(8,128)(2,1)S(1)}, bf16[1040,512]{1,0:T(8,128)(2,1)}, u32[]{:S(2)}) copy-start(bf16[1040,512]{1,0:T(8,128)(2,1)} %get-tuple-element.41.refs_0_) | copy-start | bytes 3194884
  225.9 53.0 %collective-permute-start = (bf16[528,512]{1,0:T(8,128)(2,1)}, bf16[528,512]{1,0:T(8,128)(2,1)S(1)}, u32[]{:S(2)}, u32[]{:S(2)}) collective-permute-start(bf16[528,512]{1,0:T(8,128)(2,1)} %get-tuple-element.37), channel_id=1, source_target_pairs={{0,1},{1,2},{2,3},{3,0},{4,5},{5,6},{6,7},{7,4},{8,9},{9,10},{10,1... | collective-permute-start | bytes 1622024 | tf_op jit(solution)/shard_map/ppermute | solution.py:478
  225.9 52.9 %collective-permute-start.1 = (bf16[528,512]{1,0:T(8,128)(2,1)}, bf16[528,512]{1,0:T(8,128)(2,1)S(1)}, u32[]{:S(2)}, u32[]{:S(2)}) collective-permute-start(bf16[528,512]{1,0:T(8,128)(2,1)} %get-tuple-element.38), channel_id=1, source_target_pairs={{0,2},{1,3},{2,0},{3,1},{4,6},{5,7},{6,4},{7,5},{8,10},{9,11},{10,... | collective-permute-start | bytes 1622024 | tf_op jit(solution)/shard_map/ppermute | solution.py:478
  227.7 51.2 %collective-permute-start.2 = (bf16[528,512]{1,0:T(8,128)(2,1)}, bf16[528,512]{1,0:T(8,128)(2,1)S(1)}, u32[]{:S(2)}, u32[]{:S(2)}) collective-permute-start(bf16[528,512]{1,0:T(8,128)(2,1)} %get-tuple-element.39), channel_id=1, source_target_pairs={{0,3},{1,0},{2,1},{3,2},{4,7},{5,4},{6,5},{7,6},{8,11},{9,8},{10,9... | collective-permute-start | bytes 1622024 | tf_op jit(solution)/shard_map/ppermute | solution.py:478
  229.8 1.2 copy-start.5
  231.1 1.2 copy-start.7
  232.3 1.2 copy-start.9
  251.8 27.1 %copy-start = (bf16[528,512]{1,0:T(8,128)(2,1)S(1)}, bf16[528,512]{1,0:T(8,128)(2,1)}, u32[]{:S(2)}) copy-start(bf16[528,512]{1,0:T(8,128)(2,1)} %get-tuple-element.36.refs_0_) | copy-start | bytes 1622020

commit v6 on v5

--- a/solution.py
+++ b/solution.py
@@ -158,10 +158,27 @@
             return carry
 
         lax.fori_loop(k * some, (k + 1) * some, body, 0)
-    for t in range(tiles):
-        pltpu.make_async_copy(box_ref.at[t], out_ref.at[t], out_sems.at[t]).start()
-    for t in range(tiles):
-        pltpu.make_async_copy(box_ref.at[t], out_ref.at[t], out_sems.at[t]).wait()
+    half = capacity // 2 * rows
+
+    def leave(t, k, at, size):
+        span = pl.ds(at, size)
+        return pltpu.make_async_copy(box_ref.at[t, span], out_ref.at[t, span], out_sems.at[t, k])
+
+    def upper(t, act):
+        @pl.when(filled[t] > capacity // 2)
+        def _():
+            act(leave(t, 1, half, half + NOTE))
+
+        @pl.when(filled[t] <= capacity // 2)
+        def _():
+            act(leave(t, 2, capacity * rows, NOTE))
+
+    for t in range(tiles):
+        leave(t, 0, 0, half).start()
+        upper(t, lambda copy: copy.start())
+    for t in range(tiles):
+        leave(t, 0, 0, half).wait()
+        upper(t, lambda copy: copy.wait())
 
 
 def post(blocks, dest, note, fields, tiles, capacity, cost):
@@ -177,7 +194,7 @@
             pltpu.VMEM((slots, len(fields), BPHI, COLS), jnp.bfloat16),
             pltpu.SMEM((tiles,), jnp.int32),
             pltpu.SemaphoreType.DMA((4,)),
-            pltpu.SemaphoreType.DMA((tiles,)),
+            pltpu.SemaphoreType.DMA((tiles, 3)),
         ],
         compiler_params=params(),
         cost_estimate=cost,
@@ -308,10 +325,10 @@
             n = len(copies)
             if f == 0:
                 pltpu.make_async_copy(basis.at[j], basis.at[j], basis_sems.at[j]).wait()
+            if n >= 2:
+                copies[n - 2].wait()
             if beside is not None:
                 beside(n)
-            if n >= 2:
-                copies[n - 2].wait()
             acc[n % 2] = jnp.dot(
                 rows[f][...], basis[j], preferred_element_type=jnp.float32
             ).reshape(acc.shape[1:])

time: 289 us -> 288 us (level)
  no operation moved by 1% of the time
where the time goes in v6:
time: 288 us; the launch traced here: 286 us
  waiting for transfers between devices  151 us (52%)
  Pallas kernels  77.4 us (27%)
  starting transfers between devices  30.6 us (11%)
  other arithmetic  15.6 us (5%)
  local copies, waits for them, and re-layouts  10.5 us (4%)
    all_to_all x3, waiting for transfers between devices, over_tile(): return lax.all_to_all(box, 'tile', split_axis=0, concat_axis=0, tiled=True)  100 us
    ppermute x9, waiting for transfers between devices, over_phi(): moved.append(lax.ppermute(parts[d], 'phi', pairs))  51.3 us
    pallas_call x4, Pallas kernels, transform(): pl.pallas_call(kernel, in_specs=specs, out_specs=HBM, out_shape=pltpu.HBM...  41.5 us
    all_to_all x3, starting transfers between devices, over_tile(): return lax.all_to_all(box, 'tile', split_axis=0, concat_axis=0, tiled=True)  17.8 us
    pallas_call x2, Pallas kernels, sort(): pl.pallas_call(functools.partial(sort_kernel, planes, count, capacity), i...  13.1 us
    ppermute x9, starting transfers between devices, over_phi(): moved.append(lax.ppermute(parts[d], 'phi', pairs))  12.8 us
    pallas_call x2, Pallas kernels, post(): pl.pallas_call(functools.partial(post_kernel, fields, tiles, capacity), i...  10.1 us
    pallas_call x1, Pallas kernels, mail(): pl.pallas_call(functools.partial(mail_kernel, planes, tiles, capacity), i...  7.73 us
  transfers between devices with their start and end apart: 12, of which 6 were waited for; matrix products, arithmetic and copies ran while one was open for 6% of the time, Pallas kernels for 22%

profile of v6, /device:TPU:10, one launch (start us, length us, event | category | flops | bytes accessed | tf_op | source)
XLA Modules:
  0.0 286.0 jit_solution(14845654014024353300)
XLA Ops:
  0.0 0.7 add_bitcast_fusion
  0.7 0.7 pad.14
  1.4 0.7 copy-done.1
  2.1 5.8 %post.2 = bf16[8,2064,256]{2,1,0:T(8,128)(2,1)} custom-call(s32[64]{0:T(128)S(1)} %copy-done.1, bf16[16,256]{1,0:T(8,128)(2,1)S(1)} %select_convert_fusion.1.note_ref, bf16[64,5,64,256]{3,2,1,0:T(8,128)(2,1)} %x_ref.4), custom_call_target="tpu_custom_call" | custom-call | tf_op jit(solution)/shard_map/post/pallas_call | solution.py:187
  8.0 5.4 %all-to-all-start = ((bf16[8,2064,256]{2,1,0:T(8,128)(2,1)}), bf16[8,2064,256]{2,1,0:T(8,128)(2,1)}, u32[]{:S(2)}, u32[]{:S(2)}) async-start(bf16[8,2064,256]{2,1,0:T(8,128)(2,1)} %post.2), calls=%async_computation | async-start | bytes 16908288 | tf_op jit(solution)/shard_map/all_to_all | solution.py:499
  13.5 5.0 %cut.1 = (bf16[4112,128]{1,0:T(8,128)(2,1)}, bf16[4112,128]{1,0:T(8,128)(2,1)}, bf16[4112,128]{1,0:T(8,128)(2,1)}, bf16[4112,128]{1,0:T(8,128)(2,1)}) custom-call(s32[1]{0:T(128)} %bitcast.me_ref, f32[64]{0:T(128)S(1)} %convert_divide_fusion.weight_ref, bf16[16,128]{1,0:T(8,128)(2,1)S(1)} %select_convert_fusion.2.note_ref, bf16[64,5,64,256]{3,2,1,0:T(8,128)(2,1)} %x_ref.4), custom_call_target="tpu_custom_call" | custom-call | tf_op jit(solution)/shard_map/cut/pallas_call | solution.py:116
  18.5 1.6 collective-permute-start.6
  20.1 0.9 collective-permute-start.7
  21.1 1.9 collective-permute-start.8
  23.2 1.1 select_multiply_fusion
  24.4 2.0 fusion.10
  26.5 7.0 %add_convert_fusion = bf16[4,32,64,512]{3,2,1,0:T(8,128)(2,1)} fusion(f32[4,64,512]{2,1,0:T(8,128)S(1)} %bitcast.45, f32[4,32,512]{2,1,0:T(8,128)S(1)} %bitcast.47, f32[4,64,512]{2,1,0:T(8,128)S(1)} %bitcast.46, f32[4,32,512]{2,1,0:T(8,128)S(1)} %bitcast.48), kind=kLoop, calls=%fused_computation | loop fusion | flops 16777216 | bytes 9961472 | tf_op jit(solution)/shard_map/convert_element_type | solution.py:59
  33.5 4.2 %post.3 = bf16[8,1040,256]{2,1,0:T(8,128)(2,1)} custom-call(s32[64]{0:T(128)S(1)} %copy-done.2, bf16[16,256]{1,0:T(8,128)(2,1)S(1)} %select_convert_fusion.1.note_ref, bf16[64,5,64,256]{3,2,1,0:T(8,128)(2,1)} %x_ref.4), custom_call_target="tpu_custom_call" | custom-call | flops 30000001024 | tf_op jit(solution)/shard_map/post/pallas_call | solution.py:187
  37.8 69.0 %all-to-all-done.x_ref = bf16[8,2064,256]{2,1,0:T(8,128)(2,1)} async-done(((bf16[8,2064,256]{2,1,0:T(8,128)(2,1)}), bf16[8,2064,256]{2,1,0:T(8,128)(2,1)}, u32[]{:S(2)}, u32[]{:S(2)}) %all-to-all-start) | async-done | bytes 8454176 | tf_op jit(solution)/shard_map/all_to_all | solution.py:499
  106.7 6.0 %all-to-all-start.1 = ((bf16[8,1040,256]{2,1,0:T(8,128)(2,1)}), bf16[8,1040,256]{2,1,0:T(8,128)(2,1)}, u32[]{:S(2)}, u32[]{:S(2)}) async-start(bf16[8,1040,256]{2,1,0:T(8,128)(2,1)} %post.3), calls=%async_computation.1 | async-start | bytes 8519680 | tf_op jit(solution)/shard_map/all_to_all | solution.py:499
  112.8 0.9 convert_convert_fusion
  113.7 0.3 convert_reduce_fusion.1
  114.1 0.4 select_reduce_fusion.1
  114.7 7.8 %sort.3 = (bf16[1040,512]{1,0:T(8,128)(2,1)}, bf16[1040,512]{1,0:T(8,128)(2,1)}, bf16[1040,512]{1,0:T(8,128)(2,1)}, bf16[1040,512]{1,0:T(8,128)(2,1)}) custom-call(s32[1]{0:T(128)} %bitcast.me_ref, s32[64]{0:T(128)S(1)} %get-tuple-element.56.slot_ref, f32[64]{0:T(128)S(1)} %convert_divide_fusion.1.weight_ref, ...), custom_call_target="tpu_custom_call" | custom-call | tf_op jit(solution)/shard_map/sort/pallas_call | solution.py:253
  122.5 1.0 copy-done.11
  123.5 0.3 copy-done.12
  123.9 1.6 collective-permute-start.3
  125.4 1.2 collective-permute-start.4
  126.7 1.6 collective-permute-start.5
  128.3 0.7 slice_bitcast_fusion.7
  129.0 0.7 slice_bitcast_fusion.6
  129.7 0.7 slice_bitcast_fusion.5
  130.3 0.7 slice_bitcast_fusion.4
  131.3 7.7 %mail.1 = bf16[8,4096,128]{2,1,0:T(8,128)(2,1)} custom-call(s32[4,64]{1,0:T(4,128)S(1)} %multiply_add_fusion.1.slot_ref, bf16[4112,128]{1,0:T(8,128)(2,1)} %get-tuple-element.48.refs_0_, bf16[4112,128]{1,0:T(8,128)(2,1)} %copy-done.11, bf16[4112,128]{1,0:T(8,128)(2,1)} %copy-done.12, bf16[4112,128]{1,0:T(8,128)(2,1)} %copy-done.13), custom_call_target="tpu_custom_call" | custom-call | flops 20000000000 | tf_op jit(solution)/shard_map/mail/pallas_call | solution.py:298
  139.0 22.2 %all-to-all-done.1.x_ref = bf16[8,1040,256]{2,1,0:T(8,128)(2,1)} async-done(((bf16[8,1040,256]{2,1,0:T(8,128)(2,1)}), bf16[8,1040,256]{2,1,0:T(8,128)(2,1)}, u32[]{:S(2)}, u32[]{:S(2)}) %all-to-all-start.1) | async-done | bytes 4259872 | tf_op jit(solution)/shard_map/all_to_all | solution.py:499
  161.2 6.4 %all-to-all-start.2 = ((bf16[8,4096,128]{2,1,0:T(8,128)(2,1)}), bf16[8,4096,128]{2,1,0:T(8,128)(2,1)}, u32[]{:S(2)}, u32[]{:S(2)}) async-start(bf16[8,4096,128]{2,1,0:T(8,128)(2,1)} %mail.1), calls=%async_computation.2 | async-start | bytes 16777216 | tf_op jit(solution)/shard_map/all_to_all | solution.py:499
  167.5 27.7 %collective-permute-done.3.refs_1_ = bf16[1040,512]{1,0:T(8,128)(2,1)S(1)} collective-permute-done((bf16[1040,512]{1,0:T(8,128)(2,1)}, bf16[1040,512]{1,0:T(8,128)(2,1)S(1)}, u32[]{:S(2)}, u32[]{:S(2)}) %collective-permute-start.3) | collective-permute-done | bytes 1064992 | tf_op jit(solution)/shard_map/ppermute | solution.py:495
  195.3 22.0 %collective-permute-done.4.refs_2_ = bf16[1040,512]{1,0:T(8,128)(2,1)S(1)} collective-permute-done((bf16[1040,512]{1,0:T(8,128)(2,1)}, bf16[1040,512]{1,0:T(8,128)(2,1)S(1)}, u32[]{:S(2)}, u32[]{:S(2)}) %collective-permute-start.4) | collective-permute-done | bytes 1064992 | tf_op jit(solution)/shard_map/ppermute | solution.py:495
  217.3 1.5 collective-permute-done.5.refs_3_
  218.8 1.0 copy-done.8
  219.9 5.3 %sort.2 = (bf16[528,512]{1,0:T(8,128)(2,1)}, bf16[528,512]{1,0:T(8,128)(2,1)}, bf16[528,512]{1,0:T(8,128)(2,1)}, bf16[528,512]{1,0:T(8,128)(2,1)}) custom-call(s32[1]{0:T(128)} %bitcast.me_ref, s32[64]{0:T(128)S(1)} %get-tuple-element.56.slot_ref, f32[64]{0:T(128)S(1)} %convert_divide_fusion.1.weight_ref, bf16[16,512]{1,0:T(8,128)(2,1)S(1)} %select_convert_fusion.note_ref, ...), custom_call_target="tpu_custom_call" | custom-call | tf_op jit(solution)/shard_map/sort/pallas_call | solution.py:253
  225.3 1.9 collective-permute-start.1
  227.1 1.9 collective-permute-start.2
  229.3 1.2 copy-done.5
  230.6 1.2 copy-done.7
  231.8 1.2 copy-done.9
  233.0 8.0 %rows.3.refs_5_ = f32[5,8,64,2048]{3,2,1,0:T(8,128)} custom-call(bf16[1040,512]{1,0:T(8,128)(2,1)S(1)} %copy-done.3, bf16[1040,512]{1,0:T(8,128)(2,1)S(1)} %copy-done.5, bf16[1040,512]{1,0:T(8,128)(2,1)S(1)} %copy-done.7, bf16[1040,512]{1,0:T(8,128)(2,1)S(1)} %copy-done.9, bf16[4,2048,512]{2,1,0:T(8,128)(2,1)} %bitcast.41), custom_call_target="tpu_custom_call" | custom-call | flops 30000001024 | tf_op jit(solution)/shard_map/rows/pallas_call | solution.py:414
  241.0 8.0 %rows.4.refs_3_ = f32[5,8,64,2048]{3,2,1,0:T(8,128)} custom-call(bf16[1040,512]{1,0:T(8,128)(2,1)S(1)} %copy-done.3, bf16[1040,512]{1,0:T(8,128)(2,1)S(1)} %copy-done.5, bf16[1040,512]{1,0:T(8,128)(2,1)S(1)} %copy-done.7, bf16[1040,512]{1,0:T(8,128)(2,1)S(1)} %copy-done.9, bf16[4,2048,512]{2,1,0:T(8,128)(2,1)} %bitcast.42, ...), custom_call_target="tpu_custom_call", output_to_operand_aliasing={{}: (5, {})} | custom-call | flops 30000001024 | tf_op jit(solution)/shard_map/rows/pallas_call | solution.py:414
  249.0 0.9 convert_reduce_fusion
  250.0 1.4 select_reduce_fusion.refs_0_
  251.3 8.9 %all-to-all-done.2.refs_1_ = bf16[8,4096,128]{2,1,0:T(8,128)(2,1)} async-done(((bf16[8,4096,128]{2,1,0:T(8,128)(2,1)}), bf16[8,4096,128]{2,1,0:T(8,128)(2,1)}, u32[]{:S(2)}, u32[]{:S(2)}) %all-to-all-start.2) | async-done | bytes 8388640 | tf_op jit(solution)/shard_map/all_to_all | solution.py:499
  260.2 17.6 %box.1.refs_5_ = f32[5,8,64,2048]{3,2,1,0:T(8,128)} custom-call(s32[4,64]{1,0:T(4,128)S(1)} %select_reduce_fusion.refs_0_, bf16[8,4096,128]{2,1,0:T(8,128)(2,1)} %all-to-all-done.2.refs_1_, bf16[4,2048,512]{2,1,0:T(8,128)(2,1)} %bitcast.43, f32[5,8,64,2048]{3,2,1,0:T(8,128)} %rows.4.refs_3_), custom_call_target="tpu_custom_call", output_to_operand_aliasing={{}: (3, {})} | custom-call | tf_op jit(solution)/shard_map/box/pallas_call | solution.py:414
  277.8 8.0 %rows.5 = f32[5,8,64,2048]{3,2,1,0:T(8,128)} custom-call(bf16[528,512]{1,0:T(8,128)(2,1)S(1)} %copy-done, bf16[528,512]{1,0:T(8,128)(2,1)S(1)} %collective-permute-done.refs_1_, bf16[528,512]{1,0:T(8,128)(2,1)S(1)} %collective-permute-done.1.refs_2_, bf16[528,512]{1,0:T(8,128)(2,1)S(1)} %collective-permute-done.2.refs_3_, ...), custom_call_target="tpu_custom_call", output_to_operand_aliasing={{}: (5, {})} | custom-call | tf_op jit(solution)/shard_map/rows/pallas_call | solution.py:414
  (69 shorter events, 1.4 us)
Async XLA Ops:
  1.4 0.7 copy-start.1
  7.9 5.4 %copy-start.2 = (s32[64]{0:T(128)S(1)}, s32[64]{0:T(128)}, u32[]{:S(2)}) copy-start(s32[64]{0:T(128)} %dest_ref.3) | copy-start | bytes 772
  8.0 5.4 %copy-start.10 = (s32[64]{0:T(128)S(1)}, s32[64]{0:T(128)}, u32[]{:S(2)}) copy-start(s32[64]{0:T(128)} %param.6) | copy-start | bytes 772
  8.0 98.8 %all-to-all-start = ((bf16[8,2064,256]{2,1,0:T(8,128)(2,1)}), bf16[8,2064,256]{2,1,0:T(8,128)(2,1)}, u32[]{:S(2)}, u32[]{:S(2)}) async-start(bf16[8,2064,256]{2,1,0:T(8,128)(2,1)} %post.2), calls=%async_computation | async-start | bytes 16908288 | tf_op jit(solution)/shard_map/all_to_all | solution.py:499
  18.5 104.0 %collective-permute-start.6 = (bf16[4112,128]{1,0:T(8,128)(2,1)}, bf16[4112,128]{1,0:T(8,128)(2,1)S(1)}, u32[]{:S(2)}, u32[]{:S(2)}) collective-permute-start(bf16[4112,128]{1,0:T(8,128)(2,1)} %get-tuple-element.45), channel_id=1, source_target_pairs={{0,1},{1,2},{2,3},{3,0},{4,5},{5,6},{6,7},{7,4},{8,9},{9,10},{10,1... | collective-permute-start | bytes 3158024 | tf_op jit(solution)/shard_map/ppermute | solution.py:495
  20.1 102.4 %collective-permute-start.7 = (bf16[4112,128]{1,0:T(8,128)(2,1)}, bf16[4112,128]{1,0:T(8,128)(2,1)S(1)}, u32[]{:S(2)}, u32[]{:S(2)}) collective-permute-start(bf16[4112,128]{1,0:T(8,128)(2,1)} %get-tuple-element.46), channel_id=1, source_target_pairs={{0,2},{1,3},{2,0},{3,1},{4,6},{5,7},{6,4},{7,5},{8,10},{9,11},{10,... | collective-permute-start | bytes 3158024 | tf_op jit(solution)/shard_map/ppermute | solution.py:495
  21.1 101.4 %collective-permute-start.8 = (bf16[4112,128]{1,0:T(8,128)(2,1)}, bf16[4112,128]{1,0:T(8,128)(2,1)S(1)}, u32[]{:S(2)}, u32[]{:S(2)}) collective-permute-start(bf16[4112,128]{1,0:T(8,128)(2,1)} %get-tuple-element.47), channel_id=1, source_target_pairs={{0,3},{1,0},{2,1},{3,2},{4,7},{5,4},{6,5},{7,6},{8,11},{9,8},{10,9... | collective-permute-start | bytes 3158024 | tf_op jit(solution)/shard_map/ppermute | solution.py:495
  106.7 54.5 %all-to-all-start.1 = ((bf16[8,1040,256]{2,1,0:T(8,128)(2,1)}), bf16[8,1040,256]{2,1,0:T(8,128)(2,1)}, u32[]{:S(2)}, u32[]{:S(2)}) async-start(bf16[8,1040,256]{2,1,0:T(8,128)(2,1)} %post.3), calls=%async_computation.1 | async-start | bytes 8519680 | tf_op jit(solution)/shard_map/all_to_all | solution.py:499
  122.5 1.0 copy-start.11
  122.5 1.3 copy-start.12
  122.5 2.9 %copy-start.13 = (bf16[4112,128]{1,0:T(8,128)(2,1)}, bf16[4112,128]{1,0:T(8,128)(2,1)S(1)}, u32[]{:S(2)}) copy-start(bf16[4112,128]{1,0:T(8,128)(2,1)S(1)} %collective-permute-done.8.refs_3_) | copy-start | bytes 3158020
  123.9 71.4 %collective-permute-start.3 = (bf16[1040,512]{1,0:T(8,128)(2,1)}, bf16[1040,512]{1,0:T(8,128)(2,1)S(1)}, u32[]{:S(2)}, u32[]{:S(2)}) collective-permute-start(bf16[1040,512]{1,0:T(8,128)(2,1)} %get-tuple-element.42), channel_id=1, source_target_pairs={{0,1},{1,2},{2,3},{3,0},{4,5},{5,6},{6,7},{7,4},{8,9},{9,10},{10,1... | collective-permute-start | bytes 3194888 | tf_op jit(solution)/shard_map/ppermute | solution.py:495
  125.4 91.9 %collective-permute-start.4 = (bf16[1040,512]{1,0:T(8,128)(2,1)}, bf16[1040,512]{1,0:T(8,128)(2,1)S(1)}, u32[]{:S(2)}, u32[]{:S(2)}) collective-permute-start(bf16[1040,512]{1,0:T(8,128)(2,1)} %get-tuple-element.43), channel_id=1, source_target_pairs={{0,2},{1,3},{2,0},{3,1},{4,6},{5,7},{6,4},{7,5},{8,10},{9,11},{10,... | collective-permute-start | bytes 3194888 | tf_op jit(solution)/shard_map/ppermute | solution.py:495
  126.7 92.2 %collective-permute-start.5 = (bf16[1040,512]{1,0:T(8,128)(2,1)}, bf16[1040,512]{1,0:T(8,128)(2,1)S(1)}, u32[]{:S(2)}, u32[]{:S(2)}) collective-permute-start(bf16[1040,512]{1,0:T(8,128)(2,1)} %get-tuple-element.44), channel_id=1, source_target_pairs={{0,3},{1,0},{2,1},{3,2},{4,7},{5,4},{6,5},{7,6},{8,11},{9,8},{10,9... | collective-permute-start | bytes 3194888 | tf_op jit(solution)/shard_map/ppermute | solution.py:495
  161.2 99.0 %all-to-all-start.2 = ((bf16[8,4096,128]{2,1,0:T(8,128)(2,1)}), bf16[8,4096,128]{2,1,0:T(8,128)(2,1)}, u32[]{:S(2)}, u32[]{:S(2)}) async-start(bf16[8,4096,128]{2,1,0:T(8,128)(2,1)} %mail.1), calls=%async_computation.2 | async-start | bytes 16777216 | tf_op jit(solution)/shard_map/all_to_all | solution.py:499
  195.3 29.9 %copy-start.4 = (bf16[1040,512]{1,0:T(8,128)(2,1)}, bf16[1040,512]{1,0:T(8,128)(2,1)S(1)}, u32[]{:S(2)}) copy-start(bf16[1040,512]{1,0:T(8,128)(2,1)S(1)} %collective-permute-done.3.refs_1_) | copy-start | bytes 3194884
  217.3 7.9 %copy-start.6 = (bf16[1040,512]{1,0:T(8,128)(2,1)}, bf16[1040,512]{1,0:T(8,128)(2,1)S(1)}, u32[]{:S(2)}) copy-start(bf16[1040,512]{1,0:T(8,128)(2,1)S(1)} %collective-permute-done.4.refs_2_) | copy-start | bytes 3194884
  218.8 1.0 copy-start.8
  219.9 9.2 %copy-start.3 = (bf16[1040,512]{1,0:T(8,128)(2,1)S(1)}, bf16[1040,512]{1,0:T(8,128)(2,1)}, u32[]{:S(2)}) copy-start(bf16[1040,512]{1,0:T(8,128)(2,1)} %get-tuple-element.41.refs_0_) | copy-start | bytes 3194884
  225.2 52.6 %collective-permute-start = (bf16[528,512]{1,0:T(8,128)(2,1)}, bf16[528,512]{1,0:T(8,128)(2,1)S(1)}, u32[]{:S(2)}, u32[]{:S(2)}) collective-permute-start(bf16[528,512]{1,0:T(8,128)(2,1)} %get-tuple-element.37), channel_id=1, source_target_pairs={{0,1},{1,2},{2,3},{3,0},{4,5},{5,6},{6,7},{7,4},{8,9},{9,10},{10,1... | collective-permute-start | bytes 1622024 | tf_op jit(solution)/shard_map/ppermute | solution.py:495
  225.3 52.5 %collective-permute-start.1 = (bf16[528,512]{1,0:T(8,128)(2,1)}, bf16[528,512]{1,0:T(8,128)(2,1)S(1)}, u32[]{:S(2)}, u32[]{:S(2)}) collective-permute-start(bf16[528,512]{1,0:T(8,128)(2,1)} %get-tuple-element.38), channel_id=1, source_target_pairs={{0,2},{1,3},{2,0},{3,1},{4,6},{5,7},{6,4},{7,5},{8,10},{9,11},{10,... | collective-permute-start | bytes 1622024 | tf_op jit(solution)/shard_map/ppermute | solution.py:495
  227.1 50.7 %collective-permute-start.2 = (bf16[528,512]{1,0:T(8,128)(2,1)}, bf16[528,512]{1,0:T(8,128)(2,1)S(1)}, u32[]{:S(2)}, u32[]{:S(2)}) collective-permute-start(bf16[528,512]{1,0:T(8,128)(2,1)} %get-tuple-element.39), channel_id=1, source_target_pairs={{0,3},{1,0},{2,1},{3,2},{4,7},{5,4},{6,5},{7,6},{8,11},{9,8},{10,9... | collective-permute-start | bytes 1622024 | tf_op jit(solution)/shard_map/ppermute | solution.py:495
  229.3 1.2 copy-start.5
  230.6 1.2 copy-start.7
  231.8 1.2 copy-start.9
  251.3 26.5 %copy-start = (bf16[528,512]{1,0:T(8,128)(2,1)S(1)}, bf16[528,512]{1,0:T(8,128)(2,1)}, u32[]{:S(2)}) copy-start(bf16[528,512]{1,0:T(8,128)(2,1)} %get-tuple-element.36.refs_0_) | copy-start | bytes 1622020
